TPU v7x, 32 devices: a whole 2x2x4 slice. The times are simulated.
32 devices in a mesh: dp: 16 (over z, y, core), tensor: 2 (over x).
Axes of the slice: x: 2, y: 2, z: 4, core: 2. Of those that a mesh axis runs over, the one named last changes fastest.
Arguments:
- tokens: bfloat16 [18432, 1536], P(('dp', 'tensor')), may hold values from -6 to 6
- timestep: bfloat16 [48, 1024], P('dp'), may hold values from -6 to 6
- caption: bfloat16 [48, 256, 2048], P('dp'), may hold values from -6 to 6
- caption_mask: int32 [48, 256], P('dp'), may hold values from 0 to 1, as said below
- image_lengths: int32 [48], P('dp'), may hold values from 72 to 768, as said below
- patch_pos: int32 [2, 18432], P(None, 'dp'), may hold values from 0 to 31, as said below
- ada_weight: bfloat16 [1024, 6144], P(None, 'tensor'), may hold values from -0.1875 to 0.1875
- ada_bias: float32 [6144], P('tensor'), may hold values from -3 to 3
- attention_norm: float32 [1536], replicated, may hold values from 0.25 to 1.75
- attention_post: float32 [1536], replicated, may hold values from 0.25 to 1.75
- feedforward_norm: float32 [1536], replicated, may hold values from 0.25 to 1.75
- feedforward_post: float32 [1536], replicated, may hold values from 0.25 to 1.75
- query_weight: bfloat16 [1536, 1536], P(None, 'tensor'), may hold values from -0.15625 to 0.15625
- key_weight: bfloat16 [1536, 1536], P(None, 'tensor'), may hold values from -0.15625 to 0.15625
- value_weight: bfloat16 [1536, 1536], P(None, 'tensor'), may hold values from -0.15625 to 0.15625
- query_gain: float32 [24, 64], P('tensor'), may hold values from 0.8 to 2
- key_gain: float32 [24, 64], P('tensor'), may hold values from 0.8 to 2
- cross_keys: bfloat16 [2048, 1536], P(None, 'tensor'), may hold values from -0.125 to 0.125
- cross_values: bfloat16 [2048, 1536], P(None, 'tensor'), may hold values from -0.125 to 0.125
- cross_gain: float32 [24, 64], P('tensor'), may hold values from 0.8 to 2
- cross_gate: float32 [24], P('tensor'), may hold values from -1.5 to 1.5
- output_weight: bfloat16 [1536, 1536], P('tensor'), may hold values from -0.15625 to 0.15625
- gate_weight: bfloat16 [1536, 4096], P(None, 'tensor'), may hold values from -0.15625 to 0.15625
- up_weight: bfloat16 [1536, 4096], P(None, 'tensor'), may hold values from -0.15625 to 0.15625
- down_weight: bfloat16 [4096, 1536], P('tensor'), may hold values from -0.09375 to 0.09375
- cotangent: bfloat16 [18432, 1536], P(('dp', 'tensor')), may hold values from -6 to 6
Outputs:
- out: bfloat16 [18432, 1536], P(('dp', 'tensor'))
- tokens_grad: float32 [18432, 1536], P(('dp', 'tensor'))
- ada_weight_grad: float32 [1024, 6144], P('dp', 'tensor')
- ada_bias_grad: float32 [6144], P('tensor')
- attention_norm_grad: float32 [1536], replicated
- attention_post_grad: float32 [1536], replicated
- feedforward_norm_grad: float32 [1536], replicated
- feedforward_post_grad: float32 [1536], replicated
- query_weight_grad: float32 [1536, 1536], P('dp', 'tensor')
- key_weight_grad: float32 [1536, 1536], P('dp', 'tensor')
- value_weight_grad: float32 [1536, 1536], P('dp', 'tensor')
- query_gain_grad: float32 [24, 64], P('tensor')
- key_gain_grad: float32 [24, 64], P('tensor')
- cross_keys_grad: float32 [2048, 1536], P('dp', 'tensor')
- cross_values_grad: float32 [2048, 1536], P('dp', 'tensor')
- cross_gain_grad: float32 [24, 64], P('tensor')
- cross_gate_grad: float32 [24], P('tensor')
- output_weight_grad: float32 [1536, 1536], P('tensor', 'dp')
- gate_weight_grad: float32 [1536, 4096], P('dp', 'tensor')
- up_weight_grad: float32 [1536, 4096], P('dp', 'tensor')
- down_weight_grad: float32 [4096, 1536], P('tensor', 'dp')
Inputs may be any that keep to these rules, and one draw needn't show every extreme that they name: `image_lengths`: the 3 lengths of each index of dp sum to 1152. `caption_mask`: each row is 1 on a leading run of 8 to 256 positions and 0 after it; in each index of dp one image uses all 256. `patch_pos`: patch rows and columns of the tokens of an image, its rows of 16 to 32 patches read one after another; the longest image of each index of dp has rows of 32.
All inputs are finite; a program needn't handle non-finite values.
Results may differ from a plain program's by a relative error of at most 0.022.
Values may be sent and summed in bfloat16 or wider, within the bound.
No kernel may reach another device: no remote copies, remote signals or barrier semaphores. Data moves between devices by JAX's collectives and lax.ppermute only.
A program may use at most 576 MiB of HBM per device.

v0:
```python
import math

import jax
import jax.numpy as jnp
from jax import lax
from jax.sharding import PartitionSpec as P

epsilon = 1e-05
negative = -1e30
theta = 10000.0
highest = lax.Precision.HIGHEST


def sigmoid_of(values):
    return 1.0 / (1.0 + jnp.exp(-values))


def unit_rows(values):
    factor = lax.rsqrt(jnp.mean(values * values, axis=-1, keepdims=True) + epsilon)
    return (values * factor, factor)


def unit_back(gradient, normed, factor):
    return factor * (gradient - normed * jnp.mean(gradient * normed, axis=-1, keepdims=True))


def softmax_kept(scores):
    top = jnp.max(scores, axis=-1, keepdims=True)
    expo = jnp.exp(scores - top)
    total = jnp.sum(expo, axis=-1, keepdims=True)
    return (expo / total, top + jnp.log(total))


def rope_tables(positions, head_size):
    quarter = head_size // 4
    freqs = jnp.power(theta, -(jnp.arange(quarter, dtype=jnp.float32) / quarter))
    angles = jnp.concatenate(
        [
            positions[0].astype(jnp.float32)[:, None] * freqs[None, :],
            positions[1].astype(jnp.float32)[:, None] * freqs[None, :],
        ],
        axis=1,
    )
    return (jnp.cos(angles), jnp.sin(angles))


def rotate(values, cosine, sine):
    half = values.shape[-1] // 2
    first = values[..., :half]
    second = values[..., half:]
    cosine = cosine[:, None, :]
    sine = sine[:, None, :]
    return jnp.concatenate(
        [first * cosine - second * sine, first * sine + second * cosine], axis=-1
    )


def rotate_back(gradient, cosine, sine):
    half = gradient.shape[-1] // 2
    first = gradient[..., :half]
    second = gradient[..., half:]
    cosine = cosine[:, None, :]
    sine = sine[:, None, :]
    return jnp.concatenate(
        [first * cosine + second * sine, second * cosine - first * sine], axis=-1
    )


def outer(left, right):
    return lax.dot_general(
        left, right, (((0,), (0,)), ((), ())), preferred_element_type=jnp.float32
    )


def outer_exact(left, right):
    return lax.dot_general(
        left, right, (((0,), (0,)), ((), ())), precision=highest, preferred_element_type=jnp.float32
    )


def back_dot(gradient, weight):
    return lax.dot_general(
        gradient, weight, (((1,), (1,)), ((), ())), preferred_element_type=jnp.float32
    )


def on_device(
    tokens,
    timestep,
    caption,
    caption_mask,
    image_lengths,
    patch_pos,
    ada_weight,
    ada_bias,
    attention_norm,
    attention_post,
    feedforward_norm,
    feedforward_post,
    query_weight,
    key_weight,
    value_weight,
    query_gain,
    key_gain,
    cross_keys,
    cross_values,
    cross_gain,
    cross_gate,
    output_weight,
    gate_weight,
    up_weight,
    down_weight,
    cotangent,
):
    local_rows, model_width = tokens.shape
    tensor_count = lax.axis_size("tensor")
    tensor_place = lax.axis_index("tensor")
    group_tokens = local_rows * tensor_count
    image_count, cap_len, cap_width = caption.shape
    local_heads, head_size = query_gain.shape
    head_columns = local_heads * head_size
    mod_columns = ada_weight.shape[1]
    cap_total = image_count * cap_len
    score_scale = 1.0 / math.sqrt(head_size)
    image_ends = jnp.cumsum(image_lengths)
    places = jnp.arange(group_tokens, dtype=jnp.int32)
    image_all = jnp.sum((places[:, None] >= image_ends[None, :]).astype(jnp.int32), axis=1)
    image_own = lax.dynamic_slice_in_dim(image_all, tensor_place * local_rows, local_rows)
    own_onehot = (image_own[:, None] == jnp.arange(image_count, dtype=jnp.int32)[None, :]).astype(
        jnp.float32
    )
    time_float = timestep.astype(jnp.float32)
    silu_time = (time_float * sigmoid_of(time_float)).astype(jnp.bfloat16)
    mod_part = jnp.dot(silu_time, ada_weight, preferred_element_type=jnp.float32) + ada_bias
    modulation = lax.all_gather(mod_part, "tensor", axis=1, tiled=True)
    token_mod = jnp.dot(own_onehot, modulation, precision=highest)
    scale_attn = token_mod[:, :model_width]
    gate_attn = jnp.tanh(token_mod[:, model_width : 2 * model_width])
    scale_ffn = token_mod[:, 2 * model_width : 3 * model_width]
    gate_ffn = jnp.tanh(token_mod[:, 3 * model_width :])
    x_float = tokens.astype(jnp.float32)
    x_unit, x_factor = unit_rows(x_float)
    normed_rows = (x_unit * attention_norm * (1.0 + scale_attn)).astype(jnp.bfloat16)
    normed_all = lax.all_gather(normed_rows, "tensor", axis=0, tiled=True)
    q_raw = jnp.dot(normed_all, query_weight, preferred_element_type=jnp.float32).reshape(
        group_tokens, local_heads, head_size
    )
    k_raw = jnp.dot(normed_all, key_weight, preferred_element_type=jnp.float32).reshape(
        group_tokens, local_heads, head_size
    )
    values = (
        jnp.dot(normed_all, value_weight, preferred_element_type=jnp.float32)
        .astype(jnp.bfloat16)
        .reshape(group_tokens, local_heads, head_size)
    )
    cosine, sine = rope_tables(patch_pos, head_size)
    q_unit, q_factor = unit_rows(q_raw)
    queries = rotate(q_unit * query_gain, cosine, sine).astype(jnp.bfloat16)
    k_unit, k_factor = unit_rows(k_raw)
    keys = rotate(k_unit * key_gain, cosine, sine).astype(jnp.bfloat16)
    cap_flat = caption.reshape(cap_total, cap_width)
    ck_raw = jnp.dot(cap_flat, cross_keys, preferred_element_type=jnp.float32).reshape(
        cap_total, local_heads, head_size
    )
    ck_unit, ck_factor = unit_rows(ck_raw)
    cap_keys = (ck_unit * cross_gain).astype(jnp.bfloat16)
    cap_values = (
        jnp.dot(cap_flat, cross_values, preferred_element_type=jnp.float32)
        .astype(jnp.bfloat16)
        .reshape(cap_total, local_heads, head_size)
    )
    key_image = jnp.arange(cap_total, dtype=jnp.int32) // cap_len
    key_valid = caption_mask.reshape(-1) > 0
    head_gate = jnp.tanh(cross_gate)
    block_count = max(1, group_tokens // 512)
    block_rows = group_tokens // block_count

    def self_scores(block_q, block_image):
        scores = (
            jnp.einsum("qhd,khd->hqk", block_q, keys, preferred_element_type=jnp.float32)
            * score_scale
        )
        allowed = block_image[:, None] == image_all[None, :]
        return jnp.where(allowed[None], scores, negative)

    def cross_scores(block_q, block_image):
        scores = (
            jnp.einsum("qhd,khd->hqk", block_q, cap_keys, preferred_element_type=jnp.float32)
            * score_scale
        )
        allowed = (block_image[:, None] == key_image[None, :]) & key_valid[None, :]
        return jnp.where(allowed[None], scores, negative)

    mixed_blocks = []
    self_lse = []
    cross_lse = []
    for block_index in range(block_count):
        start = block_index * block_rows
        block_q = queries[start : start + block_rows]
        block_image = image_all[start : start + block_rows]
        self_probs, self_top = softmax_kept(self_scores(block_q, block_image))
        self_out = jnp.einsum(
            "hqk,khd->qhd",
            self_probs.astype(jnp.bfloat16),
            values,
            preferred_element_type=jnp.float32,
        )
        cross_probs, cross_top = softmax_kept(cross_scores(block_q, block_image))
        cross_out = jnp.einsum(
            "hqk,khd->qhd",
            cross_probs.astype(jnp.bfloat16),
            cap_values,
            preferred_element_type=jnp.float32,
        )
        mixed_blocks.append((self_out + head_gate[None, :, None] * cross_out).astype(jnp.bfloat16))
        self_lse.append(self_top)
        cross_lse.append(cross_top)
    mixed = jnp.concatenate(mixed_blocks, axis=0).reshape(group_tokens, head_columns)
    attn_rows = lax.psum_scatter(
        jnp.dot(mixed, output_weight, preferred_element_type=jnp.float32).astype(jnp.bfloat16),
        "tensor",
        scatter_dimension=0,
        tiled=True,
    ).astype(jnp.float32)
    attn_unit, attn_factor = unit_rows(attn_rows)
    hidden = x_float + gate_attn * attn_unit * attention_post
    hidden_unit, hidden_factor = unit_rows(hidden)
    ffn_in_rows = (hidden_unit * feedforward_norm * (1.0 + scale_ffn)).astype(jnp.bfloat16)
    ffn_in_all = lax.all_gather(ffn_in_rows, "tensor", axis=0, tiled=True)
    gate_pre = jnp.dot(ffn_in_all, gate_weight, preferred_element_type=jnp.float32)
    up_pre = jnp.dot(ffn_in_all, up_weight, preferred_element_type=jnp.float32)
    gate_sig = sigmoid_of(gate_pre)
    gate_act = gate_pre * gate_sig
    hidden_act = (gate_act * up_pre).astype(jnp.bfloat16)
    ffn_rows = lax.psum_scatter(
        jnp.dot(hidden_act, down_weight, preferred_element_type=jnp.float32).astype(jnp.bfloat16),
        "tensor",
        scatter_dimension=0,
        tiled=True,
    ).astype(jnp.float32)
    ffn_unit, ffn_factor = unit_rows(ffn_rows)
    layer_out = (hidden + gate_ffn * ffn_unit * feedforward_post).astype(jnp.bfloat16)
    grad_out = cotangent.astype(jnp.float32)
    grad_post_ffn = jnp.sum(grad_out * gate_ffn * ffn_unit, axis=0)
    grad_gate_ffn = grad_out * ffn_unit * feedforward_post * (1.0 - gate_ffn * gate_ffn)
    grad_ffn_rows = unit_back(grad_out * gate_ffn * feedforward_post, ffn_unit, ffn_factor).astype(
        jnp.bfloat16
    )
    grad_ffn_all = lax.all_gather(grad_ffn_rows, "tensor", axis=0, tiled=True)
    down_grad = outer(hidden_act, grad_ffn_all)
    grad_inner = back_dot(grad_ffn_all, down_weight)
    grad_up = (grad_inner * gate_act).astype(jnp.bfloat16)
    grad_gate = (grad_inner * up_pre * gate_sig * (1.0 + gate_pre * (1.0 - gate_sig))).astype(
        jnp.bfloat16
    )
    gate_grad = outer(ffn_in_all, grad_gate)
    up_grad = outer(ffn_in_all, grad_up)
    grad_ffn_in = lax.psum_scatter(
        (back_dot(grad_gate, gate_weight) + back_dot(grad_up, up_weight)).astype(jnp.bfloat16),
        "tensor",
        scatter_dimension=0,
        tiled=True,
    ).astype(jnp.float32)
    grad_norm_ffn = jnp.sum(grad_ffn_in * hidden_unit * (1.0 + scale_ffn), axis=0)
    grad_scale_ffn = grad_ffn_in * hidden_unit * feedforward_norm
    grad_hidden = grad_out + unit_back(
        grad_ffn_in * feedforward_norm * (1.0 + scale_ffn), hidden_unit, hidden_factor
    )
    grad_post_attn = jnp.sum(grad_hidden * gate_attn * attn_unit, axis=0)
    grad_gate_attn = grad_hidden * attn_unit * attention_post * (1.0 - gate_attn * gate_attn)
    grad_attn_rows = unit_back(
        grad_hidden * gate_attn * attention_post, attn_unit, attn_factor
    ).astype(jnp.bfloat16)
    grad_attn_all = lax.all_gather(grad_attn_rows, "tensor", axis=0, tiled=True)
    output_grad = outer(mixed, grad_attn_all)
    grad_mixed = (
        back_dot(grad_attn_all, output_weight)
        .astype(jnp.bfloat16)
        .reshape(group_tokens, local_heads, head_size)
    )
    grad_keys = jnp.zeros((group_tokens, local_heads, head_size), jnp.float32)
    grad_values = jnp.zeros((group_tokens, local_heads, head_size), jnp.float32)
    grad_cap_keys = jnp.zeros((cap_total, local_heads, head_size), jnp.float32)
    grad_cap_values = jnp.zeros((cap_total, local_heads, head_size), jnp.float32)
    grad_head_gate = jnp.zeros((local_heads,), jnp.float32)
    query_blocks = []
    for block_index in range(block_count):
        start = block_index * block_rows
        block_q = queries[start : start + block_rows]
        block_image = image_all[start : start + block_rows]
        block_grad = grad_mixed[start : start + block_rows]
        self_probs = jnp.exp(self_scores(block_q, block_image) - self_lse[block_index])
        grad_probs = jnp.einsum(
            "qhd,khd->hqk", block_grad, values, preferred_element_type=jnp.float32
        )
        grad_self = (
            self_probs * (grad_probs - jnp.sum(grad_probs * self_probs, axis=-1, keepdims=True))
        ).astype(jnp.bfloat16)
        grad_block = (
            jnp.einsum("hqk,khd->qhd", grad_self, keys, preferred_element_type=jnp.float32)
            * score_scale
        )
        grad_keys = (
            grad_keys
            + jnp.einsum("hqk,qhd->khd", grad_self, block_q, preferred_element_type=jnp.float32)
            * score_scale
        )
        grad_values = grad_values + jnp.einsum(
            "hqk,qhd->khd",
            self_probs.astype(jnp.bfloat16),
            block_grad,
            preferred_element_type=jnp.float32,
        )
        cross_probs = jnp.exp(cross_scores(block_q, block_image) - cross_lse[block_index])
        cross_low = cross_probs.astype(jnp.bfloat16)
        cross_out = jnp.einsum(
            "hqk,khd->qhd", cross_low, cap_values, preferred_element_type=jnp.float32
        )
        grad_head_gate = grad_head_gate + jnp.sum(
            block_grad.astype(jnp.float32) * cross_out, axis=(0, 2)
        )
        grad_cprobs = (
            jnp.einsum("qhd,khd->hqk", block_grad, cap_values, preferred_element_type=jnp.float32)
            * head_gate[:, None, None]
        )
        grad_cross = (
            cross_probs * (grad_cprobs - jnp.sum(grad_cprobs * cross_probs, axis=-1, keepdims=True))
        ).astype(jnp.bfloat16)
        grad_block = (
            grad_block
            + jnp.einsum("hqk,khd->qhd", grad_cross, cap_keys, preferred_element_type=jnp.float32)
            * score_scale
        )
        grad_cap_keys = (
            grad_cap_keys
            + jnp.einsum("hqk,qhd->khd", grad_cross, block_q, preferred_element_type=jnp.float32)
            * score_scale
        )
        grad_cap_values = (
            grad_cap_values
            + jnp.einsum("hqk,qhd->khd", cross_low, block_grad, preferred_element_type=jnp.float32)
            * head_gate[None, :, None]
        )
        query_blocks.append(grad_block)
    grad_head_gate = grad_head_gate * (1.0 - head_gate * head_gate)
    grad_queries = jnp.concatenate(query_blocks, axis=0)
    query_turned = rotate_back(grad_queries, cosine, sine)
    query_gain_part = jnp.sum(query_turned * q_unit, axis=0)
    grad_q_raw = (
        unit_back(query_turned * query_gain, q_unit, q_factor)
        .astype(jnp.bfloat16)
        .reshape(group_tokens, head_columns)
    )
    key_turned = rotate_back(grad_keys, cosine, sine)
    key_gain_part = jnp.sum(key_turned * k_unit, axis=0)
    grad_k_raw = (
        unit_back(key_turned * key_gain, k_unit, k_factor)
        .astype(jnp.bfloat16)
        .reshape(group_tokens, head_columns)
    )
    cross_gain_part = jnp.sum(grad_cap_keys * ck_unit, axis=0)
    grad_ck_raw = (
        unit_back(grad_cap_keys * cross_gain, ck_unit, ck_factor)
        .astype(jnp.bfloat16)
        .reshape(cap_total, head_columns)
    )
    grad_v_raw = grad_values.astype(jnp.bfloat16).reshape(group_tokens, head_columns)
    grad_cv_raw = grad_cap_values.astype(jnp.bfloat16).reshape(cap_total, head_columns)
    query_grad = outer(normed_all, grad_q_raw)
    key_grad = outer(normed_all, grad_k_raw)
    value_grad = outer(normed_all, grad_v_raw)
    ckey_grad = outer(cap_flat, grad_ck_raw)
    cvalue_grad = outer(cap_flat, grad_cv_raw)
    grad_normed_in = lax.psum_scatter(
        (
            back_dot(grad_q_raw, query_weight)
            + back_dot(grad_k_raw, key_weight)
            + back_dot(grad_v_raw, value_weight)
        ).astype(jnp.bfloat16),
        "tensor",
        scatter_dimension=0,
        tiled=True,
    ).astype(jnp.float32)
    grad_norm_attn = jnp.sum(grad_normed_in * x_unit * (1.0 + scale_attn), axis=0)
    grad_scale_attn = grad_normed_in * x_unit * attention_norm
    tokens_grad = grad_hidden + unit_back(
        grad_normed_in * attention_norm * (1.0 + scale_attn), x_unit, x_factor
    )
    grad_mod_tokens = jnp.concatenate(
        [grad_scale_attn, grad_gate_attn, grad_scale_ffn, grad_gate_ffn], axis=1
    )
    grad_mod_part = outer_exact(own_onehot, grad_mod_tokens)
    grad_mod = lax.psum_scatter(
        grad_mod_part.astype(jnp.bfloat16), "tensor", scatter_dimension=1, tiled=True
    ).astype(jnp.float32)
    ada_grad = outer_exact(silu_time.astype(jnp.float32), grad_mod)
    bias_part = jnp.sum(grad_mod, axis=0)
    heads_total = local_heads * tensor_count
    zero_index = jnp.zeros((), jnp.int32)
    head_offset = tensor_place * local_heads
    column_offset = tensor_place * mod_columns
    norm_parts = jnp.stack([grad_norm_attn, grad_post_attn, grad_norm_ffn, grad_post_ffn])
    head_parts = lax.dynamic_update_slice(
        jnp.zeros((3, heads_total, head_size), jnp.float32),
        jnp.stack([query_gain_part, key_gain_part, cross_gain_part]),
        (zero_index, head_offset, zero_index),
    )
    gate_parts = lax.dynamic_update_slice(
        jnp.zeros((heads_total,), jnp.float32), grad_head_gate, (head_offset,)
    )
    bias_parts = lax.dynamic_update_slice(
        jnp.zeros((mod_columns * tensor_count,), jnp.float32), bias_part, (column_offset,)
    )
    norm_sums, head_sums, gate_sums, bias_sums = lax.psum(
        (norm_parts, head_parts, gate_parts, bias_parts), ("dp", "tensor")
    )
    head_own = lax.dynamic_slice_in_dim(head_sums, head_offset, local_heads, axis=1)
    gate_own = lax.dynamic_slice_in_dim(gate_sums, head_offset, local_heads)
    bias_own = lax.dynamic_slice_in_dim(bias_sums, column_offset, mod_columns)
    (
        query_sum,
        key_sum,
        value_sum,
        ckey_sum,
        cvalue_sum,
        output_sum,
        ada_sum,
        gate_sum,
        up_sum,
        down_sum,
    ) = (
        lax.psum_scatter(
            query_grad.astype(jnp.bfloat16), "dp", scatter_dimension=0, tiled=True
        ).astype(jnp.float32),
        lax.psum_scatter(
            key_grad.astype(jnp.bfloat16), "dp", scatter_dimension=0, tiled=True
        ).astype(jnp.float32),
        lax.psum_scatter(
            value_grad.astype(jnp.bfloat16), "dp", scatter_dimension=0, tiled=True
        ).astype(jnp.float32),
        lax.psum_scatter(
            ckey_grad.astype(jnp.bfloat16), "dp", scatter_dimension=0, tiled=True
        ).astype(jnp.float32),
        lax.psum_scatter(
            cvalue_grad.astype(jnp.bfloat16), "dp", scatter_dimension=0, tiled=True
        ).astype(jnp.float32),
        lax.psum_scatter(
            output_grad.astype(jnp.bfloat16), "dp", scatter_dimension=1, tiled=True
        ).astype(jnp.float32),
        lax.psum_scatter(
            ada_grad.astype(jnp.bfloat16), "dp", scatter_dimension=0, tiled=True
        ).astype(jnp.float32),
        lax.psum_scatter(
            gate_grad.astype(jnp.bfloat16), "dp", scatter_dimension=0, tiled=True
        ).astype(jnp.float32),
        lax.psum_scatter(
            up_grad.astype(jnp.bfloat16), "dp", scatter_dimension=0, tiled=True
        ).astype(jnp.float32),
        lax.psum_scatter(
            down_grad.astype(jnp.bfloat16), "dp", scatter_dimension=1, tiled=True
        ).astype(jnp.float32),
    )
    return (
        layer_out,
        tokens_grad,
        ada_sum,
        bias_own,
        norm_sums[0],
        norm_sums[1],
        norm_sums[2],
        norm_sums[3],
        query_sum,
        key_sum,
        value_sum,
        head_own[0],
        head_own[1],
        ckey_sum,
        cvalue_sum,
        head_own[2],
        gate_own,
        output_sum,
        gate_sum,
        up_sum,
        down_sum,
    )


def solution(mesh):
    placed = (
        P(("dp", "tensor"), None),
        P("dp", None),
        P("dp", None, None),
        P("dp", None),
        P("dp"),
        P(None, "dp"),
        P(None, "tensor"),
        P("tensor"),
        P(),
        P(),
        P(),
        P(),
        P(None, "tensor"),
        P(None, "tensor"),
        P(None, "tensor"),
        P("tensor", None),
        P("tensor", None),
        P(None, "tensor"),
        P(None, "tensor"),
        P("tensor", None),
        P("tensor"),
        P("tensor", None),
        P(None, "tensor"),
        P(None, "tensor"),
        P("tensor", None),
        P(("dp", "tensor"), None),
    )
    return jax.shard_map(
        on_device,
        mesh=mesh,
        in_specs=placed,
        out_specs=(
            P(("dp", "tensor"), None),
            P(("dp", "tensor"), None),
            P("dp", "tensor"),
            P("tensor"),
            P(),
            P(),
            P(),
            P(),
            P("dp", "tensor"),
            P("dp", "tensor"),
            P("dp", "tensor"),
            P("tensor", None),
            P("tensor", None),
            P("dp", "tensor"),
            P("dp", "tensor"),
            P("tensor", None),
            P("tensor"),
            P("tensor", "dp"),
            P("dp", "tensor"),
            P("dp", "tensor"),
            P("tensor", "dp"),
        ),
        check_vma=False,
    )
```

profile of v0, /device:TPU:0, one launch (start us, length us, event | category | flops | bytes accessed | tf_op | source)
XLA Modules:
  0.0 1972.5 jit_solution(1857712941480433018)
XLA Ops:
  52.3 32.0 %all-gather.5.cloned.1.call-done = bf16[1152,1536]{1,0:T(8,128)(2,1)} async-done(((bf16[576,1536]{1,0:T(8,128)(2,1)}), bf16[1152,1536]{1,0:T(8,128)(2,1)}) %all-gather.5.cloned.1.call-update) | async-done | bytes 3538960 | tf_op jit(solution)/shard_map/all_gather | solution.py:144
  121.0 13.7 fusion.138
  134.8 13.5 fusion.136
  148.3 15.6 fusion
  168.5 14.8 fusion.14
  183.3 15.0 fusion.1
  198.3 14.8 fusion.15
  258.8 47.4 %reduce-scatter.22.cloned.1.call-done = bf16[576,1536]{1,0:T(8,128)(2,1)} async-done(((bf16[1152,1536]{1,0:T(8,128)(2,1)}), bf16[576,1536]{1,0:T(8,128)(2,1)}) %reduce-scatter.22.cloned.1.call-update) | async-done | bytes 1769488 | tf_op jit(solution)/shard_map/reduce_scatter | solution.py:219
  318.1 49.5 %all-gather.7.cloned.1.call-done = bf16[1152,1536]{1,0:T(8,128)(2,1)} async-done(((bf16[576,1536]{1,0:T(8,128)(2,1)}), bf16[1152,1536]{1,0:T(8,128)(2,1)}) %all-gather.7.cloned.1.call-update) | async-done | bytes 3538960 | tf_op jit(solution)/shard_map/all_gather | solution.py:229
  367.6 13.5 fusion.142
  381.1 14.1 multiply_convert_fusion.6
  406.5 47.8 %reduce-scatter.24.cloned.1.call-done = bf16[576,1536]{1,0:T(8,128)(2,1)} async-done(((bf16[1152,1536]{1,0:T(8,128)(2,1)}), bf16[576,1536]{1,0:T(8,128)(2,1)}) %reduce-scatter.24.cloned.1.call-update) | async-done | bytes 1769488 | tf_op jit(solution)/shard_map/reduce_scatter | solution.py:235
  466.7 49.3 %all-gather.9.cloned.1.call-done = bf16[1152,1536]{1,0:T(8,128)(2,1)} async-done(((bf16[576,1536]{1,0:T(8,128)(2,1)}), bf16[1152,1536]{1,0:T(8,128)(2,1)}) %all-gather.9.cloned.1.call-update) | async-done | bytes 3538960 | tf_op jit(solution)/shard_map/all_gather | solution.py:249
  516.0 19.7 multiply_convert_fusion.4
  535.7 11.3 fusion.143
  546.9 11.1 fusion.28
  558.4 47.6 %reduce-scatter.26.cloned.1.call-done = bf16[576,1536]{1,0:T(8,128)(2,1)} async-done(((bf16[1152,1536]{1,0:T(8,128)(2,1)}), bf16[576,1536]{1,0:T(8,128)(2,1)}) %reduce-scatter.26.cloned.1.call-update) | async-done | bytes 1769488 | tf_op jit(solution)/shard_map/reduce_scatter | solution.py:258
  611.8 11.3 fusion.56
  634.9 46.8 %all-gather.11.cloned.1.call-done = bf16[1152,1536]{1,0:T(8,128)(2,1)} async-done(((bf16[576,1536]{1,0:T(8,128)(2,1)}), bf16[1152,1536]{1,0:T(8,128)(2,1)}) %all-gather.11.cloned.1.call-update) | async-done | bytes 3538960 | tf_op jit(solution)/shard_map/all_gather | solution.py:274
  691.4 24.7 %multiply_reduce_fusion.1 = (f32[12,576]{1,0:T(8,128)S(1)}, f32[12,576,1152]{2,1,0:T(8,128)}) fusion(f32[12,576,1152]{2,1,0:T(8,128)} %get-tuple-element.185, f32[12,576]{1,0:T(8,128)S(1)} %log_add_fusion.3, bf16[576,12,64]{0,2,1:T(8,128)(2,1)} %bitcast.221, bf16[1152,12,64]{0,2,1:T(8,128)(2,1)} %bitcast.234), kind=kOutput, calls=%fused_computation.4 | convolution fusion | flops 1043096832 | bytes 66410496 | tf_op jit(solution)/shard_map/qhd,khd->hqk/dot_general | solution.py:293
  716.1 26.5 %multiply_convert_fusion.1 = bf16[12,576,1152]{2,1,0:T(8,128)(2,1)} fusion(f32[12,576,1152]{2,1,0:T(8,128)} %get-tuple-element.191, f32[12,576,1152]{2,1,0:T(8,128)} %get-tuple-element.185, f32[12,576]{1,0:T(8,128)S(1)} %get-tuple-element.190, f32[12,576]{1,0:T(8,128)S(1)} %log_add_fusion.3), kind=kLoop, calls=%fused_computation.3 | loop fusion | flops 31850496 | bytes 79681536 | tf_op jit(solution)/shard_map/convert_element_type | solution.py:298
  742.6 12.2 fusion.133
  767.6 11.7 fusion.144
  779.3 14.8 fusion.8
  794.1 24.2 %multiply_reduce_fusion = (f32[12,576]{1,0:T(8,128)S(1)}, f32[12,576,1152]{2,1,0:T(8,128)}) fusion(f32[12,576,1152]{2,1,0:T(8,128)} %get-tuple-element.179, f32[12,576]{1,0:T(8,128)S(1)} %log_add_fusion.1, bf16[576,12,64]{0,2,1:T(8,128)(2,1)S(1)} %bitcast.219, bf16[1152,12,64]{0,2,1:T(8,128)(2,1)S(1)} %bitcast.235), kind=kOutput, calls=%fused_computation.1 | convolution fusion | flops 1043096832 | bytes 66410496 | tf_op jit(solution)/shard_map/qhd,khd->hqk/dot_general | solution.py:293
  818.4 14.9 fusion.85
  833.3 26.7 %multiply_convert_fusion = bf16[12,576,1152]{2,1,0:T(8,128)(2,1)} fusion(f32[12,576,1152]{2,1,0:T(8,128)} %get-tuple-element.193, f32[12,576,1152]{2,1,0:T(8,128)} %get-tuple-element.179, f32[12,576]{1,0:T(8,128)S(1)} %get-tuple-element.192, f32[12,576]{1,0:T(8,128)S(1)} %log_add_fusion.1), kind=kLoop, calls=%fused_computation | loop fusion | flops 31850496 | bytes 79681536 | tf_op jit(solution)/shard_map/convert_element_type | solution.py:298
  860.0 12.1 fusion.132
  872.0 11.5 fusion.49
  883.6 30.6 %multiply_reduce_fusion.3 = (f32[12,576]{1,0:T(8,128)S(1)}, f32[12,576]{1,0:T(8,128)S(1)}, f32[12,576,768]{2,1,0:T(8,128)}) fusion(f32[12,576,768]{2,1,0:T(8,128)} %get-tuple-element.187, f32[12]{0:T(128)S(1)} %copy-done.91, f32[12,576]{1,0:T(8,128)S(1)} %copy-done.51, f32[12,576,768]{2,1,0:T(8,128)} %get-tuple-element.183, f32[12,576]{1,0:T(8,128)S(1)} %copy-done.50, ...), kind=kOutput, calls=%fused_computation.20 | convolution fusion | flops 721930752 | bytes 87109680 | tf_op jit(solution)/shard_map/qhd,khd->hqk/dot_general | solution.py:323
  914.2 31.6 %multiply_convert_fusion.3 = (bf16[12,576,768]{2,1,0:T(8,128)(2,1)}, bf16[12,576,768]{2,1,0:T(8,128)(2,1)S(1)}) fusion(f32[12,576,768]{2,1,0:T(8,128)} %get-tuple-element.194, f32[12,576,768]{2,1,0:T(8,128)} %get-tuple-element.187, f32[12,576]{1,0:T(8,128)S(1)} %get-tuple-element.121, f32[12]{0:T(128)S(1)} %copy-done.91, f32[12,576]{1,0:T(8,128)S(1)} %copy-done.51, ...), kind=kLoop, calls=%fused_computation.19 | loop fusion | flops 53084160 | bytes 106278960 | tf_op jit(solution)/shard_map/convert_element_type | solution.py:328
  945.9 11.9 multiply_bitcast_fusion.1
  989.8 47.8 %reduce-scatter.28.cloned.1.call-done = bf16[576,1536]{1,0:T(8,128)(2,1)} async-done(((bf16[1152,1536]{1,0:T(8,128)(2,1)}), bf16[576,1536]{1,0:T(8,128)(2,1)}) %reduce-scatter.28.cloned.1.call-update) | async-done | bytes 1769488 | tf_op jit(solution)/shard_map/reduce_scatter | solution.py:374
  1050.2 13.3 convolution_convert_fusion
  1063.6 13.1 convolution_convert_fusion.1
  1076.7 13.4 convolution_convert_fusion.2
  1171.6 12.9 fusion.106
  1184.5 12.7 fusion.105
  1208.3 46.1 %reduce-scatter.42.cloned.1.call-done = bf16[96,2048]{1,0:T(8,128)(2,1)} async-done(((bf16[1536,2048]{1,0:T(8,128)(2,1)}), bf16[96,2048]{1,0:T(8,128)(2,1)}) %reduce-scatter.42.cloned.1.call-update) | async-done | bytes 393232 | tf_op jit(solution)/shard_map/reduce_scatter | solution.py:456
  1256.4 86.8 %reduce-scatter.40.cloned.1.call-done = bf16[96,2048]{1,0:T(8,128)(2,1)} async-done(((bf16[1536,2048]{1,0:T(8,128)(2,1)}), bf16[96,2048]{1,0:T(8,128)(2,1)}) %reduce-scatter.40.cloned.1.call-update) | async-done | bytes 393232 | tf_op jit(solution)/shard_map/reduce_scatter | solution.py:453
  1345.1 63.9 %reduce-scatter.38.cloned.1.call-done = bf16[768,96]{0,1:T(8,128)(2,1)} async-done(((bf16[768,1536]{0,1:T(8,128)(2,1)}), bf16[768,96]{0,1:T(8,128)(2,1)}) %reduce-scatter.38.cloned.1.call-update) | async-done | bytes 147472 | tf_op jit(solution)/shard_map/reduce_scatter | solution.py:447
  1410.7 64.5 %reduce-scatter.36.cloned.1.call-done = bf16[96,768]{1,0:T(8,128)(2,1)} async-done(((bf16[1536,768]{1,0:T(8,128)(2,1)}), bf16[96,768]{1,0:T(8,128)(2,1)}) %reduce-scatter.36.cloned.1.call-update) | async-done | bytes 147472 | tf_op jit(solution)/shard_map/reduce_scatter | solution.py:438
  1476.8 64.0 %reduce-scatter.34.cloned.1.call-done = bf16[96,768]{1,0:T(8,128)(2,1)} async-done(((bf16[1536,768]{1,0:T(8,128)(2,1)}), bf16[96,768]{1,0:T(8,128)(2,1)}) %reduce-scatter.34.cloned.1.call-update) | async-done | bytes 147472 | tf_op jit(solution)/shard_map/reduce_scatter | solution.py:435
  1542.5 64.5 %reduce-scatter.32.cloned.1.call-done = bf16[96,768]{1,0:T(8,128)(2,1)} async-done(((bf16[1536,768]{1,0:T(8,128)(2,1)}), bf16[96,768]{1,0:T(8,128)(2,1)}) %reduce-scatter.32.cloned.1.call-update) | async-done | bytes 147472 | tf_op jit(solution)/shard_map/reduce_scatter | solution.py:432
  1608.6 67.3 %reduce-scatter.50.cloned.1.call-done = bf16[128,768]{1,0:T(8,128)(2,1)} async-done(((bf16[2048,768]{1,0:T(8,128)(2,1)}), bf16[128,768]{1,0:T(8,128)(2,1)}) %reduce-scatter.50.cloned.1.call-update) | async-done | bytes 196624
  1678.0 66.8 %reduce-scatter.48.cloned.1.call-done = bf16[128,768]{1,0:T(8,128)(2,1)} async-done(((bf16[2048,768]{1,0:T(8,128)(2,1)}), bf16[128,768]{1,0:T(8,128)(2,1)}) %reduce-scatter.48.cloned.1.call-update) | async-done | bytes 196624
  1753.8 118.8 %all-reduce.3.cloned.1.call-done = (f32[6144]{0:T(1024)}, f32[4,1536]{1,0:T(4,128)}, f32[3,24,64]{2,1,0:T(8,128)}, f32[24]{0:T(128)}) async-done(((f32[6144]{0:T(1024)}, f32[4,1536]{1,0:T(4,128)}, f32[3,24,64]{2,1,0:T(8,128)}, f32[24]{0:T(128)}), (f32[6144]{0:T(1024)}, f32[4,1536]{1,0:T(4,128)}, f32[3,24,64]{2,1,0:T(8,128)}, f32[24]{0:T(128)})) %all-reduce.3.cloned.1.call-update) | async-done | bytes 67696 | tf_op jit(solution)/shard_map/psum | solution.py:414
  1878.0 85.2 %reduce-scatter.30.cloned.1.call-done = bf16[64,3072]{1,0:T(8,128)(2,1)} async-done(((bf16[1024,3072]{1,0:T(8,128)(2,1)}), bf16[64,3072]{1,0:T(8,128)(2,1)}) %reduce-scatter.30.cloned.1.call-update) | async-done | bytes 393232 | tf_op jit(solution)/shard_map/reduce_scatter | solution.py:450
  (409 shorter events, 372.9 us)
Async XLA Ops:
  7.2 31.3 %copy-start = (bf16[3,256,2048]{2,1,0:T(8,128)(2,1)S(1)}, bf16[3,256,2048]{2,1,0:T(8,128)(2,1)}, u32[]{:S(2)}) copy-start(bf16[3,256,2048]{2,1,0:T(8,128)(2,1)} %param.28) | copy-start | bytes 9437188
  7.2 77.1 %all-gather.5.cloned.1.call-start = ((), (), s32[]{:S(2)}) async-start(), calls=%async_computation.15 | async-start | bytes 5308416 | tf_op jit(solution)/shard_map/all_gather | solution.py:144
  10.1 15.8 copy-start.79
  32.9 273.3 %reduce-scatter.22.cloned.1.call-start = ((), (), s32[]{:S(2)}) async-start(), calls=%async_computation.16 | async-start | bytes 5308416 | tf_op jit(solution)/shard_map/reduce_scatter | solution.py:219
  43.7 55.5 %copy-start.42 = (f32[1152,32]{0,1:T(8,128)}, f32[1152,32]{0,1:T(8,128)S(1)}, u32[]{:S(2)}) copy-start(f32[1152,32]{0,1:T(8,128)S(1)} %get-tuple-element.162) | copy-start | bytes 442372
  43.7 55.5 %copy-start.44 = (f32[1152,32]{0,1:T(8,128)}, f32[1152,32]{0,1:T(8,128)S(1)}, u32[]{:S(2)}) copy-start(f32[1152,32]{0,1:T(8,128)S(1)} %get-tuple-element.163) | copy-start | bytes 442372
  100.2 34.6 %copy-start.25 = (bf16[1152,12,32]{0,2,1:T(8,128)(2,1)}, bf16[1152,12,32]{0,2,1:T(8,128)(2,1)S(1)}, u32[]{:S(2)}) copy-start(bf16[1152,12,32]{0,2,1:T(8,128)(2,1)S(1)} %get-tuple-element.145) | copy-start | bytes 2654212
  100.2 34.6 %copy-start.26 = (bf16[1152,12,32]{0,2,1:T(8,128)(2,1)}, bf16[1152,12,32]{0,2,1:T(8,128)(2,1)S(1)}, u32[]{:S(2)}) copy-start(bf16[1152,12,32]{0,2,1:T(8,128)(2,1)S(1)} %get-tuple-element.146) | copy-start | bytes 2654212
  100.8 20.3 %copy-start.20 = (bf16[576,12,64]{0,2,1:T(8,128)(2,1)}, bf16[576,12,64]{0,2,1:T(8,128)(2,1)S(1)}, u32[]{:S(2)}) copy-start(bf16[576,12,64]{0,2,1:T(8,128)(2,1)S(1)} %get-tuple-element.156) | copy-start | bytes 2654212
  100.8 34.0 %copy-start.16 = (bf16[576,12,64]{0,2,1:T(8,128)(2,1)}, bf16[576,12,64]{0,2,1:T(8,128)(2,1)S(1)}, u32[]{:S(2)}) copy-start(bf16[576,12,64]{0,2,1:T(8,128)(2,1)S(1)} %get-tuple-element.157) | copy-start | bytes 2654212
  111.9 121.1 %copy-start.56 = (f32[12,576]{1,0:T(8,128)}, f32[12,576]{1,0:T(8,128)S(1)}, u32[]{:S(2)}) copy-start(f32[12,576]{1,0:T(8,128)S(1)} %get-tuple-element.186) | copy-start | bytes 82948
  121.0 13.7 copy-start.32
  134.7 33.7 %copy-start.52 = (f32[12,576]{1,0:T(8,128)}, f32[12,576]{1,0:T(8,128)S(1)}, u32[]{:S(2)}) copy-start(f32[12,576]{1,0:T(8,128)S(1)} %get-tuple-element.184) | copy-start | bytes 82948
  148.3 50.0 %copy-start.54 = (f32[12,576]{1,0:T(8,128)}, f32[12,576]{1,0:T(8,128)S(1)}, u32[]{:S(2)}) copy-start(f32[12,576]{1,0:T(8,128)S(1)} %get-tuple-element.178) | copy-start | bytes 82948
  148.3 15.6 copy-start.97
  148.3 15.6 copy-start.104
  198.3 14.8 copy-start.60
  258.3 49.8 %copy-start.65 = (f32[1536]{0:T(1024)S(1)}, f32[1536]{0:T(1024)}, u32[]{:S(2)}) copy-start(f32[1536]{0:T(1024)} %param.35) | copy-start | bytes 18436
  258.4 109.2 %all-gather.7.cloned.1.call-start = ((), (), s32[]{:S(2)}) async-start(), calls=%async_computation.17 | async-start | bytes 5308416 | tf_op jit(solution)/shard_map/all_gather | solution.py:229
  318.1 136.2 %reduce-scatter.24.cloned.1.call-start = ((), (), s32[]{:S(2)}) async-start(), calls=%async_computation.18 | async-start | bytes 5308416 | tf_op jit(solution)/shard_map/reduce_scatter | solution.py:235
  367.6 13.5 copy-start.98
  367.6 29.8 %slice-start.4 = ((s8[6291456]{0:T(1024)(128)(4,1)}), s8[4194304]{0:T(1024)(128)(4,1)S(1)}, s32[]{:S(2)}) async-start(s8[6291456]{0:T(1024)(128)(4,1)} %bitcast.247), calls=%async_computation.39 | async-start | bytes 8388608
  381.1 16.3 slice-start.5
  406.4 49.8 %copy-start.78 = (f32[1536]{0:T(1024)S(1)}, f32[1536]{0:T(1024)}, u32[]{:S(2)}) copy-start(f32[1536]{0:T(1024)} %param.37) | copy-start | bytes 18436
  406.5 109.5 %all-gather.9.cloned.1.call-start = ((), (), s32[]{:S(2)}) async-start(), calls=%async_computation.19 | async-start | bytes 5308416 | tf_op jit(solution)/shard_map/all_gather | solution.py:249
  466.5 139.5 %reduce-scatter.26.cloned.1.call-start = ((), (), s32[]{:S(2)}) async-start(), calls=%async_computation.20 | async-start | bytes 5308416 | tf_op jit(solution)/shard_map/reduce_scatter | solution.py:258
  558.1 123.6 %all-gather.11.cloned.1.call-start = ((), (), s32[]{:S(2)}) async-start(), calls=%async_computation.21 | async-start | bytes 5308416 | tf_op jit(solution)/shard_map/all_gather | solution.py:274
  605.9 17.2 slice-start
  611.8 13.2 slice-start.3
  632.2 405.4 %reduce-scatter.28.cloned.1.call-start = ((), (), s32[]{:S(2)}) async-start(), calls=%async_computation.22 | async-start | bytes 5308416 | tf_op jit(solution)/shard_map/reduce_scatter | solution.py:374
  779.3 14.8 copy-start.27
  794.1 24.3 %copy-start.14 = (bf16[576,768]{0,1:T(8,128)(2,1)S(1)}, bf16[576,768]{0,1:T(8,128)(2,1)}, u32[]{:S(2)}) copy-start(bf16[576,768]{0,1:T(8,128)(2,1)} %copy.71) | copy-start | bytes 2654212
  989.7 47.9 %copy-start.76 = (f32[1536]{0:T(1024)S(1)}, f32[1536]{0:T(1024)}, u32[]{:S(2)}) copy-start(f32[1536]{0:T(1024)} %param.34) | copy-start | bytes 18436
  989.7 47.9 %copy-start.80 = (f32[576]{0:T(1024)S(1)}, f32[576]{0:T(1024)}, u32[]{:S(2)}) copy-start(f32[576]{0:T(1024)} %copy-done.79) | copy-start | bytes 6916
  989.8 52.9 %copy-start.67 = (s32[576]{0:T(1024)S(1)}, s32[576]{0:T(1024)}, u32[]{:S(2)}) copy-start(s32[576]{0:T(1024)} %copy-done.66) | copy-start | bytes 6916
  989.8 208.1 %reduce-scatter.46.cloned.1.call-start = ((), (), s32[]{:S(2)}) async-start(), calls=%async_computation.31 | async-start | bytes 2359296
  1050.2 156.2 %reduce-scatter.44.cloned.1.call-start = ((), (), s32[]{:S(2)}) async-start(), calls=%async_computation.30 | async-start | bytes 6684672 | tf_op jit(solution)/shard_map/reduce_scatter | solution.py:459
  1063.5 190.9 %reduce-scatter.42.cloned.1.call-start = ((), (), s32[]{:S(2)}) async-start(), calls=%async_computation.29 | async-start | bytes 6684672 | tf_op jit(solution)/shard_map/reduce_scatter | solution.py:456
  1076.7 266.5 %reduce-scatter.40.cloned.1.call-start = ((), (), s32[]{:S(2)}) async-start(), calls=%async_computation.28 | async-start | bytes 6684672 | tf_op jit(solution)/shard_map/reduce_scatter | solution.py:453
  1090.1 318.9 %reduce-scatter.38.cloned.1.call-start = ((), (), s32[]{:S(2)}) async-start(), calls=%async_computation.27 | async-start | bytes 2506752 | tf_op jit(solution)/shard_map/reduce_scatter | solution.py:447
  1097.9 377.3 %reduce-scatter.36.cloned.1.call-start = ((), (), s32[]{:S(2)}) async-start(), calls=%async_computation.26 | async-start | bytes 2506752 | tf_op jit(solution)/shard_map/reduce_scatter | solution.py:438
  1105.6 435.2 %reduce-scatter.34.cloned.1.call-start = ((), (), s32[]{:S(2)}) async-start(), calls=%async_computation.25 | async-start | bytes 2506752 | tf_op jit(solution)/shard_map/reduce_scatter | solution.py:435
  1113.1 493.9 %reduce-scatter.32.cloned.1.call-start = ((), (), s32[]{:S(2)}) async-start(), calls=%async_computation.24 | async-start | bytes 2506752 | tf_op jit(solution)/shard_map/reduce_scatter | solution.py:432
  1120.5 555.5 %reduce-scatter.50.cloned.1.call-start = ((), (), s32[]{:S(2)}) async-start(), calls=%async_computation.33 | async-start | bytes 3342336
  1148.1 596.7 %reduce-scatter.48.cloned.1.call-start = ((), (), s32[]{:S(2)}) async-start(), calls=%async_computation.32 | async-start | bytes 3342336
  1171.0 701.6 %all-reduce.3.cloned.1.call-start = ((), (), s32[]{:S(2)}) async-start(), calls=%async_computation.34 | async-start | bytes 173056 | tf_op jit(solution)/shard_map/psum | solution.py:414
  1184.5 16.2 copy-start.81
  1200.4 762.9 %reduce-scatter.30.cloned.1.call-start = ((), (), s32[]{:S(2)}) async-start(), calls=%async_computation.23 | async-start | bytes 6684672 | tf_op jit(solution)/shard_map/reduce_scatter | solution.py:450
  (88 other events, 502.1 us)
Sparse Core Ops, SparseCore 0:
  33.1 51.1 all-gather.4
  258.5 47.6 reduce-scatter.21
  318.2 49.3 all-gather.6
  406.6 47.6 reduce-scatter.23
  466.6 49.3 all-gather.8
  558.2 47.6 reduce-scatter.25
  632.3 49.3 all-gather.10
  989.9 47.6 reduce-scatter.27
  1050.3 26.0 reduce-scatter.45
  1080.7 85.2 reduce-scatter.43
  1169.9 84.4 reduce-scatter.41
  1258.7 84.4 reduce-scatter.39
  1347.0 62.0 reduce-scatter.37
  1413.2 61.9 reduce-scatter.35
  1478.8 61.9 reduce-scatter.33
  1544.9 62.0 reduce-scatter.31
  1610.7 65.2 reduce-scatter.49
  1679.6 65.0 reduce-scatter.47
  1752.1 120.5 all-reduce.2
  1876.4 86.7 reduce-scatter.29
where the time goes:
time: 1980 us; the launch traced here: 1970 us
  waiting for transfers between devices  1100 us (56%)
  matrix products  561 us (28%)
  other arithmetic  233 us (12%)
  local copies, waits for them, and re-layouts  57.8 us (3%)
    unnamed x23, waiting for transfers between devices  134 us
    psum x1, waiting for transfers between devices, on_device(): lax.psum((norm_parts, head_parts, gate_parts, bias_parts), ('dp', 'tensor'))  119 us
    reduce_scatter x1, waiting for transfers between devices, on_device(): lax.psum_scatter(gate_grad.astype(jnp.bfloat16), 'dp', scatter_dimension=...  86.8 us
    reduce_scatter x1, waiting for transfers between devices, on_device(): lax.psum_scatter(ada_grad.astype(jnp.bfloat16), 'dp', scatter_dimension=0...  85.2 us
    dot_general x9, matrix products, outer(): lax.dot_general(left, right, (((0,), (0,)), ((), ())), preferred_element_...  77.6 us
    reduce_scatter x1, waiting for transfers between devices, on_device(): lax.psum_scatter(query_grad.astype(jnp.bfloat16), 'dp', scatter_dimension...  64.5 us
    reduce_scatter x1, waiting for transfers between devices, on_device(): lax.psum_scatter(value_grad.astype(jnp.bfloat16), 'dp', scatter_dimension...  64.5 us
    reduce_scatter x1, waiting for transfers between devices, on_device(): lax.psum_scatter(key_grad.astype(jnp.bfloat16), 'dp', scatter_dimension=0...  64 us
  transfers between devices with their start and end apart: 20, of which 18 were waited for; matrix products, arithmetic and copies ran while one was open for 10% of the time, Pallas kernels for 0%

commit v1 on v0

v1 whole, which is shorter than its diff:
```python
import math

import jax
import jax.numpy as jnp
from jax import lax
from jax.experimental import pallas as pl
from jax.experimental.pallas import tpu as pltpu
from jax.sharding import PartitionSpec as P

epsilon = 1e-05
penalty = 1024.0
theta = 10000.0
lanes = 128
half_lanes = 64
query_block = 256
bf16 = jnp.bfloat16
f32 = jnp.float32
vmem_bytes = 60 * 1024 * 1024


def sigmoid_of(values):
    return 1.0 / (1.0 + jnp.exp(-values))


def unit_rows(values):
    factor = lax.rsqrt(jnp.mean(values * values, axis=-1, keepdims=True) + epsilon)
    return (values * factor, factor)


def unit_back(gradient, normed, factor):
    return factor * (gradient - normed * jnp.mean(gradient * normed, axis=-1, keepdims=True))


def dot_nn(left, right):
    return lax.dot_general(left, right, (((1,), (0,)), ((), ())), preferred_element_type=f32)


def dot_nt(left, right):
    return lax.dot_general(left, right, (((1,), (1,)), ((), ())), preferred_element_type=f32)


def dot_tn(left, right):
    return lax.dot_general(left, right, (((0,), (0,)), ((), ())), preferred_element_type=f32)


def lane_index(rows):
    return lax.broadcasted_iota(jnp.int32, (rows, lanes), 1)


def halves_matrix(crossed):
    row = lax.broadcasted_iota(jnp.int32, (lanes, lanes), 0) // half_lanes
    col = lax.broadcasted_iota(jnp.int32, (lanes, lanes), 1) // half_lanes
    same = (row != col) if crossed else (row == col)
    return jnp.where(same, 1.0, 0.0).astype(bf16)


def half_sums(values, matrix):
    high = values.astype(bf16)
    rest = (values - high.astype(f32)).astype(bf16)
    return dot_nn(high, matrix) + dot_nn(rest, matrix)


def head_unit(values, matrix):
    factor = lax.rsqrt(half_sums(values * values, matrix) * (1.0 / half_lanes) + epsilon)
    return values * factor, factor


def head_unit_back(gradient, normed, factor, matrix):
    mean = half_sums(gradient * normed, matrix) * (1.0 / half_lanes)
    return factor * (gradient - normed * mean)


def swap_quarters(values):
    lane = lane_index(values.shape[0])
    ahead = pltpu.roll(values, lanes - 32, 1)
    behind = pltpu.roll(values, 32, 1)
    return jnp.where(lane % half_lanes < 32, ahead, behind)


def three_parts(values):
    first = values.astype(bf16)
    rest = values - first.astype(f32)
    second = rest.astype(bf16)
    third = (rest - second.astype(f32)).astype(bf16)
    return first, second, third


def put_lanes(target, place, head, values):
    lane = lane_index(target.shape[0])
    base = half_lanes * (1 - head) + place
    for offset, part in enumerate(three_parts(values)):
        target = jnp.where(lane == base + offset, part, target)
    return target


def both(head_zero, head_one):
    return jnp.where(lane_index(head_zero.shape[0]) < half_lanes, head_zero, head_one)


def pair_operands(values, features):
    return both(values, features), both(features, values)


def blocks_of(rows):
    starts = list(range(0, rows, query_block))
    return [(start, min(query_block, rows - start)) for start in starts]


def forward_kernel(block_count, image_count, present, *refs):
    q_refs = refs[:block_count]
    k_refs = refs[block_count : 2 * block_count]
    v_refs = refs[2 * block_count : 3 * block_count]
    (
        ck_ref,
        cv_ref,
        gain_ref,
        cos_ref,
        sin_ref,
        fq_ref,
        fk_ref,
        fc_ref,
        mixed_ref,
        so_ref,
        co_ref,
        qa_ref,
        ka_ref,
        ca_ref,
        va_ref,
        cva_ref,
        acc_ref,
    ) = refs[3 * block_count :]
    rows = cos_ref.shape[0]
    cap_rows = ck_ref.shape[0] // image_count
    same = halves_matrix(False)
    q_raw = jnp.concatenate([ref[...] for ref in q_refs], axis=0).astype(f32)
    k_raw = jnp.concatenate([ref[...] for ref in k_refs], axis=0).astype(f32)
    cosine = cos_ref[...]
    sine = sin_ref[...]
    q_gained = head_unit(q_raw, same)[0] * gain_ref[0, 0:1, :]
    q_turned = q_gained * cosine + swap_quarters(q_gained) * sine
    queries = (q_turned.astype(bf16).astype(f32) * (1.0 / math.sqrt(half_lanes))).astype(bf16)
    k_gained = head_unit(k_raw, same)[0] * gain_ref[0, 1:2, :]
    keys = (k_gained * cosine + swap_quarters(k_gained) * sine).astype(bf16)
    cap_keys = (head_unit(ck_ref[...].astype(f32), same)[0] * gain_ref[0, 2:3, :]).astype(bf16)
    values = jnp.concatenate([ref[...] for ref in v_refs], axis=0)
    cap_values = cv_ref[...]
    ones = jnp.ones_like(values)
    cap_ones = jnp.ones_like(cap_values)
    for head, (qa, ka, ca, va, cva) in enumerate(
        zip(
            pair_operands(queries, fq_ref[...]),
            pair_operands(keys, fk_ref[...]),
            pair_operands(cap_keys, fc_ref[...]),
            pair_operands(values, ones),
            pair_operands(cap_values, cap_ones),
        )
    ):
        span = slice(head * lanes, (head + 1) * lanes)
        qa_ref[:, span] = qa
        ka_ref[:, span] = ka
        ca_ref[:, span] = ca
        va_ref[:, span] = va
        cva_ref[:, span] = cva
    gate = gain_ref[0, 3:4, :]
    for index, (start, size) in enumerate(blocks_of(rows)):
        own = slice(start, start + size)
        self_parts = []
        for head in range(2):
            span = slice(head * lanes, (head + 1) * lanes)
            scores = dot_nt(qa_ref[own, span], ka_ref[:, span])
            self_parts.append(dot_nn(jnp.exp(scores).astype(bf16), va_ref[:, span]))
        acc_ref[0:size, :] = jnp.zeros((size, 2 * lanes), f32)
        for image in range(image_count):

            @pl.when(present[index * image_count + image] > 0)
            def _():
                caps = slice(image * cap_rows, (image + 1) * cap_rows)
                for head in range(2):
                    span = slice(head * lanes, (head + 1) * lanes)
                    scores = dot_nt(qa_ref[own, span], ca_ref[caps, span])
                    acc_ref[0:size, span] += dot_nn(
                        jnp.exp(scores).astype(bf16), cva_ref[caps, span]
                    )

        cross_parts = [acc_ref[0:size, 0:lanes], acc_ref[0:size, lanes:]]
        outs = []
        for parts in (self_parts, cross_parts):
            total = pltpu.roll(both(parts[1], parts[0]), half_lanes, 1)
            outs.append(both(parts[0], parts[1]) / total)
        so_ref[own, :] = outs[0].astype(bf16)
        co_ref[own, :] = outs[1].astype(bf16)
        mixed_ref[own, :] = (outs[0] + gate * outs[1]).astype(bf16)
        for head in range(2):
            span = slice(head * lanes, (head + 1) * lanes)
            qa = qa_ref[own, span]
            qa = put_lanes(qa, 3, head, -jnp.log(self_parts[head]))
            qa = put_lanes(qa, 6, head, -jnp.log(cross_parts[head]))
            qa_ref[own, span] = qa


def backward_kernel(block_count, image_count, present, *refs):
    q_refs = refs[:block_count]
    k_refs = refs[block_count : 2 * block_count]
    v_refs = refs[2 * block_count : 3 * block_count]
    (
        ck_ref,
        cv_ref,
        gain_ref,
        cos_ref,
        sin_ref,
        so_ref,
        co_ref,
        qa_ref,
        ka_ref,
        ca_ref,
        gm_ref,
        gq_ref,
        gk_ref,
        gv_ref,
        gck_ref,
        gcv_ref,
        stat_ref,
        ga_ref,
        va_ref,
        cva_ref,
        kt_ref,
        ct_ref,
        dq_ref,
        dk_ref,
        dv_ref,
        dck_ref,
        dcv_ref,
    ) = refs[3 * block_count :]
    rows = cos_ref.shape[0]
    cap_rows = ck_ref.shape[0] // image_count
    same = halves_matrix(False)
    crossed = halves_matrix(True)
    grads = gm_ref[...]
    grads_float = grads.astype(f32)
    cross_product = grads_float * co_ref[...].astype(f32)
    self_delta = half_sums(grads_float * so_ref[...].astype(f32), crossed)
    cross_delta = half_sums(cross_product, crossed)
    values = jnp.concatenate([ref[...] for ref in v_refs], axis=0)
    blank = jnp.zeros_like(grads)
    lane = lane_index(rows) % half_lanes
    self_ones = jnp.where(lane < 3, 1.0, 0.0).astype(bf16)
    lane_cap = lane_index(ck_ref.shape[0]) % half_lanes
    cross_ones = jnp.where((lane_cap >= 3) & (lane_cap < 6), 1.0, 0.0).astype(bf16)
    for head, (ga, va, cva) in enumerate(
        zip(
            pair_operands(grads, blank),
            pair_operands(values, self_ones),
            pair_operands(cv_ref[...], cross_ones),
        )
    ):
        span = slice(head * lanes, (head + 1) * lanes)
        ga = put_lanes(ga, 0, head, -self_delta)
        ga = put_lanes(ga, 3, head, -cross_delta)
        ga_ref[:, span] = ga
        va_ref[:, span] = va
        cva_ref[:, span] = cva
        kt_ref[span, :] = ka_ref[:, span].astype(f32).T.astype(bf16)
        ct_ref[span, :] = ca_ref[:, span].astype(f32).T.astype(bf16)
    dk_ref[...] = jnp.zeros_like(dk_ref)
    dv_ref[...] = jnp.zeros_like(dv_ref)
    dck_ref[...] = jnp.zeros_like(dck_ref)
    dcv_ref[...] = jnp.zeros_like(dcv_ref)
    for index, (start, size) in enumerate(blocks_of(rows)):
        own = slice(start, start + size)
        for head in range(2):
            span = slice(head * lanes, (head + 1) * lanes)
            top = head * half_lanes
            place = slice(head * lanes + top, head * lanes + top + half_lanes)
            qa = qa_ref[own, span]
            ga = ga_ref[own, span]
            probs = jnp.exp(dot_nt(ka_ref[:, span], qa))
            grad_scores = (probs * dot_nt(va_ref[:, span], ga)).astype(bf16)
            dv_ref[:, span] += dot_nn(probs.astype(bf16), ga)
            dk_ref[:, span] += dot_nn(grad_scores, qa)
            dq_ref[top : top + half_lanes, own] = dot_nn(kt_ref[place, :], grad_scores)
        for image in range(image_count):

            @pl.when(present[index * image_count + image] > 0)
            def _():
                caps = slice(image * cap_rows, (image + 1) * cap_rows)
                for head in range(2):
                    span = slice(head * lanes, (head + 1) * lanes)
                    top = head * half_lanes
                    place = slice(head * lanes + top, head * lanes + top + half_lanes)
                    gate = gain_ref[0, 3:4, top : top + 1]
                    qa = qa_ref[own, span]
                    ga = ga_ref[own, span]
                    probs = jnp.exp(dot_nt(ca_ref[caps, span], qa))
                    grad_scores = (probs * dot_nt(cva_ref[caps, span], ga)).astype(bf16)
                    dcv_ref[caps, span] += dot_nn(probs.astype(bf16), ga)
                    dck_ref[caps, span] += dot_nn(grad_scores, qa)
                    dq_ref[top : top + half_lanes, own] += gate * dot_nn(
                        ct_ref[place, caps], grad_scores
                    )

    cosine = cos_ref[...]
    sine = sin_ref[...]
    gate_row = gain_ref[0, 3:4, :]
    scale = 1.0 / math.sqrt(half_lanes)
    sums = []
    for refs_of, place, out_ref, grad in (
        (q_refs, 0, gq_ref, dq_ref[...].T * scale),
        (k_refs, 1, gk_ref, both(dk_ref[:, 0:lanes], dk_ref[:, lanes:])),
    ):
        raw = jnp.concatenate([ref[...] for ref in refs_of], axis=0).astype(f32)
        normed, factor = head_unit(raw, same)
        turned = grad * cosine - swap_quarters(grad) * sine
        sums.append(jnp.sum(turned * normed, axis=0, keepdims=True))
        gain = gain_ref[0, place : place + 1, :]
        out_ref[...] = head_unit_back(turned * gain, normed, factor, same).astype(bf16)
    gv_ref[...] = both(dv_ref[:, 0:lanes], dv_ref[:, lanes:]).astype(bf16)
    grad = both(dck_ref[:, 0:lanes], dck_ref[:, lanes:]) * gate_row
    normed, factor = head_unit(ck_ref[...].astype(f32), same)
    sums.append(jnp.sum(grad * normed, axis=0, keepdims=True))
    gck_ref[...] = head_unit_back(grad * gain_ref[0, 2:3, :], normed, factor, same).astype(bf16)
    gcv_ref[...] = (both(dcv_ref[:, 0:lanes], dcv_ref[:, lanes:]) * gate_row).astype(bf16)
    sums.append(jnp.sum(cross_product, axis=0, keepdims=True))
    stat_ref[0] = jnp.concatenate(sums + [jnp.zeros((4, lanes), f32)], axis=0)


def columns_spec(rows, width):
    return pl.BlockSpec((rows, width), lambda pair, *_: (0, pair))


def whole_spec(rows):
    return pl.BlockSpec((rows, lanes), lambda pair, *_: (0, 0))


def gain_spec():
    return pl.BlockSpec((1, 8, lanes), lambda pair, *_: (pair, 0, 0))


def attention_forward(present, q_raw, k_raw, values, ck_raw, cap_values, gains, tables, images):
    cosine, sine, fq, fk, fc = tables
    count = len(q_raw)
    local = q_raw[0].shape[0]
    rows = local * count
    caps = ck_raw.shape[0]
    pairs = q_raw[0].shape[1] // lanes
    width = pairs * lanes
    grid = pltpu.PrefetchScalarGridSpec(
        num_scalar_prefetch=1,
        grid=(pairs,),
        in_specs=[columns_spec(local, lanes)] * (3 * count)
        + [columns_spec(caps, lanes)] * 2
        + [gain_spec()]
        + [whole_spec(rows)] * 4
        + [whole_spec(caps)],
        out_specs=[columns_spec(rows, lanes)] * 3
        + [columns_spec(rows, 2 * lanes)] * 2
        + [columns_spec(caps, 2 * lanes)],
        scratch_shapes=[
            pltpu.VMEM((rows, 2 * lanes), bf16),
            pltpu.VMEM((caps, 2 * lanes), bf16),
            pltpu.VMEM((query_block, 2 * lanes), f32),
        ],
    )
    return pl.pallas_call(
        lambda *refs: forward_kernel(count, images, *refs),
        grid_spec=grid,
        out_shape=[jax.ShapeDtypeStruct((rows, width), bf16)] * 3
        + [jax.ShapeDtypeStruct((rows, 2 * width), bf16)] * 2
        + [jax.ShapeDtypeStruct((caps, 2 * width), bf16)],
        compiler_params=pltpu.CompilerParams(vmem_limit_bytes=vmem_bytes),
        name="attention_forward",
    )(present, *q_raw, *k_raw, *values, ck_raw, cap_values, gains, cosine, sine, fq, fk, fc)


def attention_backward(
    present, q_raw, k_raw, values, ck_raw, cap_values, gains, tables, kept, grad_mixed, images
):
    cosine, sine = tables[:2]
    self_out, cross_out, qa, ka, ca = kept
    count = len(q_raw)
    local = q_raw[0].shape[0]
    rows = local * count
    caps = ck_raw.shape[0]
    pairs = q_raw[0].shape[1] // lanes
    width = pairs * lanes
    grid = pltpu.PrefetchScalarGridSpec(
        num_scalar_prefetch=1,
        grid=(pairs,),
        in_specs=[columns_spec(local, lanes)] * (3 * count)
        + [columns_spec(caps, lanes)] * 2
        + [gain_spec()]
        + [whole_spec(rows)] * 2
        + [columns_spec(rows, lanes)] * 2
        + [columns_spec(rows, 2 * lanes)] * 2
        + [columns_spec(caps, 2 * lanes)]
        + [columns_spec(rows, lanes)],
        out_specs=[columns_spec(rows, lanes)] * 3
        + [columns_spec(caps, lanes)] * 2
        + [gain_spec()],
        scratch_shapes=[
            pltpu.VMEM((rows, 2 * lanes), bf16),
            pltpu.VMEM((rows, 2 * lanes), bf16),
            pltpu.VMEM((caps, 2 * lanes), bf16),
            pltpu.VMEM((2 * lanes, rows), bf16),
            pltpu.VMEM((2 * lanes, caps), bf16),
            pltpu.VMEM((lanes, rows), f32),
            pltpu.VMEM((rows, 2 * lanes), f32),
            pltpu.VMEM((rows, 2 * lanes), f32),
            pltpu.VMEM((caps, 2 * lanes), f32),
            pltpu.VMEM((caps, 2 * lanes), f32),
        ],
    )
    return pl.pallas_call(
        lambda *refs: backward_kernel(count, images, *refs),
        grid_spec=grid,
        out_shape=[jax.ShapeDtypeStruct((rows, width), bf16)] * 3
        + [jax.ShapeDtypeStruct((caps, width), bf16)] * 2
        + [jax.ShapeDtypeStruct((pairs, 8, lanes), f32)],
        compiler_params=pltpu.CompilerParams(vmem_limit_bytes=vmem_bytes),
        name="attention_backward",
    )(
        present,
        *q_raw,
        *k_raw,
        *values,
        ck_raw,
        cap_values,
        gains,
        cosine,
        sine,
        self_out,
        cross_out,
        qa,
        ka,
        ca,
        grad_mixed,
    )


def gather_blocks(block):
    count = lax.axis_size("tensor")
    return [block] + [
        lax.ppermute(block, "tensor", [((i + step) % count, i) for i in range(count)])
        for step in range(1, count)
    ]


def scatter_blocks(own, others):
    count = lax.axis_size("tensor")
    for step in range(1, count):
        moved = lax.ppermute(
            others[step - 1].astype(bf16),
            "tensor",
            [(i, (i + step) % count) for i in range(count)],
        )
        own = own + moved.astype(f32)
    return own


def per_token(table, images):
    rows = table[0:1]
    for image in range(1, table.shape[0]):
        rows = jnp.where(images[:, None] == image, table[image : image + 1], rows)
    return rows


def image_sums(values, images, count):
    chosen = (jnp.arange(count, dtype=jnp.int32)[:, None] == images[None, :]).astype(bf16)
    return dot_nn(chosen, values.astype(bf16))


def rope_tables(positions):
    lane = jnp.arange(lanes, dtype=jnp.int32)
    place = lane % 32
    freqs = jnp.power(theta, -((place % 16).astype(f32) / 16))
    spot = jnp.where(place[None, :] < 16, positions[0][:, None], positions[1][:, None])
    angles = spot.astype(f32) * freqs[None, :]
    sign = jnp.where(lane % half_lanes < 32, -1.0, 1.0)
    return (jnp.cos(angles), jnp.sin(angles) * sign[None, :])


def feature_lanes(images, valid, count, ones_at):
    lane = (jnp.arange(lanes, dtype=jnp.int32) % half_lanes)[None, :]
    outside = (lane < count) & ((lane != images[:, None]) | ~valid[:, None])
    ones = (lane >= ones_at) & (lane < ones_at + 3)
    return jnp.where(outside, -penalty, jnp.where(ones, 1.0, 0.0)).astype(bf16)


def pad_columns(values, width):
    return jnp.pad(values, ((0, 0), (0, width - values.shape[1])))


def on_device(
    tokens,
    timestep,
    caption,
    caption_mask,
    image_lengths,
    patch_pos,
    ada_weight,
    ada_bias,
    attention_norm,
    attention_post,
    feedforward_norm,
    feedforward_post,
    query_weight,
    key_weight,
    value_weight,
    query_gain,
    key_gain,
    cross_keys,
    cross_values,
    cross_gain,
    cross_gate,
    output_weight,
    gate_weight,
    up_weight,
    down_weight,
    cotangent,
):
    local_rows, model_width = tokens.shape
    tensor_count = lax.axis_size("tensor")
    tensor_place = lax.axis_index("tensor")
    group_tokens = local_rows * tensor_count
    image_count, cap_len, cap_width = caption.shape
    local_heads, head_size = query_gain.shape
    head_columns = local_heads * head_size
    pairs = (local_heads + 1) // 2
    pair_columns = pairs * lanes
    cap_total = image_count * cap_len

    token_blocks = gather_blocks(tokens)

    places = (
        jnp.arange(group_tokens, dtype=jnp.int32) + tensor_place * local_rows
    ) % group_tokens
    image_all = jnp.zeros((group_tokens,), jnp.int32)
    end = jnp.zeros((), jnp.int32)
    for image in range(image_count - 1):
        end = end + image_lengths[image]
        image_all = image_all + (places >= end).astype(jnp.int32)
    image_own = image_all[:local_rows]
    positions = jnp.roll(patch_pos, -tensor_place * local_rows, axis=1)
    cosine, sine = rope_tables(positions)
    lane = (jnp.arange(lanes, dtype=jnp.int32) % half_lanes)[None, :]
    query_features = (lane == image_all[:, None]).astype(bf16)
    everywhere = jnp.ones((group_tokens,), jnp.bool_)
    key_features = feature_lanes(image_all, everywhere, image_count, 3)
    cap_features = feature_lanes(
        jnp.arange(cap_total, dtype=jnp.int32) // cap_len,
        caption_mask.reshape(-1) > 0,
        image_count,
        6,
    )
    block_total = -(-group_tokens // query_block)
    block_place = jnp.arange(group_tokens, dtype=jnp.int32) // query_block
    hit = (block_place[None, None, :] == jnp.arange(block_total)[:, None, None]) & (
        image_all[None, None, :] == jnp.arange(image_count)[None, :, None]
    )
    present = jnp.max(hit.astype(jnp.int32), axis=2).reshape(-1)
    head_gate = jnp.tanh(cross_gate)
    gain_rows = jnp.stack(
        [
            query_gain.reshape(-1),
            key_gain.reshape(-1),
            cross_gain.reshape(-1),
            jnp.repeat(head_gate, head_size),
        ]
    )
    gains = (
        jnp.pad(gain_rows, ((0, 4), (0, pair_columns - head_columns)))
        .reshape(8, pairs, lanes)
        .transpose(1, 0, 2)
    )
    tables = (cosine, sine, query_features, key_features, cap_features)

    time_float = timestep.astype(f32)
    silu_time = (time_float * sigmoid_of(time_float)).astype(bf16)
    mod_part = dot_nn(silu_time, ada_weight) + ada_bias
    modulation = lax.all_gather(mod_part, "tensor", axis=1, tiled=True)
    scale_attn = 1.0 + modulation[:, :model_width]
    gate_attn = jnp.tanh(modulation[:, model_width : 2 * model_width])
    scale_ffn = 1.0 + modulation[:, 2 * model_width : 3 * model_width]
    gate_ffn = jnp.tanh(modulation[:, 3 * model_width :])
    norm_attn = scale_attn * attention_norm
    post_attn = gate_attn * attention_post
    norm_ffn = scale_ffn * feedforward_norm
    post_ffn = gate_ffn * feedforward_post

    cap_flat = caption.reshape(cap_total, cap_width)
    ck_raw = pad_columns(dot_nn(cap_flat, cross_keys), pair_columns)
    cap_values = pad_columns(dot_nn(cap_flat, cross_values).astype(bf16), pair_columns)

    normed, q_raw, k_raw, values = [], [], [], []
    for index, block in enumerate(token_blocks):
        images = image_all[index * local_rows : (index + 1) * local_rows]
        unit = unit_rows(block.astype(f32))[0]
        rows = (unit * per_token(norm_attn, images)).astype(bf16)
        normed.append(rows)
        q_raw.append(pad_columns(dot_nn(rows, query_weight), pair_columns))
        k_raw.append(pad_columns(dot_nn(rows, key_weight), pair_columns))
        values.append(pad_columns(dot_nn(rows, value_weight).astype(bf16), pair_columns))

    mixed, *kept = attention_forward(
        present, q_raw, k_raw, values, ck_raw, cap_values, gains, tables, image_count
    )
    mixed = mixed[:, :head_columns]

    def block_rows(array, index):
        return array[index * local_rows : (index + 1) * local_rows]

    attn_others = [
        dot_nn(block_rows(mixed, index), output_weight) for index in range(1, tensor_count)
    ]
    attn_rows = scatter_blocks(dot_nn(block_rows(mixed, 0), output_weight), attn_others)
    attn_unit, attn_factor = unit_rows(attn_rows)
    x_float = tokens.astype(f32)
    hidden = x_float + attn_unit * per_token(post_attn, image_own)
    hidden_unit, hidden_factor = unit_rows(hidden)
    ffn_in = gather_blocks((hidden_unit * per_token(norm_ffn, image_own)).astype(bf16))

    gate_pre, up_pre, inner, ffn_parts = [], [], [], []
    for rows in ffn_in:
        gate_block = dot_nn(rows, gate_weight)
        up_block = dot_nn(rows, up_weight)
        inner_block = (gate_block * sigmoid_of(gate_block) * up_block).astype(bf16)
        gate_pre.append(gate_block)
        up_pre.append(up_block)
        inner.append(inner_block)
        ffn_parts.append(dot_nn(inner_block, down_weight))
    ffn_rows = scatter_blocks(ffn_parts[0], ffn_parts[1:])
    ffn_unit, ffn_factor = unit_rows(ffn_rows)
    layer_out = (hidden + ffn_unit * per_token(post_ffn, image_own)).astype(bf16)

    grad_out = cotangent.astype(f32)
    sums_ffn_post = image_sums(grad_out * ffn_unit, image_own, image_count)
    grad_ffn = gather_blocks(
        unit_back(grad_out * per_token(post_ffn, image_own), ffn_unit, ffn_factor).astype(bf16)
    )
    grad_gate, grad_up, grad_in_parts = [], [], []
    for index, rows in enumerate(grad_ffn):
        grad_inner = dot_nt(rows, down_weight)
        sig = sigmoid_of(gate_pre[index])
        act = gate_pre[index] * sig
        grad_up_block = (grad_inner * act).astype(bf16)
        grad_gate_block = (
            grad_inner * up_pre[index] * sig * (1.0 + gate_pre[index] * (1.0 - sig))
        ).astype(bf16)
        grad_up.append(grad_up_block)
        grad_gate.append(grad_gate_block)
        grad_in_parts.append(
            dot_nt(grad_gate_block, gate_weight) + dot_nt(grad_up_block, up_weight)
        )
    grad_ffn_in = scatter_blocks(grad_in_parts[0], grad_in_parts[1:])

    def joined(blocks):
        return jnp.concatenate(blocks, axis=0)

    ffn_in_all = joined(ffn_in)
    gate_up_grad = dot_tn(
        ffn_in_all, jnp.concatenate([joined(grad_gate), joined(grad_up)], axis=1)
    ).astype(bf16)
    down_grad = dot_tn(joined(grad_ffn), joined(inner)).astype(bf16)

    sums_ffn_norm = image_sums(grad_ffn_in * hidden_unit, image_own, image_count)
    grad_hidden = grad_out + unit_back(
        grad_ffn_in * per_token(norm_ffn, image_own), hidden_unit, hidden_factor
    )
    sums_attn_post = image_sums(grad_hidden * attn_unit, image_own, image_count)
    grad_attn = joined(
        gather_blocks(
            unit_back(
                grad_hidden * per_token(post_attn, image_own), attn_unit, attn_factor
            ).astype(bf16)
        )
    )
    output_grad = dot_tn(grad_attn, mixed).astype(bf16)
    grad_mixed = pad_columns(dot_nt(grad_attn, output_weight).astype(bf16), pair_columns)
    grad_q, grad_k, grad_v, grad_ck, grad_cv, stats = attention_backward(
        present,
        q_raw,
        k_raw,
        values,
        ck_raw,
        cap_values,
        gains,
        tables,
        kept,
        grad_mixed,
        image_count,
    )
    stats = stats.transpose(1, 0, 2).reshape(8, pair_columns)[:, :head_columns]
    stats = stats.reshape(8, local_heads, head_size)
    grad_head_gate = jnp.sum(stats[3], axis=1) * (1.0 - head_gate * head_gate)
    grad_qkv = jnp.concatenate(
        [part[:, :head_columns] for part in (grad_q, grad_k, grad_v)], axis=1
    )
    grad_cap = jnp.concatenate([part[:, :head_columns] for part in (grad_ck, grad_cv)], axis=1)

    def input_part(index):
        return sum(
            dot_nt(block_rows(part[:, :head_columns], index), weight)
            for part, weight in (
                (grad_q, query_weight),
                (grad_k, key_weight),
                (grad_v, value_weight),
            )
        )

    grad_normed_others = [input_part(index) for index in range(1, tensor_count)]
    grad_normed = scatter_blocks(input_part(0), grad_normed_others)
    cap_grad = dot_tn(cap_flat, grad_cap).astype(bf16)
    qkv_grad = dot_tn(joined(normed), grad_qkv).astype(bf16)

    x_unit, x_factor = unit_rows(x_float)
    sums_attn_norm = image_sums(grad_normed * x_unit, image_own, image_count)
    tokens_grad = grad_hidden + unit_back(
        grad_normed * per_token(norm_attn, image_own), x_unit, x_factor
    )

    norm_parts = jnp.stack(
        [
            jnp.sum(sums_attn_norm * scale_attn, axis=0),
            jnp.sum(sums_attn_post * gate_attn, axis=0),
            jnp.sum(sums_ffn_norm * scale_ffn, axis=0),
            jnp.sum(sums_ffn_post * gate_ffn, axis=0),
        ]
    )
    grad_mod_part = jnp.concatenate(
        [
            sums_attn_norm * attention_norm,
            sums_attn_post * attention_post * (1.0 - gate_attn * gate_attn),
            sums_ffn_norm * feedforward_norm,
            sums_ffn_post * feedforward_post * (1.0 - gate_ffn * gate_ffn),
        ],
        axis=1,
    )
    norm_sums = lax.psum(norm_parts, ("dp", "tensor"))
    grad_mod = lax.psum_scatter(grad_mod_part, "tensor", scatter_dimension=1, tiled=True)
    mod_all = lax.all_gather(grad_mod, "dp", axis=0, tiled=True)
    time_all = lax.all_gather(silu_time, "dp", axis=0, tiled=True)
    bias_own = jnp.sum(mod_all, axis=0)
    dp_count = lax.axis_size("dp")
    ada_rows = silu_time.shape[1] // dp_count
    time_own = lax.dynamic_slice_in_dim(time_all, lax.axis_index("dp") * ada_rows, ada_rows, axis=1)
    ada_grad = dot_tn(time_own, mod_all.astype(bf16))
    head_parts = jnp.concatenate([stats[:3].reshape(-1), grad_head_gate])
    head_sums = lax.psum(head_parts, "dp")
    gain_sums = head_sums[: 3 * head_columns].reshape(3, local_heads, head_size)
    gate_own = head_sums[3 * head_columns :]

    def over_dp(gradient):
        return lax.psum_scatter(gradient, "dp", scatter_dimension=0, tiled=True).astype(f32)

    gate_up_sum = over_dp(gate_up_grad)
    down_sum = over_dp(down_grad).T
    output_sum = over_dp(output_grad).T
    cap_sum = over_dp(cap_grad)
    qkv_sum = over_dp(qkv_grad)
    hidden_columns = gate_weight.shape[1]
    return (
        layer_out,
        tokens_grad,
        ada_grad,
        bias_own,
        norm_sums[0],
        norm_sums[1],
        norm_sums[2],
        norm_sums[3],
        qkv_sum[:, :head_columns],
        qkv_sum[:, head_columns : 2 * head_columns],
        qkv_sum[:, 2 * head_columns :],
        gain_sums[0],
        gain_sums[1],
        cap_sum[:, :head_columns],
        cap_sum[:, head_columns:],
        gain_sums[2],
        gate_own,
        output_sum,
        gate_up_sum[:, :hidden_columns],
        gate_up_sum[:, hidden_columns:],
        down_sum,
    )


def solution(mesh):
    placed = (
        P(("dp", "tensor"), None),
        P("dp", None),
        P("dp", None, None),
        P("dp", None),
        P("dp"),
        P(None, "dp"),
        P(None, "tensor"),
        P("tensor"),
        P(),
        P(),
        P(),
        P(),
        P(None, "tensor"),
        P(None, "tensor"),
        P(None, "tensor"),
        P("tensor", None),
        P("tensor", None),
        P(None, "tensor"),
        P(None, "tensor"),
        P("tensor", None),
        P("tensor"),
        P("tensor", None),
        P(None, "tensor"),
        P(None, "tensor"),
        P("tensor", None),
        P(("dp", "tensor"), None),
    )
    return jax.shard_map(
        on_device,
        mesh=mesh,
        in_specs=placed,
        out_specs=(
            P(("dp", "tensor"), None),
            P(("dp", "tensor"), None),
            P("dp", "tensor"),
            P("tensor"),
            P(),
            P(),
            P(),
            P(),
            P("dp", "tensor"),
            P("dp", "tensor"),
            P("dp", "tensor"),
            P("tensor", None),
            P("tensor", None),
            P("dp", "tensor"),
            P("dp", "tensor"),
            P("tensor", None),
            P("tensor"),
            P("tensor", "dp"),
            P("dp", "tensor"),
            P("dp", "tensor"),
            P("tensor", "dp"),
        ),
        check_vma=False,
    )
```

time: 1980 us -> 1150 us (0.58)
  waiting for transfers between devices: 1100 us -> 487 us
  matrix products: 561 us -> 214 us
  other arithmetic: 233 us -> 37.1 us
  blocking collectives: 5.65 us -> 167 us
  Pallas kernels: 0 us -> 145 us
  starting transfers between devices: 2.26 us -> 25.8 us
    reduce_scatter x12 -> x4, waiting for transfers between devices: 666 us -> 224 us  [over_dp(): lax.psum_scatter(gradient, 'dp', scatter_dimension=0, tiled=True)]
    dot_general x55 -> x40, matrix products: 561 us -> 214 us  [the longest x21 75.3 us: dot_nn(): lax.dot_general(left, right, (((1,), (0,)), ((), ())), preferred_element_...]
    ppermute x0 -> x8, waiting for transfers between devices: none -> 211 us  [the longest x4 108 us: gather_blocks(): lax.ppermute(block, 'tensor', [((i + step) % count, i) for i in range(cou...]
    all_gather x4 -> x0, waiting for transfers between devices: 178 us -> none  [the longest x1 49.5 us: on_device(): ffn_in_all = lax.all_gather(ffn_in_rows, 'tensor', axis=0, tiled=True)]
    pallas_call x0 -> x2, Pallas kernels: none -> 145 us  [the longest x1 87.5 us: attention_backward(): pl.pallas_call(lambda *refs: backward_kernel(count, images, *refs), grid_...]
    psum x1 -> x0, waiting for transfers between devices: 119 us -> none  [on_device(): lax.psum((norm_parts, head_parts, gate_parts, bias_parts), ('dp', 'tensor'))]
    convert_element_type x17 -> x7, other arithmetic: 109 us -> 11.2 us  [the longest x1 3.2 us: on_device(): rows = (unit * per_token(norm_attn, images)).astype(bf16)]
    psum x0 -> x2, blocking collectives: none -> 96.6 us  [the longest x1 58.6 us: on_device(): head_sums = lax.psum(head_parts, 'dp')]
  transfers between devices with their start and end apart: 20 -> 14, of which waited for: 18 -> 10; matrix products, arithmetic and copies ran while one was open for 10% -> 15% of each run, Pallas kernels for 0% -> 0%
where the time goes in v1:
time: 1150 us; the launch traced here: 1140 us
  waiting for transfers between devices  487 us (42%)
  matrix products  214 us (19%)
  blocking collectives  167 us (15%)
  Pallas kernels  145 us (13%)
  local copies, waits for them, and re-layouts  45 us (4%)
  other arithmetic  37.1 us (3%)
  starting transfers between devices  25.8 us (2%)
  between operations  16.7 us (1%)
    reduce_scatter x4, waiting for transfers between devices, over_dp(): lax.psum_scatter(gradient, 'dp', scatter_dimension=0, tiled=True)  224 us
    ppermute x4, waiting for transfers between devices, gather_blocks(): lax.ppermute(block, 'tensor', [((i + step) % count, i) for i in range(cou...  108 us
    ppermute x4, waiting for transfers between devices, scatter_blocks(): lax.ppermute(others[step - 1].astype(bf16), 'tensor', [(i, (i + step) % c...  103 us
    pallas_call x1, Pallas kernels, attention_backward(): pl.pallas_call(lambda *refs: backward_kernel(count, images, *refs), grid_...  87.5 us
    dot_general x21, matrix products, dot_nn(): lax.dot_general(left, right, (((1,), (0,)), ((), ())), preferred_element_...  75.3 us
    dot_general x13, matrix products, dot_nt(): lax.dot_general(left, right, (((1,), (1,)), ((), ())), preferred_element_...  70 us
    dot_general x6, matrix products, dot_tn(): lax.dot_general(left, right, (((0,), (0,)), ((), ())), preferred_element_...  69 us
    psum x1, blocking collectives, on_device(): head_sums = lax.psum(head_parts, 'dp')  58.6 us
  transfers between devices with their start and end apart: 14, of which 10 were waited for; matrix products, arithmetic and copies ran while one was open for 15% of the time, Pallas kernels for 0%

profile of v1, /device:TPU:0, one launch (start us, length us, event | category | flops | bytes accessed | tf_op | source)
XLA Modules:
  0.0 1137.6 jit_solution(12236311115267578391)
XLA Ops:
  7.3 3.0 collective-permute-start
  21.2 3.9 convolution_add_fusion
  25.0 25.1 %all_gather.9 = f32[3,6144]{1,0:T(4,128)S(1)} all-gather(f32[3,3072]{1,0:T(4,128)S(1)} %convolution_add_fusion), channel_id=1, replica_groups=mesh['dp'=16,'tensor'=2] {'tensor'}, dimensions={1}, use_global_device_ids=true | all-gather | bytes 110592 | tf_op jit(solution)/shard_map/all_gather | solution.py:579
  53.4 4.0 sine_multiply_fusion
  58.3 3.7 convolution_convert_fusion.8.refs_8_
  62.0 4.0 fusion.124.refs_7_
  68.0 3.2 fusion.24
  87.3 58.0 %attention_forward.1 = (bf16[1152,768]{1,0:T(8,128)(2,1)}, bf16[1152,768]{1,0:T(8,128)(2,1)}, bf16[1152,768]{1,0:T(8,128)(2,1)}, bf16[1152,1536]{1,0:T(8,128)(2,...) custom-call(s32[15]{0:T(128)} %reshape.321.refs_0_, f32[576,768]{1,0:T(8,128)} %fusion.120.refs_1_, ...), custom_call_target="tpu_custom_call" | custom-call | tf_op jit(solution)/shard_map/attention_forward/pallas_call | solution.py:363
  145.3 3.6 convolution_convert_fusion.7
  148.9 8.1 collective-permute-start.1
  157.1 37.9 %collective-permute-done.1 = bf16[576,1536]{1,0:T(8,128)(2,1)S(1)} collective-permute-done((bf16[576,1536]{1,0:T(8,128)(2,1)S(1)}, bf16[576,1536]{1,0:T(8,128)(2,1)S(1)}, u32[]{:S(2)}, u32[]{:S(2)}) %collective-permute-start.1) | collective-permute-done | bytes 1769504 | tf_op jit(solution)/shard_map/ppermute | solution.py:450
  200.5 37.3 %collective-permute-done.2 = bf16[576,1536]{1,0:T(8,128)(2,1)S(1)} collective-permute-done((bf16[576,1536]{1,0:T(8,128)(2,1)S(1)}, bf16[576,1536]{1,0:T(8,128)(2,1)S(1)}, u32[]{:S(2)}, u32[]{:S(2)}) %collective-permute-start.2) | collective-permute-done | bytes 1769504 | tf_op jit(solution)/shard_map/ppermute | solution.py:442
  237.8 3.8 fusion.126
  241.7 11.2 multiply_convert_fusion.4
  252.9 5.5 convolution_convert_fusion.6
  260.0 3.8 fusion.125
  263.8 10.7 multiply_convert_fusion.5
  274.6 22.1 %collective-permute-done.3 = bf16[576,1536]{1,0:T(8,128)(2,1)S(1)} collective-permute-done((bf16[576,1536]{1,0:T(8,128)(2,1)S(1)}, bf16[576,1536]{1,0:T(8,128)(2,1)S(1)}, u32[]{:S(2)}, u32[]{:S(2)}) %collective-permute-start.3) | collective-permute-done | bytes 1769504 | tf_op jit(solution)/shard_map/ppermute | solution.py:450
  296.7 4.0 multiply_reduce_fusion.3
  302.5 3.1 multiply_convert_fusion.9
  306.7 36.1 %collective-permute-done.4 = bf16[576,1536]{1,0:T(8,128)(2,1)S(1)} collective-permute-done((bf16[576,1536]{1,0:T(8,128)(2,1)S(1)}, bf16[576,1536]{1,0:T(8,128)(2,1)S(1)}, u32[]{:S(2)}, u32[]{:S(2)}) %collective-permute-start.4) | collective-permute-done | bytes 1769504 | tf_op jit(solution)/shard_map/ppermute | solution.py:442
  342.8 11.4 multiply_convert_fusion
  354.2 6.9 fusion.128
  361.1 7.8 add_convert_fusion.1
  369.8 10.7 multiply_convert_fusion.2
  380.5 6.7 fusion.127
  387.2 18.2 %collective-permute-done.5 = bf16[576,1536]{1,0:T(8,128)(2,1)S(1)} collective-permute-done((bf16[576,1536]{1,0:T(8,128)(2,1)}, bf16[576,1536]{1,0:T(8,128)(2,1)S(1)}, u32[]{:S(2)}, u32[]{:S(2)}) %collective-permute-start.5) | collective-permute-done | bytes 1769504 | tf_op jit(solution)/shard_map/ppermute | solution.py:450
  406.6 8.8 multiply_reduce_fusion.1
  420.2 34.7 %collective-permute-done.6 = bf16[576,1536]{1,0:T(8,128)(2,1)S(1)} collective-permute-done((bf16[576,1536]{1,0:T(8,128)(2,1)S(1)}, bf16[576,1536]{1,0:T(8,128)(2,1)S(1)}, u32[]{:S(2)}, u32[]{:S(2)}) %collective-permute-start.6) | collective-permute-done | bytes 1769504 | tf_op jit(solution)/shard_map/ppermute | solution.py:442
  454.9 5.3 convolution_convert_fusion.5.refs_17_
  460.2 87.5 %attention_backward.1 = (bf16[1152,768]{1,0:T(8,128)(2,1)}, bf16[1152,768]{1,0:T(8,128)(2,1)}, bf16[1152,768]{1,0:T(8,128)(2,1)}, bf16[768,768]{1,0:T(8,128)(2,1...) custom-call(s32[15]{0:T(128)} %reshape.321.refs_0_, f32[576,768]{1,0:T(8,128)} %fusion.120.refs_1_, ...), custom_call_target="tpu_custom_call" | custom-call | tf_op jit(solution)/shard_map/attention_backward/pallas_call | solution.py:412
  547.7 3.6 fusion.61
  555.1 7.8 collective-permute-start.7
  571.4 24.4 %collective-permute-done.7 = bf16[576,1536]{1,0:T(8,128)(2,1)S(1)} collective-permute-done((bf16[576,1536]{1,0:T(8,128)(2,1)S(1)}, bf16[576,1536]{1,0:T(8,128)(2,1)S(1)}, u32[]{:S(2)}, u32[]{:S(2)}) %collective-permute-start.7) | collective-permute-done | bytes 1769504 | tf_op jit(solution)/shard_map/ppermute | solution.py:450
  606.7 7.3 convolution_convert_fusion.4
  614.1 13.2 %convolution_convert_fusion.3 = bf16[1536,2048]{1,0:T(8,128)(2,1)} fusion(bf16[576,2048]{1,0:T(8,128)(2,1)} %get-tuple-element.195, bf16[576,2048]{1,0:T(8,128)(2,1)} %copy-done.66, bf16[576,1536]{1,0:T(8,128)(2,1)} %copy-done.58, bf16[576,1536]{1,0:T(8,128)(2,1)} %copy-done.26), kind=kOutput, calls=%fused_computation.10 | convolution fusion | flops 7267418112 | bytes 14548992 | tf_op jit(solution)/shard_map/dot_general | solution.py:43
  627.3 8.7 fusion.7
  636.0 8.7 copy.60
  645.0 14.5 %convolution_convert_fusion.1 = bf16[1536,2304]{1,0:T(8,128)(2,1)} fusion(bf16[1152,768]{1,0:T(8,128)(2,1)} %get-tuple-element.41, bf16[1152,768]{1,0:T(8,128)(2,1)} %get-tuple-element.40, bf16[1152,768]{1,0:T(8,128)(2,1)} %get-tuple-element.39, bf16[576,1536]{1,0:T(8,128)(2,1)} %copy-done.21, bf16[576,1536]{1,0:T(8,128)(2,1)} %copy-done.22), kind=kOutput, calls=%fused_computation.1 | convolution fusion | flops 8180269056 | bytes 15925248 | tf_op jit(solution)/shard_map/dot_general | solution.py:43
  659.6 23.1 %convolution_convert_fusion = bf16[1536,4096]{1,0:T(8,128)(2,1)} fusion(bf16[576,2048]{1,0:T(8,128)(2,1)} %get-tuple-element.157, bf16[576,2048]{1,0:T(8,128)(2,1)} %get-tuple-element.155, bf16[576,2048]{1,0:T(8,128)(2,1)} %get-tuple-element.158, bf16[576,2048]{1,0:T(8,128)(2,1)} %get-tuple-element.156, bf16[576,1536]{1,0:T(8,128)(2,1)} %copy-done.56, ...), kind=kOutput, calls=%fused_computation | convolution fusion | flops 14546632704 | bytes 25559040 | tf_op jit(solution)/shard_map/dot_general | solution.py:43
  683.4 21.9 %all-gather = bf16[16,3,1024]{2,1,0:T(4,128)(2,1)S(1)} all-gather(bf16[1,3,1024]{2,1,0:T(4,128)(2,1)S(1)} %fusion.112), channel_id=1, replica_groups=mesh['dp'=16,'tensor'=2] {'dp'}, dimensions={0}, use_global_device_ids=true | all-gather | bytes 104448 | tf_op jit(solution)/shard_map/all_gather | solution.py:740
  706.3 58.6 %psum.15 = f32[2316]{0:T(1024)S(1)} all-reduce(f32[2316]{0:T(1024)S(1)} %pad_maximum_fusion.5), channel_id=1, replica_groups=mesh['dp'=16,'tensor'=2] {'dp'}, use_global_device_ids=true, to_apply=%region_19.20 | all-reduce | flops 2316 | bytes 18528 | tf_op jit(solution)/shard_map/psum | solution.py:747
  767.5 38.0 %psum.14 = f32[4,1536]{1,0:T(4,128)S(1)} all-reduce(f32[4,1536]{1,0:T(4,128)S(1)} %pad_maximum_fusion.4), channel_id=1, replica_groups=mesh['dp'=16,'tensor'=2] {'dp','tensor'}, use_global_device_ids=true, to_apply=%region_16.17 | all-reduce | flops 6144 | bytes 49152 | tf_op jit(solution)/shard_map/psum | solution.py:737
  806.2 5.5 fusion.29
  813.6 23.0 %all-gather.1 = f32[16,3,3072]{2,1,0:T(4,128)S(1)} all-gather(f32[1,3,3072]{2,1,0:T(4,128)S(1)} %bitcast.78), channel_id=1, replica_groups=mesh['dp'=16,'tensor'=2] {'dp'}, dimensions={0}, use_global_device_ids=true | all-gather | bytes 626688 | tf_op jit(solution)/shard_map/all_gather | solution.py:739
  844.1 52.1 %reduce-scatter.21.cloned.1.call-done = bf16[128,1536]{1,0:T(8,128)(2,1)} async-done(((bf16[2048,1536]{1,0:T(8,128)(2,1)}), bf16[128,1536]{1,0:T(8,128)(2,1)}) %reduce-scatter.21.cloned.1.call-update) | async-done | bytes 393232
  902.2 87.1 %reduce-scatter.11.cloned.1.call-done = bf16[96,2304]{1,0:T(8,128)(2,1)} async-done(((bf16[1536,2304]{1,0:T(8,128)(2,1)}), bf16[96,2304]{1,0:T(8,128)(2,1)}) %reduce-scatter.11.cloned.1.call-update) | async-done | bytes 442384 | tf_op jit(solution)/shard_map/reduce_scatter | solution.py:752
  991.3 136.7 %reduce-scatter.15.cloned.1.call-done = bf16[96,4096]{1,0:T(8,128)(2,1)} async-done(((bf16[1536,4096]{1,0:T(8,128)(2,1)}), bf16[96,4096]{1,0:T(8,128)(2,1)}) %reduce-scatter.15.cloned.1.call-update) | async-done | bytes 786448 | tf_op jit(solution)/shard_map/reduce_scatter | solution.py:752
  (268 shorter events, 96.7 us)
Async XLA Ops:
  7.2 51.1 %copy-start = (bf16[3,256,2048]{2,1,0:T(8,128)(2,1)S(1)}, bf16[3,256,2048]{2,1,0:T(8,128)(2,1)}, u32[]{:S(2)}) copy-start(bf16[3,256,2048]{2,1,0:T(8,128)(2,1)} %param.28) | copy-start | bytes 9437188
  7.2 804.5 %reduce-scatter.19.cloned.1.call-start = ((), (), s32[]{:S(2)}) async-start(), calls=%async_computation.10 | async-start | bytes 4718592
  7.3 58.7 %collective-permute-start = (bf16[576,1536]{1,0:T(8,128)(2,1)}, bf16[576,1536]{1,0:T(8,128)(2,1)}, u32[]{:S(2)}, u32[]{:S(2)}) collective-permute-start(bf16[576,1536]{1,0:T(8,128)(2,1)} %param.26), channel_id=1, source_target_pairs={{1,0},{0,1},{3,2},{2,3},{5,4},{4,5},{7,6},{6,7},{9,8},{8,9},{11,10... | collective-permute-start | bytes 5308424 | tf_op jit(solution)/shard_map/ppermute | solution.py:442
  12.2 38.5 %copy-start.39 = (f32[1536]{0:T(1024)S(1)}, f32[1536]{0:T(1024)}, u32[]{:S(2)}) copy-start(f32[1536]{0:T(1024)} %param.36) | copy-start | bytes 18436
  12.2 38.5 %copy-start.41 = (f32[1536]{0:T(1024)S(1)}, f32[1536]{0:T(1024)}, u32[]{:S(2)}) copy-start(f32[1536]{0:T(1024)} %param.37) | copy-start | bytes 18436
  12.3 38.5 %copy-start.43 = (f32[1536]{0:T(1024)S(1)}, f32[1536]{0:T(1024)}, u32[]{:S(2)}) copy-start(f32[1536]{0:T(1024)} %param.35) | copy-start | bytes 18436
  12.3 38.5 %copy-start.45 = (f32[1536]{0:T(1024)S(1)}, f32[1536]{0:T(1024)}, u32[]{:S(2)}) copy-start(f32[1536]{0:T(1024)} %param.34) | copy-start | bytes 18436
  15.6 41.8 %copy-start.28 = (s32[1152]{0:T(1024)}, s32[1152]{0:T(1024)S(1)}, u32[]{:S(2)}) copy-start(s32[1152]{0:T(1024)S(1)} %convert_add_fusion.6) | copy-start | bytes 13828
  19.4 48.5 %copy-start.36 = (f32[576]{0:T(1024)}, f32[576]{0:T(1024)S(1)}, u32[]{:S(2)}) copy-start(f32[576]{0:T(1024)S(1)} %add_rsqrt_fusion.4) | copy-start | bytes 6916
  21.2 37.2 %copy-start.48 = (bf16[2048,768]{1,0:T(8,128)(2,1)S(1)}, bf16[2048,768]{1,0:T(8,128)(2,1)}, u32[]{:S(2)}) copy-start(bf16[2048,768]{1,0:T(8,128)(2,1)} %param.44) | copy-start | bytes 9437188
  50.9 17.0 %copy-start.30 = (f32[1536]{0:T(1024)}, f32[1536]{0:T(1024)S(1)}, u32[]{:S(2)}) copy-start(f32[1536]{0:T(1024)S(1)} %get-tuple-element.146) | copy-start | bytes 18436
  50.9 17.0 %copy-start.32 = (f32[1536]{0:T(1024)}, f32[1536]{0:T(1024)S(1)}, u32[]{:S(2)}) copy-start(f32[1536]{0:T(1024)S(1)} %get-tuple-element.147) | copy-start | bytes 18436
  50.9 17.0 %copy-start.34 = (f32[1536]{0:T(1024)}, f32[1536]{0:T(1024)S(1)}, u32[]{:S(2)}) copy-start(f32[1536]{0:T(1024)S(1)} %get-tuple-element.148) | copy-start | bytes 18436
  71.2 13.3 %copy-start.22 = (bf16[576,1536]{1,0:T(8,128)(2,1)}, bf16[576,1536]{1,0:T(8,128)(2,1)S(1)}, u32[]{:S(2)}) copy-start(bf16[576,1536]{1,0:T(8,128)(2,1)S(1)} %get-tuple-element.179) | copy-start | bytes 5308420
  145.2 49.8 %copy-start.50 = (bf16[768,1536]{1,0:T(8,128)(2,1)S(1)}, bf16[768,1536]{1,0:T(8,128)(2,1)}, u32[]{:S(2)}) copy-start(bf16[768,1536]{1,0:T(8,128)(2,1)} %param.47) | copy-start | bytes 7077892
  145.3 49.8 %copy-start.57 = (bf16[1152,768]{1,0:T(8,128)(2,1)S(1)}, bf16[1152,768]{1,0:T(8,128)(2,1)}, u32[]{:S(2)}) copy-start(bf16[1152,768]{1,0:T(8,128)(2,1)} %get-tuple-element.33) | copy-start | bytes 5308420
  148.9 46.1 %collective-permute-start.1 = (bf16[576,1536]{1,0:T(8,128)(2,1)S(1)}, bf16[576,1536]{1,0:T(8,128)(2,1)S(1)}, u32[]{:S(2)}, u32[]{:S(2)}) collective-permute-start(bf16[576,1536]{1,0:T(8,128)(2,1)S(1)} %convolution_convert_fusion.7), channel_id=1, source_target_pairs={{0,1},{1,0},{2,3},{3,2},{4,5},{5,4},{6,7},{7,6},{8,9},{9,8},{10,11... | collective-permute-start | bytes 5308424 | tf_op jit(solution)/shard_map/ppermute | solution.py:450
  157.1 39.6 %copy-start.4 = (bf16[576,1536]{1,0:T(8,128)(2,1)S(1)}, bf16[576,1536]{1,0:T(8,128)(2,1)}, u32[]{:S(2)}) copy-start(bf16[576,1536]{1,0:T(8,128)(2,1)} %param.26) | copy-start | bytes 5308420
  196.7 221.1 %copy-start.8 = (f32[576,1536]{1,0:T(8,128)}, f32[576,1536]{1,0:T(8,128)S(1)}, u32[]{:S(2)}) copy-start(f32[576,1536]{1,0:T(8,128)S(1)} %get-tuple-element.192) | copy-start | bytes 10616836
  196.7 41.1 %slice-start.2 = ((s8[6291456]{0:T(1024)(128)(4,1)}), s8[4194304]{0:T(1024)(128)(4,1)S(1)}, s32[]{:S(2)}) async-start(s8[6291456]{0:T(1024)(128)(4,1)} %bitcast.83), calls=%async_computation.14 | async-start | bytes 8388608
  196.7 41.1 %slice-start.3 = ((s8[6291456]{0:T(1024)(128)(4,1)}), s8[2097152]{0:T(1024)(128)(4,1)S(1)}, s32[]{:S(2)}) async-start(s8[6291456]{0:T(1024)(128)(4,1)} %bitcast.83), calls=%async_computation.15 | async-start | bytes 4194304
  197.9 217.5 %copy-start.1 = (f32[576,1536]{1,0:T(8,128)}, f32[576,1536]{1,0:T(8,128)S(1)}, u32[]{:S(2)}) copy-start(f32[576,1536]{1,0:T(8,128)S(1)} %get-tuple-element.154) | copy-start | bytes 10616836
  198.6 65.2 %copy-start.23 = (bf16[576,1536]{1,0:T(8,128)(2,1)}, bf16[576,1536]{1,0:T(8,128)(2,1)S(1)}, u32[]{:S(2)}) copy-start(bf16[576,1536]{1,0:T(8,128)(2,1)S(1)} %multiply_convert_fusion.10) | copy-start | bytes 5308420
  198.6 39.2 %collective-permute-start.2 = (bf16[576,1536]{1,0:T(8,128)(2,1)S(1)}, bf16[576,1536]{1,0:T(8,128)(2,1)S(1)}, u32[]{:S(2)}, u32[]{:S(2)}) collective-permute-start(bf16[576,1536]{1,0:T(8,128)(2,1)S(1)} %multiply_convert_fusion.10), channel_id=1, source_target_pairs={{1,0},{0,1},{3,2},{2,3},{5,4},{4,5},{7,6},{6,7},{9,8},{8,9},{11,10... | collective-permute-start | bytes 5308424 | tf_op jit(solution)/shard_map/ppermute | solution.py:442
  237.8 15.1 %slice-start = ((s8[6291456]{0:T(1024)(128)(4,1)}), s8[4194304]{0:T(1024)(128)(4,1)S(1)}, s32[]{:S(2)}) async-start(s8[6291456]{0:T(1024)(128)(4,1)} %bitcast.81), calls=%async_computation.12 | async-start | bytes 8388608
  241.7 11.3 slice-start.1
  258.5 38.2 %collective-permute-start.3 = (bf16[576,1536]{1,0:T(8,128)(2,1)S(1)}, bf16[576,1536]{1,0:T(8,128)(2,1)S(1)}, u32[]{:S(2)}, u32[]{:S(2)}) collective-permute-start(bf16[576,1536]{1,0:T(8,128)(2,1)S(1)} %convolution_convert_fusion.6), channel_id=1, source_target_pairs={{0,1},{1,0},{2,3},{3,2},{4,5},{5,4},{6,7},{7,6},{8,9},{9,8},{10,11... | collective-permute-start | bytes 5308424 | tf_op jit(solution)/shard_map/ppermute | solution.py:450
  274.6 26.1 %copy-start.66 = (bf16[576,2048]{1,0:T(8,128)(2,1)}, bf16[576,2048]{1,0:T(8,128)(2,1)S(1)}, u32[]{:S(2)}) copy-start(bf16[576,2048]{1,0:T(8,128)(2,1)S(1)} %get-tuple-element.193) | copy-start | bytes 7077892
  305.6 64.2 %copy-start.26 = (bf16[576,1536]{1,0:T(8,128)(2,1)}, bf16[576,1536]{1,0:T(8,128)(2,1)S(1)}, u32[]{:S(2)}) copy-start(bf16[576,1536]{1,0:T(8,128)(2,1)S(1)} %get-tuple-element.159) | copy-start | bytes 5308420
  305.6 37.2 %collective-permute-start.4 = (bf16[576,1536]{1,0:T(8,128)(2,1)S(1)}, bf16[576,1536]{1,0:T(8,128)(2,1)S(1)}, u32[]{:S(2)}, u32[]{:S(2)}) collective-permute-start(bf16[576,1536]{1,0:T(8,128)(2,1)S(1)} %get-tuple-element.159), channel_id=1, source_target_pairs={{1,0},{0,1},{3,2},{2,3},{5,4},{4,5},{7,6},{6,7},{9,8},{8,9},{11,10... | collective-permute-start | bytes 5308424 | tf_op jit(solution)/shard_map/ppermute | solution.py:442
  342.8 11.4 copy-start.58
  368.9 36.5 %collective-permute-start.5 = (bf16[576,1536]{1,0:T(8,128)(2,1)}, bf16[576,1536]{1,0:T(8,128)(2,1)S(1)}, u32[]{:S(2)}, u32[]{:S(2)}) collective-permute-start(bf16[576,1536]{1,0:T(8,128)(2,1)} %add_convert_fusion.1), channel_id=1, source_target_pairs={{0,1},{1,0},{2,3},{3,2},{4,5},{5,4},{6,7},{7,6},{8,9},{9,8},{10,11... | collective-permute-start | bytes 5308424 | tf_op jit(solution)/shard_map/ppermute | solution.py:450
  417.7 37.1 %copy-start.51 = (bf16[768,1536]{1,0:T(8,128)(2,1)S(1)}, bf16[768,1536]{1,0:T(8,128)(2,1)}, u32[]{:S(2)}) copy-start(bf16[768,1536]{1,0:T(8,128)(2,1)} %param.47) | copy-start | bytes 7077892
  419.5 40.7 %copy-start.25 = (bf16[576,1536]{1,0:T(8,128)(2,1)}, bf16[576,1536]{1,0:T(8,128)(2,1)S(1)}, u32[]{:S(2)}) copy-start(bf16[576,1536]{1,0:T(8,128)(2,1)S(1)} %multiply_convert_fusion.8) | copy-start | bytes 5308420
  419.5 35.4 %collective-permute-start.6 = (bf16[576,1536]{1,0:T(8,128)(2,1)S(1)}, bf16[576,1536]{1,0:T(8,128)(2,1)S(1)}, u32[]{:S(2)}, u32[]{:S(2)}) collective-permute-start(bf16[576,1536]{1,0:T(8,128)(2,1)S(1)} %multiply_convert_fusion.8), channel_id=1, source_target_pairs={{1,0},{0,1},{3,2},{2,3},{5,4},{4,5},{7,6},{6,7},{9,8},{8,9},{11,10... | collective-permute-start | bytes 5308424 | tf_op jit(solution)/shard_map/ppermute | solution.py:442
  555.1 40.7 %collective-permute-start.7 = (bf16[576,1536]{1,0:T(8,128)(2,1)S(1)}, bf16[576,1536]{1,0:T(8,128)(2,1)S(1)}, u32[]{:S(2)}, u32[]{:S(2)}) collective-permute-start(bf16[576,1536]{1,0:T(8,128)(2,1)S(1)} %add_convert_fusion), channel_id=1, source_target_pairs={{0,1},{1,0},{2,3},{3,2},{4,5},{5,4},{6,7},{7,6},{8,9},{9,8},{10,11... | collective-permute-start | bytes 5308424 | tf_op jit(solution)/shard_map/ppermute | solution.py:450
  569.8 26.0 %copy-start.5 = (bf16[576,1536]{1,0:T(8,128)(2,1)S(1)}, bf16[576,1536]{1,0:T(8,128)(2,1)}, u32[]{:S(2)}) copy-start(bf16[576,1536]{1,0:T(8,128)(2,1)} %param.26) | copy-start | bytes 5308420
  569.8 26.0 %copy-start.31 = (f32[1536]{0:T(1024)S(1)}, f32[1536]{0:T(1024)}, u32[]{:S(2)}) copy-start(f32[1536]{0:T(1024)} %copy-done.30) | copy-start | bytes 18436
  569.8 26.0 %copy-start.33 = (f32[1536]{0:T(1024)S(1)}, f32[1536]{0:T(1024)}, u32[]{:S(2)}) copy-start(f32[1536]{0:T(1024)} %copy-done.32) | copy-start | bytes 18436
  569.8 26.0 %copy-start.35 = (f32[1536]{0:T(1024)S(1)}, f32[1536]{0:T(1024)}, u32[]{:S(2)}) copy-start(f32[1536]{0:T(1024)} %copy-done.34) | copy-start | bytes 18436
  569.8 26.0 %copy-start.37 = (f32[576]{0:T(1024)S(1)}, f32[576]{0:T(1024)}, u32[]{:S(2)}) copy-start(f32[576]{0:T(1024)} %copy-done.36) | copy-start | bytes 6916
  606.2 234.3 %reduce-scatter.13.cloned.1.call-start = ((), (), s32[]{:S(2)}) async-start(), calls=%async_computation.7 | async-start | bytes 2506752 | tf_op jit(solution)/shard_map/reduce_scatter | solution.py:752
  614.1 228.1 %reduce-scatter.17.cloned.1.call-start = ((), (), s32[]{:S(2)}) async-start(), calls=%async_computation.9 | async-start | bytes 6684672 | tf_op jit(solution)/shard_map/reduce_scatter | solution.py:752
  627.3 268.9 %reduce-scatter.21.cloned.1.call-start = ((), (), s32[]{:S(2)}) async-start(), calls=%async_computation.11 | async-start | bytes 6684672
  644.8 344.6 %reduce-scatter.11.cloned.1.call-start = ((), (), s32[]{:S(2)}) async-start(), calls=%async_computation.6 | async-start | bytes 7520256 | tf_op jit(solution)/shard_map/reduce_scatter | solution.py:752
  659.5 468.5 %reduce-scatter.15.cloned.1.call-start = ((), (), s32[]{:S(2)}) async-start(), calls=%async_computation.8 | async-start | bytes 13369344 | tf_op jit(solution)/shard_map/reduce_scatter | solution.py:752
  682.7 23.3 %copy-start.47 = (f32[6,8,128]{2,1,0:T(8,128)S(1)}, f32[6,8,128]{2,1,0:T(8,128)}, u32[]{:S(2)}) copy-start(f32[6,8,128]{2,1,0:T(8,128)} %get-tuple-element.42) | copy-start | bytes 73732
  682.7 23.6 %copy-start.63 = (f32[12]{0:T(128)S(1)}, f32[12]{0:T(128)}, u32[]{:S(2)}) copy-start(f32[12]{0:T(128)} %param.46) | copy-start | bytes 148
  (38 other events, 164.0 us)
Sparse Core Ops, SparseCore 0:
  606.4 44.1 reduce-scatter.18
  654.8 63.4 reduce-scatter.12
  722.3 85.2 reduce-scatter.16
  811.9 84.2 reduce-scatter.20
  900.1 89.2 reduce-scatter.10
  993.8 134.2 reduce-scatter.14

commit v2 on v1

--- a/solution.py
+++ b/solution.py
@@ -323,6 +323,12 @@
     stat_ref[0] = jnp.concatenate(sums + [jnp.zeros((4, lanes), f32)], axis=0)
 
 
+def cost_of(seconds):
+    return pl.CostEstimate(
+        flops=int(seconds * 1.1e15), bytes_accessed=int(seconds * 3e12), transcendentals=0
+    )
+
+
 def columns_spec(rows, width):
     return pl.BlockSpec((rows, width), lambda pair, *_: (0, pair))
 
@@ -367,12 +373,26 @@
         + [jax.ShapeDtypeStruct((rows, 2 * width), bf16)] * 2
         + [jax.ShapeDtypeStruct((caps, 2 * width), bf16)],
         compiler_params=pltpu.CompilerParams(vmem_limit_bytes=vmem_bytes),
+        cost_estimate=cost_of(60e-6),
         name="attention_forward",
     )(present, *q_raw, *k_raw, *values, ck_raw, cap_values, gains, cosine, sine, fq, fk, fc)
 
 
 def attention_backward(
-    present, q_raw, k_raw, values, ck_raw, cap_values, gains, tables, kept, grad_mixed, images
+    present,
+    first,
+    calls_pairs,
+    earlier,
+    q_raw,
+    k_raw,
+    values,
+    ck_raw,
+    cap_values,
+    gains,
+    tables,
+    kept,
+    grad_mixed,
+    images,
 ):
     cosine, sine = tables[:2]
     self_out, cross_out, qa, ka, ca = kept
@@ -382,43 +402,12 @@
     caps = ck_raw.shape[0]
     pairs = q_raw[0].shape[1] // lanes
     width = pairs * lanes
-    grid = pltpu.PrefetchScalarGridSpec(
-        num_scalar_prefetch=1,
-        grid=(pairs,),
-        in_specs=[columns_spec(local, lanes)] * (3 * count)
-        + [columns_spec(caps, lanes)] * 2
-        + [gain_spec()]
-        + [whole_spec(rows)] * 2
-        + [columns_spec(rows, lanes)] * 2
-        + [columns_spec(rows, 2 * lanes)] * 2
-        + [columns_spec(caps, 2 * lanes)]
-        + [columns_spec(rows, lanes)],
-        out_specs=[columns_spec(rows, lanes)] * 3
-        + [columns_spec(caps, lanes)] * 2
-        + [gain_spec()],
-        scratch_shapes=[
-            pltpu.VMEM((rows, 2 * lanes), bf16),
-            pltpu.VMEM((rows, 2 * lanes), bf16),
-            pltpu.VMEM((caps, 2 * lanes), bf16),
-            pltpu.VMEM((2 * lanes, rows), bf16),
-            pltpu.VMEM((2 * lanes, caps), bf16),
-            pltpu.VMEM((lanes, rows), f32),
-            pltpu.VMEM((rows, 2 * lanes), f32),
-            pltpu.VMEM((rows, 2 * lanes), f32),
-            pltpu.VMEM((caps, 2 * lanes), f32),
-            pltpu.VMEM((caps, 2 * lanes), f32),
-        ],
-    )
-    return pl.pallas_call(
-        lambda *refs: backward_kernel(count, images, *refs),
-        grid_spec=grid,
-        out_shape=[jax.ShapeDtypeStruct((rows, width), bf16)] * 3
-        + [jax.ShapeDtypeStruct((caps, width), bf16)] * 2
-        + [jax.ShapeDtypeStruct((pairs, 8, lanes), f32)],
-        compiler_params=pltpu.CompilerParams(vmem_limit_bytes=vmem_bytes),
-        name="attention_backward",
-    )(
-        present,
+
+    def columns(rows, width):
+        return pl.BlockSpec((rows, width), lambda pair, *_: (0, first + pair))
+
+    own_gains = pl.BlockSpec((1, 8, lanes), lambda pair, *_: (first + pair, 0, 0))
+    inputs = [
         *q_raw,
         *k_raw,
         *values,
@@ -433,39 +422,315 @@
         ka,
         ca,
         grad_mixed,
-    )
+    ]
+    earlier = list(earlier or [])
+    grid = pltpu.PrefetchScalarGridSpec(
+        num_scalar_prefetch=1,
+        grid=(calls_pairs,),
+        in_specs=[columns(local, lanes)] * (3 * count)
+        + [columns(caps, lanes)] * 2
+        + [own_gains]
+        + [whole_spec(rows)] * 2
+        + [columns(rows, lanes)] * 2
+        + [columns(rows, 2 * lanes)] * 2
+        + [columns(caps, 2 * lanes)]
+        + [columns(rows, lanes)]
+        + [pl.BlockSpec(memory_space=pl.ANY)] * len(earlier),
+        out_specs=[columns(rows, lanes)] * 3 + [columns(caps, lanes)] * 2 + [own_gains],
+        scratch_shapes=[
+            pltpu.VMEM((rows, 2 * lanes), bf16),
+            pltpu.VMEM((rows, 2 * lanes), bf16),
+            pltpu.VMEM((caps, 2 * lanes), bf16),
+            pltpu.VMEM((2 * lanes, rows), bf16),
+            pltpu.VMEM((2 * lanes, caps), bf16),
+            pltpu.VMEM((lanes, rows), f32),
+            pltpu.VMEM((rows, 2 * lanes), f32),
+            pltpu.VMEM((rows, 2 * lanes), f32),
+            pltpu.VMEM((caps, 2 * lanes), f32),
+            pltpu.VMEM((caps, 2 * lanes), f32),
+        ],
+    )
+
+    def kernel(present_ref, *refs):
+        inside = len(inputs)
+        backward_kernel(count, images, present_ref, *refs[:inside], *refs[inside + len(earlier) :])
+
+    return pl.pallas_call(
+        kernel,
+        grid_spec=grid,
+        out_shape=[jax.ShapeDtypeStruct((rows, width), bf16)] * 3
+        + [jax.ShapeDtypeStruct((caps, width), bf16)] * 2
+        + [jax.ShapeDtypeStruct((pairs, 8, lanes), f32)],
+        input_output_aliases={1 + len(inputs) + k: k for k in range(len(earlier))},
+        compiler_params=pltpu.CompilerParams(vmem_limit_bytes=vmem_bytes),
+        cost_estimate=cost_of(15e-6 * calls_pairs),
+        name="attention_backward",
+    )(present, *inputs, *earlier)
+
+
+def pick(table_ref, images):
+    rows = table_ref[0:1, :]
+    for image in range(1, table_ref.shape[0]):
+        rows = jnp.where(images == image, table_ref[image : image + 1, :], rows)
+    return rows
+
+
+def unit_of(values):
+    factor = lax.rsqrt(jnp.mean(values * values, axis=-1, keepdims=True) + epsilon)
+    return values * factor, factor
+
+
+def total_of(refs):
+    total = refs[0][...].astype(f32)
+    for ref in refs[1:]:
+        total = total + ref[...].astype(f32)
+    return total
+
+
+def row_stage(body, rows_in, tables, images, rows_out, sum_count, name):
+    count, width = rows_in[0][0].shape
+    image_count = tables[0].shape[0]
+    tile = next(size for size in (96, 48, 16) if count % size == 0)
+    flat = [array for group in rows_in for array in group]
+    lengths = [len(group) for group in rows_in]
+
+    def kernel(*refs):
+        refs = list(refs)
+        groups = []
+        for length in lengths:
+            groups.append(refs[:length])
+            refs = refs[length:]
+        table_refs, refs = refs[: len(tables)], refs[len(tables) :]
+        images_ref, refs = refs[0], refs[1:]
+        outs, sums = refs[: len(rows_out)], refs[len(rows_out) :]
+        images_here = images_ref[...]
+        if sum_count:
+
+            @pl.when(pl.program_id(0) == 0)
+            def _():
+                for ref in sums:
+                    ref[...] = jnp.zeros_like(ref)
+
+        def add(index, values):
+            for image in range(image_count):
+                part = jnp.where(images_here == image, values, 0.0)
+                sums[index][image : image + 1, :] += jnp.sum(part, axis=0, keepdims=True)
+
+        body(groups, table_refs, images_here, outs, add)
+
+    row_spec = pl.BlockSpec((tile, width), lambda i: (i, 0))
+    return pl.pallas_call(
+        kernel,
+        grid=(count // tile,),
+        in_specs=[row_spec] * len(flat)
+        + [pl.BlockSpec(table.shape, lambda i: (0, 0)) for table in tables]
+        + [pl.BlockSpec((tile, 1), lambda i: (i, 0))],
+        out_specs=[row_spec] * len(rows_out)
+        + [pl.BlockSpec((image_count, width), lambda i: (0, 0))] * sum_count,
+        out_shape=[jax.ShapeDtypeStruct((count, width), kind) for kind in rows_out]
+        + [jax.ShapeDtypeStruct((image_count, width), f32)] * sum_count,
+        compiler_params=pltpu.CompilerParams(vmem_limit_bytes=vmem_bytes),
+        cost_estimate=cost_of(3e-6),
+        name=name,
+    )(*flat, *tables, images[:, None])
+
+
+def normed_body(groups, tables, images, outs, add):
+    (tokens,) = groups
+    unit, _ = unit_of(total_of(tokens))
+    outs[0][...] = (unit * pick(tables[0], images)).astype(bf16)
+
+
+def hidden_body(groups, tables, images, outs, add):
+    attn_parts, tokens = groups
+    attn = total_of(attn_parts)
+    unit, _ = unit_of(attn)
+    hidden = total_of(tokens) + unit * pick(tables[0], images)
+    outs[0][...] = attn
+    outs[1][...] = hidden
+    unit, _ = unit_of(hidden)
+    outs[2][...] = (unit * pick(tables[1], images)).astype(bf16)
+
+
+def output_body(groups, tables, images, outs, add):
+    ffn_parts, hidden, cotangent = groups
+    unit, factor = unit_of(total_of(ffn_parts))
+    post = pick(tables[0], images)
+    grad_out = total_of(cotangent)
+    outs[0][...] = (total_of(hidden) + unit * post).astype(bf16)
+    add(0, grad_out * unit)
+    outs[1][...] = unit_back(grad_out * post, unit, factor).astype(bf16)
+
+
+def middle_body(groups, tables, images, outs, add):
+    grad_parts, hidden, attn, cotangent = groups
+    grad_in = total_of(grad_parts)
+    unit, factor = unit_of(total_of(hidden))
+    add(0, grad_in * unit)
+    grad_hidden = total_of(cotangent) + unit_back(
+        grad_in * pick(tables[0], images), unit, factor
+    )
+    outs[0][...] = grad_hidden
+    unit, factor = unit_of(total_of(attn))
+    add(1, grad_hidden * unit)
+    outs[1][...] = unit_back(grad_hidden * pick(tables[1], images), unit, factor).astype(bf16)
+
+
+def input_body(groups, tables, images, outs, add):
+    grad_parts, tokens, grad_hidden = groups
+    grad_in = total_of(grad_parts)
+    unit, factor = unit_of(total_of(tokens))
+    add(0, grad_in * unit)
+    outs[0][...] = total_of(grad_hidden) + unit_back(
+        grad_in * pick(tables[0], images), unit, factor
+    )
+
+
+def weight_grad(bits, shards, lefts, rights, name, tiles=(256, lanes)):
+    depth = lefts[0].shape[1]
+    rows = sum(left.shape[0] for left in lefts)
+    shard_rows = depth // shards
+    spans = [right[1:] for right in rights]
+    rights = [right[0] for right in rights]
+    widths = [width for _, width in spans]
+    tile = next(t for t in tiles if all(c % t == 0 for span in spans for c in span))
+    starts = [sum(widths[:k]) // tile for k in range(len(widths) + 1)]
+    ends = [len(lefts) + sum(len(pieces) for pieces in rights[:k]) for k in range(len(rights) + 1)]
+
+    def kernel(bits_ref, *refs):
+        left_refs = refs[: len(lefts)]
+        kept_ref, sent_ref, turned_ref, total_ref = refs[ends[-1] :]
+        step = pl.program_id(0)
+        bit = bits_ref[0]
+
+        @pl.when(step == 0)
+        def _():
+            left = jnp.concatenate([ref[...] for ref in left_refs], axis=0)
+            turned_ref[...] = left.astype(f32).T.astype(bf16)
+
+        for index in range(len(rights)):
+
+            @pl.when((step >= starts[index]) & (step < starts[index + 1]))
+            def _():
+                own = refs[ends[index] : ends[index + 1]]
+                right = jnp.concatenate([ref[...] for ref in own], axis=0)
+                total_ref[...] = dot_nn(turned_ref[...], right)
+
+        for place in range(shards // 2):
+            kept = pl.multiple_of((2 * place + bit) * shard_rows, 8)
+            sent = pl.multiple_of((2 * place + 1 - bit) * shard_rows, 8)
+            kept_ref[place] = total_ref[pl.ds(kept, shard_rows), :].astype(bf16)
+            sent_ref[place] = total_ref[pl.ds(sent, shard_rows), :].astype(bf16)
+
+    def right_spec(index, count):
+        first, last = starts[index], starts[index + 1] - starts[index] - 1
+        base = spans[index][0] // tile
+        return pl.BlockSpec((count, tile), lambda j, s: (0, base + jnp.clip(j - first, 0, last)))
+
+    out = jax.ShapeDtypeStruct((shards // 2, shard_rows, sum(widths)), bf16)
+    out_spec = pl.BlockSpec((shards // 2, shard_rows, tile), lambda j, s: (0, 0, j))
+    return pl.pallas_call(
+        kernel,
+        grid_spec=pltpu.PrefetchScalarGridSpec(
+            num_scalar_prefetch=1,
+            grid=(starts[-1],),
+            in_specs=[pl.BlockSpec(left.shape, lambda j, s: (0, 0)) for left in lefts]
+            + [
+                right_spec(index, piece.shape[0])
+                for index, pieces in enumerate(rights)
+                for piece in pieces
+            ],
+            out_specs=[out_spec, out_spec],
+            scratch_shapes=[pltpu.VMEM((depth, rows), bf16), pltpu.VMEM((depth, tile), f32)],
+        ),
+        out_shape=[out, out],
+        compiler_params=pltpu.CompilerParams(vmem_limit_bytes=vmem_bytes),
+        cost_estimate=pl.CostEstimate(
+            flops=2 * rows * depth * sum(widths), bytes_accessed=2 * depth * sum(widths), transcendentals=0
+        ),
+        name=name,
+    )(bits, *lefts, *[piece for pieces in rights for piece in pieces])
+
+
+def add_and_split(bits, level, kept, moved):
+    shards, rows, width = kept.shape
+
+    def kernel(bits_ref, kept_stay, moved_stay, kept_go, moved_go, stay_ref, go_ref):
+        stay_ref[...] = (kept_stay[...].astype(f32) + moved_stay[...].astype(f32)).astype(bf16)
+        go_ref[...] = (kept_go[...].astype(f32) + moved_go[...].astype(f32)).astype(bf16)
+
+    stay = pl.BlockSpec((1, rows, width), lambda j, s: (2 * j + s[level], 0, 0))
+    go = pl.BlockSpec((1, rows, width), lambda j, s: (2 * j + 1 - s[level], 0, 0))
+    put = pl.BlockSpec((1, rows, width), lambda j, s: (j, 0, 0))
+    out = jax.ShapeDtypeStruct((shards // 2, rows, width), bf16)
+    return pl.pallas_call(
+        kernel,
+        grid_spec=pltpu.PrefetchScalarGridSpec(
+            num_scalar_prefetch=1,
+            grid=(shards // 2,),
+            in_specs=[stay, stay, go, go],
+            out_specs=[put, put],
+        ),
+        out_shape=[out, out],
+        compiler_params=pltpu.CompilerParams(vmem_limit_bytes=vmem_bytes),
+        cost_estimate=cost_of(3e-6),
+        name="add_and_split",
+    )(bits, kept, moved, kept, moved)
+
+
+class DpSum:
+    def __init__(self, bits, halves):
+        self.bits = bits
+        self.kept, self.sent = halves
+        self.level = 0
+        self.levels = len(bits_of("dp"))
+
+    def send(self):
+        self.moved = partner(self.sent, "dp", self.level)
+
+    def add(self, *earlier):
+        moved = after(self.moved, *earlier) if earlier else self.moved
+        self.level += 1
+        if self.level < self.levels:
+            self.kept, self.sent = add_and_split(self.bits, self.level, self.kept, moved)
+            self.send()
+        else:
+            self.total = self.kept[0].astype(f32) + moved[0].astype(f32)
+            self.sent = self.total
+
+
+def tensor_moved(array, step):
+    count = lax.axis_size("tensor")
+    return lax.ppermute(array, "tensor", [((i + step) % count, i) for i in range(count)])
 
 
 def gather_blocks(block):
-    count = lax.axis_size("tensor")
-    return [block] + [
-        lax.ppermute(block, "tensor", [((i + step) % count, i) for i in range(count)])
-        for step in range(1, count)
-    ]
-
-
-def scatter_blocks(own, others):
-    count = lax.axis_size("tensor")
-    for step in range(1, count):
-        moved = lax.ppermute(
-            others[step - 1].astype(bf16),
-            "tensor",
-            [(i, (i + step) % count) for i in range(count)],
-        )
-        own = own + moved.astype(f32)
-    return own
-
-
-def per_token(table, images):
-    rows = table[0:1]
-    for image in range(1, table.shape[0]):
-        rows = jnp.where(images[:, None] == image, table[image : image + 1], rows)
-    return rows
-
-
-def image_sums(values, images, count):
-    chosen = (jnp.arange(count, dtype=jnp.int32)[:, None] == images[None, :]).astype(bf16)
-    return dot_nn(chosen, values.astype(bf16))
+    return [block] + [tensor_moved(block, step) for step in range(1, lax.axis_size("tensor"))]
+
+
+def after(value, *earlier):
+    return lax.optimization_barrier((value, earlier))[0]
+
+
+def bits_of(axis):
+    return range(lax.axis_size(axis).bit_length() - 1)
+
+
+def partner(array, axis, bit):
+    return lax.ppermute(array, axis, [(i, i ^ (1 << bit)) for i in range(lax.axis_size(axis))])
+
+
+def gather_over_dp(array):
+    array = array[None]
+    for bit in reversed(bits_of("dp")):
+        array = jnp.concatenate([array, partner(array, "dp", bit)], axis=0)
+    return array
+
+
+def sum_over(array, axis):
+    for bit in reversed(bits_of(axis)):
+        array = array + partner(array, axis, bit)
+    return array
 
 
 def rope_tables(positions):
@@ -487,6 +752,10 @@
 
 def pad_columns(values, width):
     return jnp.pad(values, ((0, 0), (0, width - values.shape[1])))
+
+
+def pad_rows(values, height):
+    return jnp.pad(values, ((0, height - values.shape[0]), (0, 0)))
 
 
 def on_device(
@@ -576,7 +845,8 @@
     time_float = timestep.astype(f32)
     silu_time = (time_float * sigmoid_of(time_float)).astype(bf16)
     mod_part = dot_nn(silu_time, ada_weight) + ada_bias
-    modulation = lax.all_gather(mod_part, "tensor", axis=1, tiled=True)
+    mod_stack = jnp.roll(jnp.stack(gather_blocks(mod_part)), tensor_place, axis=0)
+    modulation = mod_stack.transpose(1, 0, 2).reshape(image_count, 4 * model_width)
     scale_attn = 1.0 + modulation[:, :model_width]
     gate_attn = jnp.tanh(modulation[:, model_width : 2 * model_width])
     scale_ffn = 1.0 + modulation[:, 2 * model_width : 3 * model_width]
@@ -593,8 +863,7 @@
     normed, q_raw, k_raw, values = [], [], [], []
     for index, block in enumerate(token_blocks):
         images = image_all[index * local_rows : (index + 1) * local_rows]
-        unit = unit_rows(block.astype(f32))[0]
-        rows = (unit * per_token(norm_attn, images)).astype(bf16)
+        (rows,) = row_stage(normed_body, [[block]], [norm_attn], images, [bf16], 0, "normed_in")
         normed.append(rows)
         q_raw.append(pad_columns(dot_nn(rows, query_weight), pair_columns))
         k_raw.append(pad_columns(dot_nn(rows, key_weight), pair_columns))
@@ -603,182 +872,368 @@
     mixed, *kept = attention_forward(
         present, q_raw, k_raw, values, ck_raw, cap_values, gains, tables, image_count
     )
-    mixed = mixed[:, :head_columns]
-
-    def block_rows(array, index):
-        return array[index * local_rows : (index + 1) * local_rows]
-
-    attn_others = [
-        dot_nn(block_rows(mixed, index), output_weight) for index in range(1, tensor_count)
+    chunks = 2 if local_rows % 32 == 0 else 1
+    chunk_rows = local_rows // chunks
+    steps = range(1, tensor_count)
+    cuts = range(chunks)
+    bits = jnp.stack([(lax.axis_index("dp") >> bit) & 1 for bit in bits_of("dp")]).astype(jnp.int32)
+    shards = lax.axis_size("dp")
+
+    def piece_of(array, step, cut):
+        start = step * local_rows + cut * chunk_rows
+        return array[start : start + chunk_rows]
+
+    def returned(parts):
+        return [tensor_moved(part, -step) for step, part in enumerate(parts, 1)]
+
+    def moved_in(array):
+        return [tensor_moved(array, step) for step in steps]
+
+    output_rows = pad_rows(output_weight, pair_columns)
+    tokens_cut = [piece_of(tokens, 0, cut) for cut in cuts]
+    cotangent_cut = [piece_of(cotangent, 0, cut) for cut in cuts]
+    images_cut = [piece_of(image_own, 0, cut) for cut in cuts]
+
+    attn_moved = [
+        returned([dot_nn(piece_of(mixed, step, cut), output_rows).astype(bf16) for step in steps])
+        for cut in cuts
     ]
-    attn_rows = scatter_blocks(dot_nn(block_rows(mixed, 0), output_weight), attn_others)
-    attn_unit, attn_factor = unit_rows(attn_rows)
-    x_float = tokens.astype(f32)
-    hidden = x_float + attn_unit * per_token(post_attn, image_own)
-    hidden_unit, hidden_factor = unit_rows(hidden)
-    ffn_in = gather_blocks((hidden_unit * per_token(norm_ffn, image_own)).astype(bf16))
-
-    gate_pre, up_pre, inner, ffn_parts = [], [], [], []
-    for rows in ffn_in:
-        gate_block = dot_nn(rows, gate_weight)
-        up_block = dot_nn(rows, up_weight)
-        inner_block = (gate_block * sigmoid_of(gate_block) * up_block).astype(bf16)
-        gate_pre.append(gate_block)
-        up_pre.append(up_block)
-        inner.append(inner_block)
-        ffn_parts.append(dot_nn(inner_block, down_weight))
-    ffn_rows = scatter_blocks(ffn_parts[0], ffn_parts[1:])
-    ffn_unit, ffn_factor = unit_rows(ffn_rows)
-    layer_out = (hidden + ffn_unit * per_token(post_ffn, image_own)).astype(bf16)
-
-    grad_out = cotangent.astype(f32)
-    sums_ffn_post = image_sums(grad_out * ffn_unit, image_own, image_count)
-    grad_ffn = gather_blocks(
-        unit_back(grad_out * per_token(post_ffn, image_own), ffn_unit, ffn_factor).astype(bf16)
-    )
-    grad_gate, grad_up, grad_in_parts = [], [], []
-    for index, rows in enumerate(grad_ffn):
+    attn_kept = [dot_nn(piece_of(mixed, 0, cut), output_rows) for cut in cuts]
+    attn, hidden, ffn_in = [], [], []
+    for cut in cuts:
+        attn_rows, hidden_rows, rows = row_stage(
+            hidden_body,
+            [[attn_kept[cut]] + attn_moved[cut], [tokens_cut[cut]]],
+            [post_attn, norm_ffn],
+            images_cut[cut],
+            [f32, f32, bf16],
+            0,
+            "hidden",
+        )
+        attn.append(attn_rows)
+        hidden.append(hidden_rows)
+        ffn_in.append([rows] + moved_in(rows))
+
+    def feed_forward(rows):
+        gate = dot_nn(rows, gate_weight)
+        up = dot_nn(rows, up_weight)
+        inner = (gate * sigmoid_of(gate) * up).astype(bf16)
+        return gate.astype(bf16), up.astype(bf16), inner, dot_nn(inner, down_weight)
+
+    latest = ()
+    forward, ffn_moved = [], []
+    for cut in cuts:
+        pieces = []
+        for step in range(tensor_count):
+            ffn_in[cut][step] = after(ffn_in[cut][step], *latest)
+            gate, up, inner, part = feed_forward(ffn_in[cut][step])
+            part = part if step == 0 else part.astype(bf16)
+            pieces.append((gate, up, inner, part))
+            latest = (part,)
+        forward.append(pieces)
+        ffn_moved.append(returned([piece[3] for piece in pieces[1:]]))
+
+    layer_out, sums_ffn_post, grad_ffn = [], [], []
+    for cut in cuts:
+        out_rows, rows, sums = row_stage(
+            output_body,
+            [[forward[cut][0][3]] + ffn_moved[cut], [hidden[cut]], [cotangent_cut[cut]]],
+            [post_ffn],
+            images_cut[cut],
+            [bf16, bf16],
+            1,
+            "layer_out",
+        )
+        layer_out.append(out_rows)
+        sums_ffn_post.append(sums)
+        grad_ffn.append([rows] + moved_in(rows))
+
+    def feed_back(rows, kept):
+        gate, up = kept[0].astype(f32), kept[1].astype(f32)
         grad_inner = dot_nt(rows, down_weight)
-        sig = sigmoid_of(gate_pre[index])
-        act = gate_pre[index] * sig
-        grad_up_block = (grad_inner * act).astype(bf16)
-        grad_gate_block = (
-            grad_inner * up_pre[index] * sig * (1.0 + gate_pre[index] * (1.0 - sig))
-        ).astype(bf16)
-        grad_up.append(grad_up_block)
-        grad_gate.append(grad_gate_block)
-        grad_in_parts.append(
-            dot_nt(grad_gate_block, gate_weight) + dot_nt(grad_up_block, up_weight)
+        sig = sigmoid_of(gate)
+        grad_up = (grad_inner * (gate * sig)).astype(bf16)
+        grad_gate = (grad_inner * up * sig * (1.0 + gate * (1.0 - sig))).astype(bf16)
+        return grad_gate, grad_up, dot_nt(grad_gate, gate_weight) + dot_nt(grad_up, up_weight)
+
+    latest = ()
+    backward, grad_in_moved = [], []
+    for cut in cuts:
+        pieces = []
+        for step in range(tensor_count):
+            grad_ffn[cut][step] = after(grad_ffn[cut][step], *latest)
+            grad_gate, grad_up, part = feed_back(grad_ffn[cut][step], forward[cut][step])
+            part = part if step == 0 else part.astype(bf16)
+            pieces.append((grad_gate, grad_up, part))
+            latest = (part,)
+        backward.append(pieces)
+        grad_in_moved.append(returned([piece[2] for piece in pieces[1:]]))
+
+    def whole_right(pieces):
+        return pieces, 0, pieces[0].shape[1]
+
+    def group_pieces(of):
+        return [of(cut, step) for step in range(tensor_count) for cut in cuts]
+
+    grad_hidden, sums_ffn_norm, sums_attn_post, grad_attn = [], [], [], []
+    for cut in cuts:
+        if cut == chunks - 1:
+            lefts = group_pieces(lambda cut, step: grad_ffn[cut][step])
+            lefts[0] = after(lefts[0], latest)
+            down_sum = DpSum(
+                bits,
+                weight_grad(
+                    bits,
+                    shards,
+                    lefts,
+                    [whole_right(group_pieces(lambda cut, step: forward[cut][step][2]))],
+                    "down_grad",
+                ),
+            )
+            down_sum.send()
+            grad_in_moved[cut] = [after(moved, down_sum.sent) for moved in grad_in_moved[cut]]
+        hidden_grad, rows, norm_sums, post_sums = row_stage(
+            middle_body,
+            [
+                [backward[cut][0][2]] + grad_in_moved[cut],
+                [hidden[cut]],
+                [attn[cut]],
+                [cotangent_cut[cut]],
+            ],
+            [norm_ffn, post_attn],
+            images_cut[cut],
+            [f32, bf16],
+            2,
+            "hidden_grad",
         )
-    grad_ffn_in = scatter_blocks(grad_in_parts[0], grad_in_parts[1:])
-
-    def joined(blocks):
-        return jnp.concatenate(blocks, axis=0)
-
-    ffn_in_all = joined(ffn_in)
-    gate_up_grad = dot_tn(
-        ffn_in_all, jnp.concatenate([joined(grad_gate), joined(grad_up)], axis=1)
-    ).astype(bf16)
-    down_grad = dot_tn(joined(grad_ffn), joined(inner)).astype(bf16)
-
-    sums_ffn_norm = image_sums(grad_ffn_in * hidden_unit, image_own, image_count)
-    grad_hidden = grad_out + unit_back(
-        grad_ffn_in * per_token(norm_ffn, image_own), hidden_unit, hidden_factor
-    )
-    sums_attn_post = image_sums(grad_hidden * attn_unit, image_own, image_count)
-    grad_attn = joined(
-        gather_blocks(
-            unit_back(
-                grad_hidden * per_token(post_attn, image_own), attn_unit, attn_factor
-            ).astype(bf16)
+        grad_hidden.append(hidden_grad)
+        sums_ffn_norm.append(norm_sums)
+        sums_attn_post.append(post_sums)
+        grad_attn.append([rows] + moved_in(rows))
+        latest = rows
+    lefts = group_pieces(lambda cut, step: ffn_in[cut][step])
+    lefts[0] = after(lefts[0], latest)
+    gate_up_sum = DpSum(
+        bits,
+        weight_grad(
+            bits,
+            shards,
+            lefts,
+            [
+                whole_right(group_pieces(lambda cut, step: backward[cut][step][k]))
+                for k in (0, 1)
+            ],
+            "gate_up_grad",
+        ),
+    )
+    gate_up_sum.send()
+    down_sum.add(gate_up_sum.sent)
+
+    grad_attn = group_pieces(lambda cut, step: grad_attn[cut][step])
+    grad_attn[-1] = after(grad_attn[-1], down_sum.sent)
+    grad_mixed = jnp.concatenate(
+        [dot_nt(piece, output_rows).astype(bf16) for piece in grad_attn], axis=0
+    )
+    output_sum = DpSum(
+        bits,
+        weight_grad(
+            bits,
+            shards,
+            grad_attn,
+            [whole_right([mixed])],
+            "output_grad",
+        ),
+    )
+    output_sum.send()
+    gate_up_sum.add(output_sum.sent)
+    grad_mixed = after(grad_mixed, gate_up_sum.sent)
+
+    def projection_sum(parts, start, width):
+        rights = [([part], start, width) for part in parts[:3]]
+        return DpSum(bits, weight_grad(bits, shards, normed, rights, "projection_grad"))
+
+    def caption_sum(parts, start, width):
+        rights = [([part], start, width) for part in parts[3:5]]
+        return DpSum(bits, weight_grad(bits, shards, [cap_flat], rights, "caption_grad"))
+
+    parts = None
+    first = 0
+    call_sizes = [2] * (pairs // 2) if pairs % 2 == 0 and pairs > 2 else [1] * pairs
+    for call, size in enumerate(call_sizes):
+        parts = attention_backward(
+            present,
+            first,
+            size,
+            parts,
+            q_raw,
+            k_raw,
+            values,
+            ck_raw,
+            cap_values,
+            gains,
+            tables,
+            kept,
+            grad_mixed,
+            image_count,
         )
-    )
-    output_grad = dot_tn(grad_attn, mixed).astype(bf16)
-    grad_mixed = pad_columns(dot_nt(grad_attn, output_weight).astype(bf16), pair_columns)
-    grad_q, grad_k, grad_v, grad_ck, grad_cv, stats = attention_backward(
-        present,
-        q_raw,
-        k_raw,
-        values,
-        ck_raw,
-        cap_values,
-        gains,
-        tables,
-        kept,
-        grad_mixed,
-        image_count,
-    )
+        first += size
+        if call == 0:
+            down_sum.add(parts[0])
+            output_sum.add(parts[0])
+            grad_mixed = after(grad_mixed, down_sum.sent, output_sum.sent)
+        if call == len(call_sizes) - 2:
+            early = first * lanes
+            query_early = projection_sum(parts, 0, early)
+            query_early.send()
+            caption_early = caption_sum(parts, 0, early)
+            caption_early.send()
+            gate_up_sum.add(parts[0])
+            down_sum.add(gate_up_sum.sent)
+            query_early.add(down_sum.sent, caption_early.sent)
+            output_sum.add(query_early.sent)
+            caption_early.add(output_sum.sent)
+            parts = [parts[0]] + list(after(tuple(parts[1:]), caption_early.sent))
+            grad_mixed = after(grad_mixed, caption_early.sent)
+    grad_q, grad_k, grad_v, grad_ck, grad_cv, stats = parts
     stats = stats.transpose(1, 0, 2).reshape(8, pair_columns)[:, :head_columns]
     stats = stats.reshape(8, local_heads, head_size)
     grad_head_gate = jnp.sum(stats[3], axis=1) * (1.0 - head_gate * head_gate)
-    grad_qkv = jnp.concatenate(
-        [part[:, :head_columns] for part in (grad_q, grad_k, grad_v)], axis=1
-    )
-    grad_cap = jnp.concatenate([part[:, :head_columns] for part in (grad_ck, grad_cv)], axis=1)
-
-    def input_part(index):
+
+    weights_in = [
+        pad_columns(weight, pair_columns) for weight in (query_weight, key_weight, value_weight)
+    ]
+
+    def input_part(step, cut):
         return sum(
-            dot_nt(block_rows(part[:, :head_columns], index), weight)
-            for part, weight in (
-                (grad_q, query_weight),
-                (grad_k, key_weight),
-                (grad_v, value_weight),
-            )
+            dot_nt(piece_of(part, step, cut), weight)
+            for part, weight in zip((grad_q, grad_k, grad_v), weights_in)
         )
 
-    grad_normed_others = [input_part(index) for index in range(1, tensor_count)]
-    grad_normed = scatter_blocks(input_part(0), grad_normed_others)
-    cap_grad = dot_tn(cap_flat, grad_cap).astype(bf16)
-    qkv_grad = dot_tn(joined(normed), grad_qkv).astype(bf16)
-
-    x_unit, x_factor = unit_rows(x_float)
-    sums_attn_norm = image_sums(grad_normed * x_unit, image_own, image_count)
-    tokens_grad = grad_hidden + unit_back(
-        grad_normed * per_token(norm_attn, image_own), x_unit, x_factor
-    )
-
-    norm_parts = jnp.stack(
+    sent = [[input_part(step, cut).astype(bf16) for step in steps] for cut in cuts]
+    grad_normed_moved = [returned(part) for part in sent]
+    late = pair_columns - early
+    query_late = projection_sum([after(grad_q, sent), grad_k, grad_v], early, late)
+    query_late.send()
+    grad_ck = after(grad_ck, query_late.sent)
+    caption_late = caption_sum([grad_q, grad_k, grad_v, grad_ck, grad_cv], early, late)
+    caption_late.send()
+    query_late.add(caption_late.sent)
+    gate_up_sum.add(query_late.sent)
+    caption_late.add(gate_up_sum.sent)
+    output_sum.add(caption_late.sent)
+    query_early.add(output_sum.sent)
+    grad_q = after(grad_q, query_early.sent)
+    grad_normed_kept = [input_part(0, cut) for cut in cuts]
+    sums_attn_norm, tokens_grad = [], []
+    for cut in cuts:
+        rows, sums = row_stage(
+            input_body,
+            [[grad_normed_kept[cut]] + grad_normed_moved[cut], [tokens_cut[cut]], [grad_hidden[cut]]],
+            [norm_attn],
+            images_cut[cut],
+            [f32],
+            1,
+            "tokens_grad",
+        )
+        tokens_grad.append(rows)
+        sums_attn_norm.append(sums)
+    sums_all = (
+        down_sum,
+        gate_up_sum,
+        output_sum,
+        query_early,
+        caption_early,
+        query_late,
+        caption_late,
+    )
+    for level in range(query_late.levels + 1):
+        for running in sums_all:
+            if running.level < level:
+                running.add()
+
+    def both_totals(first_sum, second_sum, index):
+        return jnp.concatenate(
+            [
+                first_sum.total[:, index * early : (index + 1) * early],
+                second_sum.total[:, index * late : (index + 1) * late],
+            ],
+            axis=1,
+        )[:, :head_columns]
+
+    sums = jnp.concatenate(
+        [sum(part) for part in (sums_attn_norm, sums_attn_post, sums_ffn_norm, sums_ffn_post)],
+        axis=1,
+    )
+    sums = sum_over(sums, "tensor")
+    widths = [sums[:, k * model_width : (k + 1) * model_width] for k in range(4)]
+    norm_parts = jnp.concatenate(
         [
-            jnp.sum(sums_attn_norm * scale_attn, axis=0),
-            jnp.sum(sums_attn_post * gate_attn, axis=0),
-            jnp.sum(sums_ffn_norm * scale_ffn, axis=0),
-            jnp.sum(sums_ffn_post * gate_ffn, axis=0),
+            jnp.sum(part * factor, axis=0)
+            for part, factor in zip(widths, (scale_attn, gate_attn, scale_ffn, gate_ffn))
         ]
     )
-    grad_mod_part = jnp.concatenate(
+    grad_mod = jnp.concatenate(
         [
-            sums_attn_norm * attention_norm,
-            sums_attn_post * attention_post * (1.0 - gate_attn * gate_attn),
-            sums_ffn_norm * feedforward_norm,
-            sums_ffn_post * feedforward_post * (1.0 - gate_ffn * gate_ffn),
+            widths[0] * attention_norm,
+            widths[1] * attention_post * (1.0 - gate_attn * gate_attn),
+            widths[2] * feedforward_norm,
+            widths[3] * feedforward_post * (1.0 - gate_ffn * gate_ffn),
         ],
         axis=1,
     )
-    norm_sums = lax.psum(norm_parts, ("dp", "tensor"))
-    grad_mod = lax.psum_scatter(grad_mod_part, "tensor", scatter_dimension=1, tiled=True)
-    mod_all = lax.all_gather(grad_mod, "dp", axis=0, tiled=True)
-    time_all = lax.all_gather(silu_time, "dp", axis=0, tiled=True)
-    bias_own = jnp.sum(mod_all, axis=0)
+    mod_columns = ada_weight.shape[1]
+    grad_mod_own = lax.dynamic_slice_in_dim(
+        grad_mod, tensor_place * mod_columns, mod_columns, axis=1
+    )
     dp_count = lax.axis_size("dp")
-    ada_rows = silu_time.shape[1] // dp_count
-    time_own = lax.dynamic_slice_in_dim(time_all, lax.axis_index("dp") * ada_rows, ada_rows, axis=1)
-    ada_grad = dot_tn(time_own, mod_all.astype(bf16))
-    head_parts = jnp.concatenate([stats[:3].reshape(-1), grad_head_gate])
-    head_sums = lax.psum(head_parts, "dp")
-    gain_sums = head_sums[: 3 * head_columns].reshape(3, local_heads, head_size)
-    gate_own = head_sums[3 * head_columns :]
-
-    def over_dp(gradient):
-        return lax.psum_scatter(gradient, "dp", scatter_dimension=0, tiled=True).astype(f32)
-
-    gate_up_sum = over_dp(gate_up_grad)
-    down_sum = over_dp(down_grad).T
-    output_sum = over_dp(output_grad).T
-    cap_sum = over_dp(cap_grad)
-    qkv_sum = over_dp(qkv_grad)
+    ada_width = silu_time.shape[1]
+    ada_rows = ada_width // dp_count
+    gathered = gather_over_dp(
+        jnp.concatenate([grad_mod_own.astype(bf16), silu_time], axis=1).reshape(-1, lanes)
+    ).reshape(dp_count * image_count, mod_columns + ada_width)
+    time_own = lax.dynamic_slice_in_dim(
+        gathered, mod_columns + lax.axis_index("dp") * ada_rows, ada_rows, axis=1
+    )
+    ada_grad = dot_tn(time_own, gathered[:, :mod_columns])
+    small = jnp.concatenate(
+        [
+            norm_parts,
+            jnp.sum(grad_mod_own, axis=0),
+            stats[:3].reshape(-1),
+            jnp.pad(grad_head_gate, (0, -local_heads % lanes)),
+        ]
+    )
+    length = small.shape[0]
+    small = sum_over(jnp.pad(small, (0, -length % 1024)).reshape(-1, lanes), "dp").reshape(-1)
+    norm_sums = small[: 4 * model_width].reshape(4, model_width)
+    bias_own = small[4 * model_width : 4 * model_width + mod_columns]
+    start = 4 * model_width + mod_columns
+    gain_sums = small[start : start + 3 * head_columns].reshape(3, local_heads, head_size)
+    start = start + 3 * head_columns
+    gate_own = small[start : start + local_heads]
     hidden_columns = gate_weight.shape[1]
     return (
-        layer_out,
-        tokens_grad,
+        jnp.concatenate(layer_out, axis=0),
+        jnp.concatenate(tokens_grad, axis=0),
         ada_grad,
         bias_own,
         norm_sums[0],
         norm_sums[1],
         norm_sums[2],
         norm_sums[3],
-        qkv_sum[:, :head_columns],
-        qkv_sum[:, head_columns : 2 * head_columns],
-        qkv_sum[:, 2 * head_columns :],
+        both_totals(query_early, query_late, 0),
+        both_totals(query_early, query_late, 1),
+        both_totals(query_early, query_late, 2),
         gain_sums[0],
         gain_sums[1],
-        cap_sum[:, :head_columns],
-        cap_sum[:, head_columns:],
+        both_totals(caption_early, caption_late, 0),
+        both_totals(caption_early, caption_late, 1),
         gain_sums[2],
         gate_own,
-        output_sum,
-        gate_up_sum[:, :hidden_columns],
-        gate_up_sum[:, hidden_columns:],
-        down_sum,
+        output_sum.total.T[:head_columns],
+        gate_up_sum.total[:, :hidden_columns],
+        gate_up_sum.total[:, hidden_columns:],
+        down_sum.total.T,
     )
 
 

time: 1150 us -> 796 us (0.69)
  waiting for transfers between devices: 487 us -> 109 us
  Pallas kernels: 145 us -> 382 us
  blocking collectives: 167 us -> 0 us
  matrix products: 214 us -> 159 us
  starting transfers between devices: 25.8 us -> 75.4 us
  local copies, waits for them, and re-layouts: 45 us -> 29 us
  between operations: 16.7 us -> 3.86 us
    pallas_call x1 -> x41, Pallas kernels: 87.5 us -> 324 us  [the longest x3 97.1 us: attention_backward(): pl.pallas_call(kernel, grid_spec=grid, out_shape=[jax.ShapeDtypeStruct((r...]
    reduce_scatter x4 -> x0, waiting for transfers between devices: 224 us -> none  [over_dp(): lax.psum_scatter(gradient, 'dp', scatter_dimension=0, tiled=True)]
    ppermute x8 -> x53, waiting for transfers between devices: 211 us -> 109 us  [the longest x16 71.5 us: tensor_moved(): lax.ppermute(array, 'tensor', [((i + step) % count, i) for i in range(cou...]
    psum x2 -> x0, blocking collectives: 96.6 us -> none  [the longest x1 58.6 us: on_device(): head_sums = lax.psum(head_parts, 'dp')]
    all_gather x3 -> x0, blocking collectives: 70 us -> none  [the longest x1 25.1 us: on_device(): modulation = lax.all_gather(mod_part, 'tensor', axis=1, tiled=True)]
    dot_general x6 -> x1, matrix products: 69 us -> 1.25 us  [dot_tn(): lax.dot_general(left, right, (((0,), (0,)), ((), ())), preferred_element_...]
    unnamed x8 -> x0, waiting for transfers between devices: 52.2 us -> none
    ppermute x8 -> x53, starting transfers between devices: 25 us -> 75.4 us  [the longest x37 43.5 us: partner(): lax.ppermute(array, axis, [(i, i ^ 1 << bit) for i in range(lax.axis_size...]
  transfers between devices with their start and end apart: 14 -> 53, of which waited for: 10 -> 19; matrix products, arithmetic and copies ran while one was open for 15% -> 24% of each run, Pallas kernels for 0% -> 36%
where the time goes in v2:
time: 796 us; the launch traced here: 787 us
  Pallas kernels  382 us (48%)
  matrix products  159 us (20%)
  waiting for transfers between devices  109 us (14%)
  starting transfers between devices  75.4 us (9%)
  local copies, waits for them, and re-layouts  29 us (4%)
  other arithmetic  28.7 us (4%)
    pallas_call x3, Pallas kernels, attention_backward(): pl.pallas_call(kernel, grid_spec=grid, out_shape=[jax.ShapeDtypeStruct((r...  97.1 us
    pallas_call x7, Pallas kernels, weight_grad(): pl.pallas_call(kernel, grid_spec=pltpu.PrefetchScalarGridSpec(num_scalar_...  90.6 us
    dot_general x28, matrix products, dot_nt(): lax.dot_general(left, right, (((1,), (1,)), ((), ())), preferred_element_...  81.6 us
    pallas_call x21, Pallas kernels, add_and_split(): pl.pallas_call(kernel, grid_spec=pltpu.PrefetchScalarGridSpec(num_scalar_...  80.6 us
    dot_general x25, matrix products, dot_nn(): lax.dot_general(left, right, (((1,), (0,)), ((), ())), preferred_element_...  76.3 us
    ppermute x16, waiting for transfers between devices, tensor_moved(): lax.ppermute(array, 'tensor', [((i + step) % count, i) for i in range(cou...  71.5 us
    pallas_call x1, Pallas kernels, attention_forward(): pl.pallas_call(lambda *refs: forward_kernel(count, images, *refs), grid_s...  57.5 us
    pallas_call x10, Pallas kernels, row_stage(): pl.pallas_call(kernel, grid=(count // tile,), in_specs=[row_spec] * len(f...  56.1 us
  transfers between devices with their start and end apart: 53, of which 19 were waited for; matrix products, arithmetic and copies ran while one was open for 24% of the time, Pallas kernels for 36%

profile of v2, /device:TPU:0, one launch (start us, length us, event | category | flops | bytes accessed | tf_op | source)
XLA Modules:
  0.0 787.0 jit_solution(8284597669056840821)
XLA Ops:
  14.3 6.0 fusion.114.refs_7_.refs_6_
  38.2 5.3 normed_in.2.refs_0_
  43.5 5.2 fusion.110.refs_1_.refs_0_
  53.9 5.2 normed_in.3.refs_1_
  59.1 5.1 fusion.111.refs_2_.refs_1_
  69.4 57.5 %attention_forward.1 = (bf16[1152,768]{1,0:T(8,128)(2,1)}, bf16[1152,768]{1,0:T(8,128)(2,1)}, bf16[1152,768]{1,0:T(8,128)(2,1)}, bf16[1152,1536]{1,0:T(8,128)(2,...) custom-call(s32[15]{0:T(128)} %reshape.297.refs_0_.present_ref, f32[576,768]{1,0:T(8,128)} %fusion.110.refs_1_.refs_0_, ...), custom_call_target="tpu_custom_call" | custom-call | flops 65999998976 | bytes 180000000 | tf_op jit(solution)/shard_map/attention_forward/pallas_call | solution.py:369
  129.0 8.3 %collective-permute-start.2 = (bf16[288,1536]{1,0:T(8,128)(2,1)S(1)}, bf16[288,1536]{1,0:T(8,128)(2,1)}, u32[]{:S(2)}, u32[]{:S(2)}) collective-permute-start(bf16[288,1536]{1,0:T(8,128)(2,1)S(1)} %convolution_convert_fusion.3), channel_id=1, source_target_pairs={{1,0},{0,1},{3,2},{2,3},{5,4},{4,5},{7,6},{6,7},{9,8},{8,9},{11,10... | collective-permute-start | bytes 2654216 | tf_op jit(solution)/shard_map/ppermute | solution.py:704
  143.3 14.7 %collective-permute-done.2.refs_1_ = bf16[288,1536]{1,0:T(8,128)(2,1)} collective-permute-done((bf16[288,1536]{1,0:T(8,128)(2,1)S(1)}, bf16[288,1536]{1,0:T(8,128)(2,1)}, u32[]{:S(2)}, u32[]{:S(2)}) %collective-permute-start.2) | collective-permute-done | bytes 884768 | tf_op jit(solution)/shard_map/ppermute | solution.py:704
  158.0 5.1 hidden.2
  165.2 11.7 %collective-permute-done.5.refs_1_ = bf16[288,1536]{1,0:T(8,128)(2,1)S(1)} collective-permute-done((bf16[288,1536]{1,0:T(8,128)(2,1)}, bf16[288,1536]{1,0:T(8,128)(2,1)S(1)}, u32[]{:S(2)}, u32[]{:S(2)}) %collective-permute-start.5) | collective-permute-done | bytes 884768 | tf_op jit(solution)/shard_map/ppermute | solution.py:704
  177.8 5.5 hidden.3
  185.5 4.9 fusion.115
  225.0 8.7 %collective-permute-done.4.refs_1_ = bf16[288,1536]{1,0:T(8,128)(2,1)S(1)} collective-permute-done((bf16[288,1536]{1,0:T(8,128)(2,1)S(1)}, bf16[288,1536]{1,0:T(8,128)(2,1)S(1)}, u32[]{:S(2)}, u32[]{:S(2)}) %collective-permute-start.4) | collective-permute-done | bytes 884768 | tf_op jit(solution)/shard_map/ppermute | solution.py:704
  234.6 5.3 layer_out.2
  242.0 7.5 fusion.11
  249.6 6.6 fusion.121
  257.2 5.6 layer_out.3
  262.9 6.7 convolution_add_fusion.12.refs_0_
  271.7 5.7 fusion.19
  300.0 9.6 %collective-permute-done.9.refs_1_ = bf16[288,1536]{1,0:T(8,128)(2,1)S(1)} collective-permute-done((bf16[288,1536]{1,0:T(8,128)(2,1)S(1)}, bf16[288,1536]{1,0:T(8,128)(2,1)S(1)}, u32[]{:S(2)}, u32[]{:S(2)}) %collective-permute-start.9) | collective-permute-done | bytes 884768 | tf_op jit(solution)/shard_map/ppermute | solution.py:704
  310.5 6.4 hidden_grad.2
  316.9 15.7 %down_grad.1 = (bf16[8,96,2048]{2,1,0:T(8,128)(2,1)}, bf16[8,96,2048]{2,1,0:T(8,128)(2,1)}) custom-call(s32[4]{0:T(128)} %pad_add_fusion.bits_ref, bf16[288,1536]{1,0:T(8,128)(2,1)} %get-tuple-element.182.refs_0_, bf16[288,1536]{1,0:T(8,128)(2,1)} %get-tuple-element.180.refs_1_, bf16[288,1536]{1,0:T(8,128)(2,1)} %copy-done.64, bf16[288,1536]{1,0:T(8,128)(2,1)} %copy-done.66, ...), custom_call_target="tpu_custom_call" | custom-call | flops 7247757312 | bytes 6291456 | tf_op jit(solution)/shard_map/down_grad/pallas_call | solution.py:632
  333.5 6.6 hidden_grad.3
  340.1 27.1 %gate_up_grad.1 = (bf16[8,96,4096]{2,1,0:T(8,128)(2,1)}, bf16[8,96,4096]{2,1,0:T(8,128)(2,1)}) custom-call(s32[4]{0:T(128)} %pad_add_fusion.bits_ref, bf16[288,1536]{1,0:T(8,128)(2,1)} %get-tuple-element.188.refs_0_, bf16[288,1536]{1,0:T(8,128)(2,1)} %get-tuple-element.166.refs_1_, bf16[288,1536]{1,0:T(8,128)(2,1)} %copy-done.61, ...), custom_call_target="tpu_custom_call" | custom-call | flops 14495514624 | bytes 12582912 | tf_op jit(solution)/shard_map/gate_up_grad/pallas_call | solution.py:632
  374.8 15.7 %collective-permute-done.12.refs_2_ = bf16[288,1536]{1,0:T(8,128)(2,1)S(1)} collective-permute-done((bf16[288,1536]{1,0:T(8,128)(2,1)}, bf16[288,1536]{1,0:T(8,128)(2,1)S(1)}, u32[]{:S(2)}, u32[]{:S(2)}) %collective-permute-start.12) | collective-permute-done | bytes 884768 | tf_op jit(solution)/shard_map/ppermute | solution.py:704
  393.9 5.6 add_and_split.21
  401.1 8.0 %collective-permute-done.13.refs_3_ = bf16[288,1536]{1,0:T(8,128)(2,1)} collective-permute-done((bf16[288,1536]{1,0:T(8,128)(2,1)}, bf16[288,1536]{1,0:T(8,128)(2,1)}, u32[]{:S(2)}, u32[]{:S(2)}) %collective-permute-start.13) | collective-permute-done | bytes 884768 | tf_op jit(solution)/shard_map/ppermute | solution.py:704
  409.1 8.7 %output_grad.1 = (bf16[8,96,768]{2,1,0:T(8,128)(2,1)}, bf16[8,96,768]{2,1,0:T(8,128)(2,1)}) custom-call(s32[4]{0:T(128)} %pad_add_fusion.bits_ref, bf16[288,1536]{1,0:T(8,128)(2,1)} %get-tuple-element.178.refs_0_, bf16[288,1536]{1,0:T(8,128)(2,1)} %get-tuple-element.186.refs_1_, bf16[288,1536]{1,0:T(8,128)(2,1)} %copy-done.70, ...), custom_call_target="tpu_custom_call" | custom-call | flops 2717908992 | bytes 2359296 | tf_op jit(solution)/shard_map/output_grad/pallas_call | solution.py:632
  421.9 8.3 %add_and_split.22 = (bf16[4,96,4096]{2,1,0:T(8,128)(2,1)}, bf16[4,96,4096]{2,1,0:T(8,128)(2,1)}) custom-call(s32[4]{0:T(128)} %pad_add_fusion.bits_ref, bf16[8,96,4096]{2,1,0:T(8,128)(2,1)} %get-tuple-element.193.kept_stay.kept_go, bf16[8,96,4096]{2,1,0:T(8,128)(2,1)} %collective-permute-done.15.moved_stay.moved_go, ...), custom_call_target="tpu_custom_call" | custom-call | flops 3300000000 | bytes 9000000 | tf_op jit(solution)/shard_map/add_and_split/pallas_call | solution.py:666
  431.8 32.2 %attention_backward.3 = (bf16[1152,768]{1,0:T(8,128)(2,1)}, bf16[1152,768]{1,0:T(8,128)(2,1)}, bf16[1152,768]{1,0:T(8,128)(2,1)}, bf16[768,768]{1,0:T(8,128)(2,1...) custom-call(s32[15]{0:T(128)} %reshape.297.refs_0_.present_ref, f32[576,768]{1,0:T(8,128)} %fusion.110.refs_1_.refs_0_, ...), custom_call_target="tpu_custom_call" | custom-call | flops 32999999488 | bytes 90000000 | tf_op jit(solution)/shard_map/attention_backward/pallas_call | solution.py:458
  472.0 32.3 %attention_backward.4 = (bf16[1152,768]{1,0:T(8,128)(2,1)}, bf16[1152,768]{1,0:T(8,128)(2,1)}, bf16[1152,768]{1,0:T(8,128)(2,1)}, bf16[768,768]{1,0:T(8,128)(2,1...) custom-call(s32[15]{0:T(128)} %reshape.297.refs_0_.present_ref, ...), custom_call_target="tpu_custom_call", output_to_operand_aliasing={{0}: (18, {}), {1}: (19, {}), {2}: (20, {}), {3}: (21, {}),... | custom-call | flops 32999999488 | bytes 90000000 | tf_op jit(solution)/shard_map/attention_backward/pallas_call | solution.py:458
  504.3 13.2 %projection_grad.2 = (bf16[8,96,1536]{2,1,0:T(8,128)(2,1)}, bf16[8,96,1536]{2,1,0:T(8,128)(2,1)}) custom-call(s32[4]{0:T(128)} %pad_add_fusion.bits_ref, bf16[576,1536]{1,0:T(8,128)(2,1)} %normed_in.2.refs_0_, bf16[576,1536]{1,0:T(8,128)(2,1)} %normed_in.3.refs_1_, bf16[1152,768]{1,0:T(8,128)(2,1)} %get-tuple-element.216.refs_2_.refs_17_, ...), custom_call_target="tpu_custom_call" | custom-call | flops 5435817984 | bytes 4718592 | tf_op jit(solution)/shard_map/projection_grad/pallas_call | solution.py:632
  517.8 9.6 %caption_grad.2 = (bf16[8,128,1024]{2,1,0:T(8,128)(2,1)}, bf16[8,128,1024]{2,1,0:T(8,128)(2,1)}) custom-call(s32[4]{0:T(128)} %pad_add_fusion.bits_ref, bf16[768,2048]{1,0:T(8,128)(2,1)} %bitcast.161, bf16[768,768]{1,0:T(8,128)(2,1)} %get-tuple-element.237.refs_1_.refs_20_, bf16[768,768]{1,0:T(8,128)(2,1)} %get-tuple-element.238.refs_2_.refs_21_), custom_call_target="tpu_custom_call" | custom-call | flops 3221225472 | bytes 4194304 | tf_op jit(solution)/shard_map/caption_grad/pallas_call | solution.py:632
  537.8 4.9 add_and_split.25
  542.7 7.3 collective-permute-done.21.moved_stay.moved_go
  555.7 5.0 add_and_split.27
  564.3 4.9 add_and_split.29
  569.2 32.5 %attention_backward.5 = (bf16[1152,768]{1,0:T(8,128)(2,1)}, bf16[1152,768]{1,0:T(8,128)(2,1)}, bf16[1152,768]{1,0:T(8,128)(2,1)}, bf16[768,768]{1,0:T(8,128)(2,1...) custom-call(s32[15]{0:T(128)} %reshape.297.refs_0_.present_ref, ...), custom_call_target="tpu_custom_call", output_to_operand_aliasing={{0}: (18, {}), {1}: (19, {}), {2}: (20, {}), {3}: (21, {}),... | custom-call | flops 32999999488 | bytes 90000000 | tf_op jit(solution)/shard_map/attention_backward/pallas_call | solution.py:458
  616.7 9.2 %projection_grad.3 = (bf16[8,96,768]{2,1,0:T(8,128)(2,1)}, bf16[8,96,768]{2,1,0:T(8,128)(2,1)}) custom-call(s32[4]{0:T(128)} %pad_add_fusion.bits_ref, bf16[576,1536]{1,0:T(8,128)(2,1)} %normed_in.2.refs_0_, bf16[576,1536]{1,0:T(8,128)(2,1)} %normed_in.3.refs_1_, bf16[1152,768]{1,0:T(8,128)(2,1)} %get-tuple-element.264.refs_2_, ...), custom_call_target="tpu_custom_call" | custom-call | flops 2717908992 | bytes 2359296 | tf_op jit(solution)/shard_map/projection_grad/pallas_call | solution.py:632
  626.8 7.1 caption_grad.3
  639.8 6.0 collective-permute-start.28
  645.8 4.7 add_and_split.30
  682.3 5.4 tokens_grad.2
  694.4 5.6 tokens_grad.3
  704.3 6.0 collective-permute-start.30
  714.2 4.6 collective-permute-done.31
  719.2 4.6 collective-permute-done.35
  749.9 5.1 collective-permute-done.42.moved_stay.moved_go
  (500 shorter events, 290.3 us)
Async XLA Ops:
  4.5 32.9 %collective-permute-start = (f32[3,3072]{1,0:T(4,128)S(1)}, f32[3,3072]{1,0:T(4,128)S(1)}, u32[]{:S(2)}, u32[]{:S(2)}) collective-permute-start(f32[3,3072]{1,0:T(4,128)S(1)} %convolution_add_fusion), channel_id=1, source_target_pairs={{1,0},{0,1},{3,2},{2,3},{5,4},{4,5},{7,6},{6,7},{9,8},{8,9},{11,10... | collective-permute-start | bytes 110600 | tf_op jit(solution)/shard_map/ppermute | solution.py:704
  7.5 46.4 %collective-permute-start.1 = (bf16[576,1536]{1,0:T(8,128)(2,1)}, bf16[576,1536]{1,0:T(8,128)(2,1)}, u32[]{:S(2)}, u32[]{:S(2)}) collective-permute-start(bf16[576,1536]{1,0:T(8,128)(2,1)} %refs_0_.1), channel_id=1, source_target_pairs={{1,0},{0,1},{3,2},{2,3},{5,4},{4,5},{7,6},{6,7},{9,8},{8,9},{11,10... | collective-permute-start | bytes 5308424 | tf_op jit(solution)/shard_map/ppermute | solution.py:704
  129.0 29.0 %collective-permute-start.2 = (bf16[288,1536]{1,0:T(8,128)(2,1)S(1)}, bf16[288,1536]{1,0:T(8,128)(2,1)}, u32[]{:S(2)}, u32[]{:S(2)}) collective-permute-start(bf16[288,1536]{1,0:T(8,128)(2,1)S(1)} %convolution_convert_fusion.3), channel_id=1, source_target_pairs={{1,0},{0,1},{3,2},{2,3},{5,4},{4,5},{7,6},{6,7},{9,8},{8,9},{11,10... | collective-permute-start | bytes 2654216 | tf_op jit(solution)/shard_map/ppermute | solution.py:704
  139.1 37.7 %collective-permute-start.5 = (bf16[288,1536]{1,0:T(8,128)(2,1)}, bf16[288,1536]{1,0:T(8,128)(2,1)S(1)}, u32[]{:S(2)}, u32[]{:S(2)}) collective-permute-start(bf16[288,1536]{1,0:T(8,128)(2,1)} %convolution_convert_fusion.2), channel_id=1, source_target_pairs={{1,0},{0,1},{3,2},{2,3},{5,4},{4,5},{7,6},{6,7},{9,8},{8,9},{11,10... | collective-permute-start | bytes 2654216 | tf_op jit(solution)/shard_map/ppermute | solution.py:704
  163.1 33.7 %collective-permute-start.3 = (bf16[288,1536]{1,0:T(8,128)(2,1)}, bf16[288,1536]{1,0:T(8,128)(2,1)S(1)}, u32[]{:S(2)}, u32[]{:S(2)}) collective-permute-start(bf16[288,1536]{1,0:T(8,128)(2,1)} %get-tuple-element.188.refs_0_), channel_id=1, source_target_pairs={{1,0},{0,1},{3,2},{2,3},{5,4},{4,5},{7,6},{6,7},{9,8},{8,9},{11,10... | collective-permute-start | bytes 2654216 | tf_op jit(solution)/shard_map/ppermute | solution.py:704
  183.4 31.4 %collective-permute-start.6 = (bf16[288,1536]{1,0:T(8,128)(2,1)}, bf16[288,1536]{1,0:T(8,128)(2,1)S(1)}, u32[]{:S(2)}, u32[]{:S(2)}) collective-permute-start(bf16[288,1536]{1,0:T(8,128)(2,1)} %get-tuple-element.166.refs_1_), channel_id=1, source_target_pairs={{1,0},{0,1},{3,2},{2,3},{5,4},{4,5},{7,6},{6,7},{9,8},{8,9},{11,10... | collective-permute-start | bytes 2654216 | tf_op jit(solution)/shard_map/ppermute | solution.py:704
  204.1 29.6 %collective-permute-start.4 = (bf16[288,1536]{1,0:T(8,128)(2,1)S(1)}, bf16[288,1536]{1,0:T(8,128)(2,1)S(1)}, u32[]{:S(2)}, u32[]{:S(2)}) collective-permute-start(bf16[288,1536]{1,0:T(8,128)(2,1)S(1)} %convolution_convert_fusion.1), channel_id=1, source_target_pairs={{1,0},{0,1},{3,2},{2,3},{5,4},{4,5},{7,6},{6,7},{9,8},{8,9},{11,10... | collective-permute-start | bytes 2654216 | tf_op jit(solution)/shard_map/ppermute | solution.py:704
  222.9 33.3 %collective-permute-start.7 = (bf16[288,1536]{1,0:T(8,128)(2,1)S(1)}, bf16[288,1536]{1,0:T(8,128)(2,1)S(1)}, u32[]{:S(2)}, u32[]{:S(2)}) collective-permute-start(bf16[288,1536]{1,0:T(8,128)(2,1)S(1)} %convolution_convert_fusion), channel_id=1, source_target_pairs={{1,0},{0,1},{3,2},{2,3},{5,4},{4,5},{7,6},{6,7},{9,8},{8,9},{11,10... | collective-permute-start | bytes 2654216 | tf_op jit(solution)/shard_map/ppermute | solution.py:704
  240.0 31.7 %collective-permute-start.8 = (bf16[288,1536]{1,0:T(8,128)(2,1)}, bf16[288,1536]{1,0:T(8,128)(2,1)S(1)}, u32[]{:S(2)}, u32[]{:S(2)}) collective-permute-start(bf16[288,1536]{1,0:T(8,128)(2,1)} %get-tuple-element.182.refs_0_), channel_id=1, source_target_pairs={{1,0},{0,1},{3,2},{2,3},{5,4},{4,5},{7,6},{6,7},{9,8},{8,9},{11,10... | collective-permute-start | bytes 2654216 | tf_op jit(solution)/shard_map/ppermute | solution.py:704
  262.8 29.5 %collective-permute-start.10 = (bf16[288,1536]{1,0:T(8,128)(2,1)}, bf16[288,1536]{1,0:T(8,128)(2,1)S(1)}, u32[]{:S(2)}, u32[]{:S(2)}) collective-permute-start(bf16[288,1536]{1,0:T(8,128)(2,1)} %get-tuple-element.180.refs_1_), channel_id=1, source_target_pairs={{1,0},{0,1},{3,2},{2,3},{5,4},{4,5},{7,6},{6,7},{9,8},{8,9},{11,10... | collective-permute-start | bytes 2654216 | tf_op jit(solution)/shard_map/ppermute | solution.py:704
  281.7 27.9 %collective-permute-start.9 = (bf16[288,1536]{1,0:T(8,128)(2,1)S(1)}, bf16[288,1536]{1,0:T(8,128)(2,1)S(1)}, u32[]{:S(2)}, u32[]{:S(2)}) collective-permute-start(bf16[288,1536]{1,0:T(8,128)(2,1)S(1)} %fusion.2), channel_id=1, source_target_pairs={{1,0},{0,1},{3,2},{2,3},{5,4},{4,5},{7,6},{6,7},{9,8},{8,9},{11,10... | collective-permute-start | bytes 2654216 | tf_op jit(solution)/shard_map/ppermute | solution.py:704
  299.1 33.5 %collective-permute-start.11 = (bf16[288,1536]{1,0:T(8,128)(2,1)S(1)}, bf16[288,1536]{1,0:T(8,128)(2,1)S(1)}, u32[]{:S(2)}, u32[]{:S(2)}) collective-permute-start(bf16[288,1536]{1,0:T(8,128)(2,1)S(1)} %fusion.3), channel_id=1, source_target_pairs={{1,0},{0,1},{3,2},{2,3},{5,4},{4,5},{7,6},{6,7},{9,8},{8,9},{11,10... | collective-permute-start | bytes 2654216 | tf_op jit(solution)/shard_map/ppermute | solution.py:704
  367.3 54.7 %collective-permute-start.15 = (bf16[8,96,4096]{2,1,0:T(8,128)(2,1)}, bf16[8,96,4096]{2,1,0:T(8,128)(2,1)}, u32[]{:S(2)}, u32[]{:S(2)}) collective-permute-start(bf16[8,96,4096]{2,1,0:T(8,128)(2,1)} %get-tuple-element.189), channel_id=1, source_target_pairs={{0,2},{2,0},{4,6},{6,4},{8,10},{10,8},{12,14},{14,12},{16,18},{18,... | collective-permute-start | bytes 18874376 | tf_op jit(solution)/shard_map/ppermute | solution.py:720
  367.4 24.8 %collective-permute-start.14 = (bf16[8,96,2048]{2,1,0:T(8,128)(2,1)}, bf16[8,96,2048]{2,1,0:T(8,128)(2,1)S(1)}, u32[]{:S(2)}, u32[]{:S(2)}) collective-permute-start(bf16[8,96,2048]{2,1,0:T(8,128)(2,1)} %get-tuple-element.183), channel_id=1, source_target_pairs={{0,2},{2,0},{4,6},{6,4},{8,10},{10,8},{12,14},{14,12},{16,18},{18,... | collective-permute-start | bytes 9437192 | tf_op jit(solution)/shard_map/ppermute | solution.py:720
  367.9 22.7 %collective-permute-start.12 = (bf16[288,1536]{1,0:T(8,128)(2,1)}, bf16[288,1536]{1,0:T(8,128)(2,1)S(1)}, u32[]{:S(2)}, u32[]{:S(2)}) collective-permute-start(bf16[288,1536]{1,0:T(8,128)(2,1)} %get-tuple-element.178.refs_0_), channel_id=1, source_target_pairs={{1,0},{0,1},{3,2},{2,3},{5,4},{4,5},{7,6},{6,7},{9,8},{8,9},{11,10... | collective-permute-start | bytes 2654216 | tf_op jit(solution)/shard_map/ppermute | solution.py:704
  369.9 39.2 %collective-permute-start.13 = (bf16[288,1536]{1,0:T(8,128)(2,1)}, bf16[288,1536]{1,0:T(8,128)(2,1)}, u32[]{:S(2)}, u32[]{:S(2)}) collective-permute-start(bf16[288,1536]{1,0:T(8,128)(2,1)} %get-tuple-element.186.refs_1_), channel_id=1, source_target_pairs={{1,0},{0,1},{3,2},{2,3},{5,4},{4,5},{7,6},{6,7},{9,8},{8,9},{11,10... | collective-permute-start | bytes 2654216 | tf_op jit(solution)/shard_map/ppermute | solution.py:704
  399.5 64.5 %collective-permute-start.16 = (bf16[4,96,2048]{2,1,0:T(8,128)(2,1)}, bf16[4,96,2048]{2,1,0:T(8,128)(2,1)}, u32[]{:S(2)}, u32[]{:S(2)}) collective-permute-start(bf16[4,96,2048]{2,1,0:T(8,128)(2,1)} %get-tuple-element.191), channel_id=1, source_target_pairs={{0,4},{2,6},{4,0},{6,2},{8,12},{10,14},{12,8},{14,10},{16,20},{18,... | collective-permute-start | bytes 4718600 | tf_op jit(solution)/shard_map/ppermute | solution.py:720
  417.7 46.3 %collective-permute-start.17 = (bf16[8,96,768]{2,1,0:T(8,128)(2,1)}, bf16[8,96,768]{2,1,0:T(8,128)(2,1)}, u32[]{:S(2)}, u32[]{:S(2)}) collective-permute-start(bf16[8,96,768]{2,1,0:T(8,128)(2,1)} %get-tuple-element.194), channel_id=1, source_target_pairs={{0,2},{2,0},{4,6},{6,4},{8,10},{10,8},{12,14},{14,12},{16,18},{18,... | collective-permute-start | bytes 3538952 | tf_op jit(solution)/shard_map/ppermute | solution.py:720
  430.2 105.9 %collective-permute-start.22 = (bf16[4,96,4096]{2,1,0:T(8,128)(2,1)}, bf16[4,96,4096]{2,1,0:T(8,128)(2,1)S(1)}, u32[]{:S(2)}, u32[]{:S(2)}) collective-permute-start(bf16[4,96,4096]{2,1,0:T(8,128)(2,1)} %get-tuple-element.196), channel_id=1, source_target_pairs={{0,4},{2,6},{4,0},{6,2},{8,12},{10,14},{12,8},{14,10},{16,20},{18,... | collective-permute-start | bytes 9437192 | tf_op jit(solution)/shard_map/ppermute | solution.py:720
  517.5 38.2 %collective-permute-start.20 = (bf16[8,96,1536]{2,1,0:T(8,128)(2,1)}, bf16[8,96,1536]{2,1,0:T(8,128)(2,1)}, u32[]{:S(2)}, u32[]{:S(2)}) collective-permute-start(bf16[8,96,1536]{2,1,0:T(8,128)(2,1)} %get-tuple-element.220), channel_id=1, source_target_pairs={{0,2},{2,0},{4,6},{6,4},{8,10},{10,8},{12,14},{14,12},{16,18},{18,... | collective-permute-start | bytes 7077896 | tf_op jit(solution)/shard_map/ppermute | solution.py:720
  527.4 37.0 %collective-permute-start.18 = (bf16[8,128,1024]{2,1,0:T(8,128)(2,1)}, bf16[8,128,1024]{2,1,0:T(8,128)(2,1)}, u32[]{:S(2)}, u32[]{:S(2)}) collective-permute-start(bf16[8,128,1024]{2,1,0:T(8,128)(2,1)} %get-tuple-element.214), channel_id=1, source_target_pairs={{0,2},{2,0},{4,6},{6,4},{8,10},{10,8},{12,14},{14,12},{16,18},{18,... | collective-permute-start | bytes 6291464 | tf_op jit(solution)/shard_map/ppermute | solution.py:720
  527.7 22.3 %collective-permute-start.21 = (bf16[2,96,2048]{2,1,0:T(8,128)(2,1)}, bf16[2,96,2048]{2,1,0:T(8,128)(2,1)}, u32[]{:S(2)}, u32[]{:S(2)}) collective-permute-start(bf16[2,96,2048]{2,1,0:T(8,128)(2,1)} %get-tuple-element.201), channel_id=1, source_target_pairs={{0,8},{2,10},{4,12},{6,14},{8,0},{10,2},{12,4},{14,6},{16,24},{18,... | collective-permute-start | bytes 2359304 | tf_op jit(solution)/shard_map/ppermute | solution.py:720
  535.6 25.1 %collective-permute-start.19 = (bf16[4,96,768]{2,1,0:T(8,128)(2,1)}, bf16[4,96,768]{2,1,0:T(8,128)(2,1)S(1)}, u32[]{:S(2)}, u32[]{:S(2)}) collective-permute-start(bf16[4,96,768]{2,1,0:T(8,128)(2,1)} %get-tuple-element.204), channel_id=1, source_target_pairs={{0,4},{2,6},{4,0},{6,2},{8,12},{10,14},{12,8},{14,10},{16,20},{18,... | collective-permute-start | bytes 1769480 | tf_op jit(solution)/shard_map/ppermute | solution.py:720
  553.0 81.4 %collective-permute-start.52 = (bf16[1,96,2048]{2,1,0:T(8,128)(2,1)}, bf16[1,96,2048]{2,1,0:T(8,128)(2,1)S(1)}, u32[]{:S(2)}, u32[]{:S(2)}) collective-permute-start(bf16[1,96,2048]{2,1,0:T(8,128)(2,1)} %get-tuple-element.226), channel_id=1, source_target_pairs={{0,16},{2,18},{4,20},{6,22},{8,24},{10,26},{12,28},{14,30},{16,0},... | collective-permute-start | bytes 1179656 | tf_op jit(solution)/shard_map/ppermute | solution.py:720
  605.9 44.6 %collective-permute-start.26 = (bf16[2,96,4096]{2,1,0:T(8,128)(2,1)}, bf16[2,96,4096]{2,1,0:T(8,128)(2,1)}, u32[]{:S(2)}, u32[]{:S(2)}) collective-permute-start(bf16[2,96,4096]{2,1,0:T(8,128)(2,1)} %get-tuple-element.224), channel_id=1, source_target_pairs={{0,8},{2,10},{4,12},{6,14},{8,0},{10,2},{12,4},{14,6},{16,24},{18,... | collective-permute-start | bytes 4718600 | tf_op jit(solution)/shard_map/ppermute | solution.py:720
  608.7 51.7 %collective-permute-start.24 = (bf16[2,96,768]{2,1,0:T(8,128)(2,1)}, bf16[2,96,768]{2,1,0:T(8,128)(2,1)}, u32[]{:S(2)}, u32[]{:S(2)}) collective-permute-start(bf16[2,96,768]{2,1,0:T(8,128)(2,1)} %get-tuple-element.230), channel_id=1, source_target_pairs={{0,8},{2,10},{4,12},{6,14},{8,0},{10,2},{12,4},{14,6},{16,24},{18,... | collective-permute-start | bytes 884744 | tf_op jit(solution)/shard_map/ppermute | solution.py:720
  608.8 27.0 %collective-permute-start.44 = (bf16[4,128,1024]{2,1,0:T(8,128)(2,1)}, bf16[4,128,1024]{2,1,0:T(8,128)(2,1)}, u32[]{:S(2)}, u32[]{:S(2)}) collective-permute-start(bf16[4,128,1024]{2,1,0:T(8,128)(2,1)} %get-tuple-element.232), channel_id=1, source_target_pairs={{0,4},{2,6},{4,0},{6,2},{8,12},{10,14},{12,8},{14,10},{16,20},{18,... | collective-permute-start | bytes 3145736 | tf_op jit(solution)/shard_map/ppermute | solution.py:720
  625.9 13.9 %collective-permute-start.27 = (bf16[8,96,768]{2,1,0:T(8,128)(2,1)}, bf16[8,96,768]{2,1,0:T(8,128)(2,1)}, u32[]{:S(2)}, u32[]{:S(2)}) collective-permute-start(bf16[8,96,768]{2,1,0:T(8,128)(2,1)} %get-tuple-element.247), channel_id=1, source_target_pairs={{0,2},{2,0},{4,6},{6,4},{8,10},{10,8},{12,14},{14,12},{16,18},{18,... | collective-permute-start | bytes 3538952 | tf_op jit(solution)/shard_map/ppermute | solution.py:720
  634.4 20.1 %collective-permute-start.25 = (bf16[8,128,512]{2,1,0:T(8,128)(2,1)}, bf16[8,128,512]{2,1,0:T(8,128)(2,1)}, u32[]{:S(2)}, u32[]{:S(2)}) collective-permute-start(bf16[8,128,512]{2,1,0:T(8,128)(2,1)} %get-tuple-element.251), channel_id=1, source_target_pairs={{0,2},{2,0},{4,6},{6,4},{8,10},{10,8},{12,14},{14,12},{16,18},{18,... | collective-permute-start | bytes 3145736 | tf_op jit(solution)/shard_map/ppermute | solution.py:720
  635.9 29.2 %collective-permute-start.23 = (bf16[4,96,1536]{2,1,0:T(8,128)(2,1)}, bf16[4,96,1536]{2,1,0:T(8,128)(2,1)}, u32[]{:S(2)}, u32[]{:S(2)}) collective-permute-start(bf16[4,96,1536]{2,1,0:T(8,128)(2,1)} %get-tuple-element.228), channel_id=1, source_target_pairs={{0,4},{2,6},{4,0},{6,2},{8,12},{10,14},{12,8},{14,10},{16,20},{18,... | collective-permute-start | bytes 3538952 | tf_op jit(solution)/shard_map/ppermute | solution.py:720
  639.8 39.5 %collective-permute-start.28 = (bf16[288,1536]{1,0:T(8,128)(2,1)}, bf16[288,1536]{1,0:T(8,128)(2,1)}, u32[]{:S(2)}, u32[]{:S(2)}) collective-permute-start(bf16[288,1536]{1,0:T(8,128)(2,1)} %fusion), channel_id=1, source_target_pairs={{1,0},{0,1},{3,2},{2,3},{5,4},{4,5},{7,6},{6,7},{9,8},{8,9},{11,10... | collective-permute-start | bytes 2654216 | tf_op jit(solution)/shard_map/ppermute | solution.py:704
  650.6 42.9 %collective-permute-start.29 = (bf16[288,1536]{1,0:T(8,128)(2,1)S(1)}, bf16[288,1536]{1,0:T(8,128)(2,1)}, u32[]{:S(2)}, u32[]{:S(2)}) collective-permute-start(bf16[288,1536]{1,0:T(8,128)(2,1)S(1)} %copy-done.18), channel_id=1, source_target_pairs={{1,0},{0,1},{3,2},{2,3},{5,4},{4,5},{7,6},{6,7},{9,8},{8,9},{11,10... | collective-permute-start | bytes 2654216 | tf_op jit(solution)/shard_map/ppermute | solution.py:704
  654.5 49.8 %collective-permute-start.45 = (bf16[2,128,1024]{2,1,0:T(8,128)(2,1)}, bf16[2,128,1024]{2,1,0:T(8,128)(2,1)}, u32[]{:S(2)}, u32[]{:S(2)}) collective-permute-start(bf16[2,128,1024]{2,1,0:T(8,128)(2,1)} %get-tuple-element.288), channel_id=1, source_target_pairs={{0,8},{2,10},{4,12},{6,14},{8,0},{10,2},{12,4},{14,6},{16,24},{18,... | collective-permute-start | bytes 1572872 | tf_op jit(solution)/shard_map/ppermute | solution.py:720
  660.5 76.4 %collective-permute-start.41 = (bf16[4,96,768]{2,1,0:T(8,128)(2,1)}, bf16[4,96,768]{2,1,0:T(8,128)(2,1)}, u32[]{:S(2)}, u32[]{:S(2)}) collective-permute-start(bf16[4,96,768]{2,1,0:T(8,128)(2,1)} %get-tuple-element.255), channel_id=1, source_target_pairs={{0,4},{2,6},{4,0},{6,2},{8,12},{10,14},{12,8},{14,10},{16,20},{18,... | collective-permute-start | bytes 1769480 | tf_op jit(solution)/shard_map/ppermute | solution.py:720
  665.0 111.5 %collective-permute-start.51 = (bf16[1,96,4096]{2,1,0:T(8,128)(2,1)}, bf16[1,96,4096]{2,1,0:T(8,128)(2,1)S(1)}, u32[]{:S(2)}, u32[]{:S(2)}) collective-permute-start(bf16[1,96,4096]{2,1,0:T(8,128)(2,1)} %get-tuple-element.257), channel_id=1, source_target_pairs={{0,16},{2,18},{4,20},{6,22},{8,24},{10,26},{12,28},{14,30},{16,0},... | collective-permute-start | bytes 2359304 | tf_op jit(solution)/shard_map/ppermute | solution.py:720
  679.4 49.7 %collective-permute-start.50 = (bf16[1,96,768]{2,1,0:T(8,128)(2,1)}, bf16[1,96,768]{2,1,0:T(8,128)(2,1)}, u32[]{:S(2)}, u32[]{:S(2)}) collective-permute-start(bf16[1,96,768]{2,1,0:T(8,128)(2,1)} %get-tuple-element.261), channel_id=1, source_target_pairs={{0,16},{2,18},{4,20},{6,22},{8,24},{10,26},{12,28},{14,30},{16,0},... | collective-permute-start | bytes 442376 | tf_op jit(solution)/shard_map/ppermute | solution.py:720
  693.5 67.0 %collective-permute-start.47 = (bf16[4,128,512]{2,1,0:T(8,128)(2,1)}, bf16[4,128,512]{2,1,0:T(8,128)(2,1)}, u32[]{:S(2)}, u32[]{:S(2)}) collective-permute-start(bf16[4,128,512]{2,1,0:T(8,128)(2,1)} %get-tuple-element.259), channel_id=1, source_target_pairs={{0,4},{2,6},{4,0},{6,2},{8,12},{10,14},{12,8},{14,10},{16,20},{18,... | collective-permute-start | bytes 1572872 | tf_op jit(solution)/shard_map/ppermute | solution.py:720
  704.3 8.9 %collective-permute-start.30 = (f32[3,6144]{1,0:T(4,128)S(1)}, f32[3,6144]{1,0:T(4,128)S(1)}, u32[]{:S(2)}, u32[]{:S(2)}) collective-permute-start(f32[3,6144]{1,0:T(4,128)S(1)} %pad_maximum_fusion.9), channel_id=1, source_target_pairs={{0,1},{1,0},{2,3},{3,2},{4,5},{5,4},{6,7},{7,6},{8,9},{9,8},{10,11... | collective-permute-start | bytes 221192 | tf_op jit(solution)/shard_map/ppermute | solution.py:720
  713.8 5.0 collective-permute-start.31
  728.2 15.0 %collective-permute-start.46 = (bf16[1,128,1024]{2,1,0:T(8,128)(2,1)}, bf16[1,128,1024]{2,1,0:T(8,128)(2,1)S(1)}, u32[]{:S(2)}, u32[]{:S(2)}) collective-permute-start(bf16[1,128,1024]{2,1,0:T(8,128)(2,1)} %get-tuple-element.290), channel_id=1, source_target_pairs={{0,16},{2,18},{4,20},{6,22},{8,24},{10,26},{12,28},{14,30},{16,0},... | collective-permute-start | bytes 786440 | tf_op jit(solution)/shard_map/ppermute | solution.py:720
  729.0 5.3 collective-permute-start.36
  734.3 8.8 %collective-permute-start.33 = (bf16[4,96,128]{2,1,0:T(8,128)(2,1)S(1)}, bf16[4,96,128]{2,1,0:T(8,128)(2,1)S(1)}, u32[]{:S(2)}, u32[]{:S(2)}) collective-permute-start(bf16[4,96,128]{2,1,0:T(8,128)(2,1)S(1)} %pad_maximum_fusion.10), channel_id=1, source_target_pairs={{0,4},{2,6},{4,0},{6,2},{8,12},{10,14},{12,8},{14,10},{16,20},{18,... | collective-permute-start | bytes 294920 | tf_op jit(solution)/shard_map/ppermute | solution.py:720
  741.0 24.6 %collective-permute-start.39 = (bf16[2,96,1536]{2,1,0:T(8,128)(2,1)S(1)}, bf16[2,96,1536]{2,1,0:T(8,128)(2,1)}, u32[]{:S(2)}, u32[]{:S(2)}) collective-permute-start(bf16[2,96,1536]{2,1,0:T(8,128)(2,1)S(1)} %copy-done.73), channel_id=1, source_target_pairs={{0,8},{2,10},{4,12},{6,14},{8,0},{10,2},{12,4},{14,6},{16,24},{18,... | collective-permute-start | bytes 1769480 | tf_op jit(solution)/shard_map/ppermute | solution.py:720
  743.1 11.9 %collective-permute-start.42 = (bf16[2,96,768]{2,1,0:T(8,128)(2,1)}, bf16[2,96,768]{2,1,0:T(8,128)(2,1)S(1)}, u32[]{:S(2)}, u32[]{:S(2)}) collective-permute-start(bf16[2,96,768]{2,1,0:T(8,128)(2,1)} %get-tuple-element.283), channel_id=1, source_target_pairs={{0,8},{2,10},{4,12},{6,14},{8,0},{10,2},{12,4},{14,6},{16,24},{18,... | collective-permute-start | bytes 884744 | tf_op jit(solution)/shard_map/ppermute | solution.py:720
  758.2 10.3 %collective-permute-start.43 = (bf16[1,96,768]{2,1,0:T(8,128)(2,1)}, bf16[1,96,768]{2,1,0:T(8,128)(2,1)S(1)}, u32[]{:S(2)}, u32[]{:S(2)}) collective-permute-start(bf16[1,96,768]{2,1,0:T(8,128)(2,1)} %get-tuple-element.285), channel_id=1, source_target_pairs={{0,16},{2,18},{4,20},{6,22},{8,24},{10,26},{12,28},{14,30},{16,0},... | collective-permute-start | bytes 442376 | tf_op jit(solution)/shard_map/ppermute | solution.py:720
  763.2 9.4 %collective-permute-start.48 = (bf16[2,128,512]{2,1,0:T(8,128)(2,1)}, bf16[2,128,512]{2,1,0:T(8,128)(2,1)S(1)}, u32[]{:S(2)}, u32[]{:S(2)}) collective-permute-start(bf16[2,128,512]{2,1,0:T(8,128)(2,1)} %get-tuple-element.293), channel_id=1, source_target_pairs={{0,8},{2,10},{4,12},{6,14},{8,0},{10,2},{12,4},{14,6},{16,24},{18,... | collective-permute-start | bytes 786440 | tf_op jit(solution)/shard_map/ppermute | solution.py:720
  768.5 13.3 %collective-permute-start.40 = (bf16[1,96,1536]{2,1,0:T(8,128)(2,1)}, bf16[1,96,1536]{2,1,0:T(8,128)(2,1)}, u32[]{:S(2)}, u32[]{:S(2)}) collective-permute-start(bf16[1,96,1536]{2,1,0:T(8,128)(2,1)} %get-tuple-element.280), channel_id=1, source_target_pairs={{0,16},{2,18},{4,20},{6,22},{8,24},{10,26},{12,28},{14,30},{16,0},... | collective-permute-start | bytes 884744 | tf_op jit(solution)/shard_map/ppermute | solution.py:720
  776.0 9.2 %collective-permute-start.49 = (bf16[1,128,512]{2,1,0:T(8,128)(2,1)}, bf16[1,128,512]{2,1,0:T(8,128)(2,1)S(1)}, u32[]{:S(2)}, u32[]{:S(2)}) collective-permute-start(bf16[1,128,512]{2,1,0:T(8,128)(2,1)} %get-tuple-element.295), channel_id=1, source_target_pairs={{0,16},{2,18},{4,20},{6,22},{8,24},{10,26},{12,28},{14,30},{16,0},... | collective-permute-start | bytes 393224 | tf_op jit(solution)/shard_map/ppermute | solution.py:720
  (122 other events, 710.0 us)

commit v3 on v2

--- a/solution.py
+++ b/solution.py
@@ -12,7 +12,7 @@
 theta = 10000.0
 lanes = 128
 half_lanes = 64
-query_block = 256
+query_block = 384
 bf16 = jnp.bfloat16
 f32 = jnp.float32
 vmem_bytes = 60 * 1024 * 1024
@@ -169,10 +169,15 @@
             span = slice(head * lanes, (head + 1) * lanes)
             scores = dot_nt(qa_ref[own, span], ka_ref[:, span])
             self_parts.append(dot_nn(jnp.exp(scores).astype(bf16), va_ref[:, span]))
-        acc_ref[0:size, :] = jnp.zeros((size, 2 * lanes), f32)
+        first_image = pl.multiple_of(present[index * (image_count + 1) + image_count] * cap_rows, 16)
+        for head in range(2):
+            span = slice(head * lanes, (head + 1) * lanes)
+            caps = pl.ds(first_image, cap_rows)
+            scores = dot_nt(qa_ref[own, span], ca_ref[caps, span])
+            acc_ref[0:size, span] = dot_nn(jnp.exp(scores).astype(bf16), cva_ref[caps, span])
         for image in range(image_count):
 
-            @pl.when(present[index * image_count + image] > 0)
+            @pl.when(present[index * (image_count + 1) + image] > 0)
             def _():
                 caps = slice(image * cap_rows, (image + 1) * cap_rows)
                 for head in range(2):
@@ -278,25 +283,28 @@
             dv_ref[:, span] += dot_nn(probs.astype(bf16), ga)
             dk_ref[:, span] += dot_nn(grad_scores, qa)
             dq_ref[top : top + half_lanes, own] = dot_nn(kt_ref[place, :], grad_scores)
+        def cross_part(caps):
+            for head in range(2):
+                span = slice(head * lanes, (head + 1) * lanes)
+                top = head * half_lanes
+                place = slice(head * lanes + top, head * lanes + top + half_lanes)
+                gate = gain_ref[0, 3:4, top : top + 1]
+                qa = qa_ref[own, span]
+                ga = ga_ref[own, span]
+                probs = jnp.exp(dot_nt(ca_ref[caps, span], qa))
+                grad_scores = (probs * dot_nt(cva_ref[caps, span], ga)).astype(bf16)
+                dcv_ref[caps, span] += dot_nn(probs.astype(bf16), ga)
+                dck_ref[caps, span] += dot_nn(grad_scores, qa)
+                dq_ref[top : top + half_lanes, own] += gate * dot_nn(
+                    ct_ref[place, caps], grad_scores
+                )
+
+        base = index * (image_count + 1)
         for image in range(image_count):
 
-            @pl.when(present[index * image_count + image] > 0)
+            @pl.when((present[base + image] > 0) | (present[base + image_count] == image))
             def _():
-                caps = slice(image * cap_rows, (image + 1) * cap_rows)
-                for head in range(2):
-                    span = slice(head * lanes, (head + 1) * lanes)
-                    top = head * half_lanes
-                    place = slice(head * lanes + top, head * lanes + top + half_lanes)
-                    gate = gain_ref[0, 3:4, top : top + 1]
-                    qa = qa_ref[own, span]
-                    ga = ga_ref[own, span]
-                    probs = jnp.exp(dot_nt(ca_ref[caps, span], qa))
-                    grad_scores = (probs * dot_nt(cva_ref[caps, span], ga)).astype(bf16)
-                    dcv_ref[caps, span] += dot_nn(probs.astype(bf16), ga)
-                    dck_ref[caps, span] += dot_nn(grad_scores, qa)
-                    dq_ref[top : top + half_lanes, own] += gate * dot_nn(
-                        ct_ref[place, caps], grad_scores
-                    )
+                cross_part(slice(image * cap_rows, (image + 1) * cap_rows))
 
     cosine = cos_ref[...]
     sine = sin_ref[...]
@@ -325,7 +333,7 @@
 
 def cost_of(seconds):
     return pl.CostEstimate(
-        flops=int(seconds * 1.1e15), bytes_accessed=int(seconds * 3e12), transcendentals=0
+        flops=int(1.0 * seconds * 1.1e15), bytes_accessed=int(1.0 * seconds * 3e12), transcendentals=0
     )
 
 
@@ -373,7 +381,7 @@
         + [jax.ShapeDtypeStruct((rows, 2 * width), bf16)] * 2
         + [jax.ShapeDtypeStruct((caps, 2 * width), bf16)],
         compiler_params=pltpu.CompilerParams(vmem_limit_bytes=vmem_bytes),
-        cost_estimate=cost_of(60e-6),
+        cost_estimate=cost_of(44e-6),
         name="attention_forward",
     )(present, *q_raw, *k_raw, *values, ck_raw, cap_values, gains, cosine, sine, fq, fk, fc)
 
@@ -393,6 +401,7 @@
     kept,
     grad_mixed,
     images,
+    seconds,
 ):
     cosine, sine = tables[:2]
     self_out, cross_out, qa, ka, ca = kept
@@ -463,7 +472,7 @@
         + [jax.ShapeDtypeStruct((pairs, 8, lanes), f32)],
         input_output_aliases={1 + len(inputs) + k: k for k in range(len(earlier))},
         compiler_params=pltpu.CompilerParams(vmem_limit_bytes=vmem_bytes),
-        cost_estimate=cost_of(15e-6 * calls_pairs),
+        cost_estimate=cost_of(seconds * calls_pairs),
         name="attention_backward",
     )(present, *inputs, *earlier)
 
@@ -487,7 +496,7 @@
     return total
 
 
-def row_stage(body, rows_in, tables, images, rows_out, sum_count, name):
+def row_stage(body, rows_in, tables, images, rows_out, sum_count, name, seconds=3e-7):
     count, width = rows_in[0][0].shape
     image_count = tables[0].shape[0]
     tile = next(size for size in (96, 48, 16) if count % size == 0)
@@ -530,7 +539,7 @@
         out_shape=[jax.ShapeDtypeStruct((count, width), kind) for kind in rows_out]
         + [jax.ShapeDtypeStruct((image_count, width), f32)] * sum_count,
         compiler_params=pltpu.CompilerParams(vmem_limit_bytes=vmem_bytes),
-        cost_estimate=cost_of(3e-6),
+        cost_estimate=cost_of(seconds),
         name=name,
     )(*flat, *tables, images[:, None])
 
@@ -586,20 +595,21 @@
     )
 
 
-def weight_grad(bits, shards, lefts, rights, name, tiles=(256, lanes)):
+def weight_grad(bits, shards, lefts, rights, name, tile, height=None, offset=0, into=None):
     depth = lefts[0].shape[1]
     rows = sum(left.shape[0] for left in lefts)
     shard_rows = depth // shards
     spans = [right[1:] for right in rights]
     rights = [right[0] for right in rights]
     widths = [width for _, width in spans]
-    tile = next(t for t in tiles if all(c % t == 0 for span in spans for c in span))
     starts = [sum(widths[:k]) // tile for k in range(len(widths) + 1)]
     ends = [len(lefts) + sum(len(pieces) for pieces in rights[:k]) for k in range(len(rights) + 1)]
+    height = height or starts[-1] * shard_rows
+    into = list(into or [])
 
     def kernel(bits_ref, *refs):
         left_refs = refs[: len(lefts)]
-        kept_ref, sent_ref, turned_ref, total_ref = refs[ends[-1] :]
+        kept_ref, sent_ref, turned_ref, total_ref = refs[ends[-1] + len(into) :]
         step = pl.program_id(0)
         bit = bits_ref[0]
 
@@ -627,8 +637,10 @@
         base = spans[index][0] // tile
         return pl.BlockSpec((count, tile), lambda j, s: (0, base + jnp.clip(j - first, 0, last)))
 
-    out = jax.ShapeDtypeStruct((shards // 2, shard_rows, sum(widths)), bf16)
-    out_spec = pl.BlockSpec((shards // 2, shard_rows, tile), lambda j, s: (0, 0, j))
+    out = jax.ShapeDtypeStruct((shards // 2, height, tile), bf16)
+    above = offset // shard_rows
+    out_spec = pl.BlockSpec((shards // 2, shard_rows, tile), lambda j, s: (0, above + j, 0))
+    aliased = 1 + ends[-1]
     return pl.pallas_call(
         kernel,
         grid_spec=pltpu.PrefetchScalarGridSpec(
@@ -639,17 +651,17 @@
                 right_spec(index, piece.shape[0])
                 for index, pieces in enumerate(rights)
                 for piece in pieces
-            ],
+            ]
+            + [pl.BlockSpec(memory_space=pl.ANY)] * len(into),
             out_specs=[out_spec, out_spec],
             scratch_shapes=[pltpu.VMEM((depth, rows), bf16), pltpu.VMEM((depth, tile), f32)],
         ),
         out_shape=[out, out],
+        input_output_aliases={aliased + k: k for k in range(len(into))},
         compiler_params=pltpu.CompilerParams(vmem_limit_bytes=vmem_bytes),
-        cost_estimate=pl.CostEstimate(
-            flops=2 * rows * depth * sum(widths), bytes_accessed=2 * depth * sum(widths), transcendentals=0
-        ),
+        cost_estimate=cost_of(5.2e-6 * starts[-1] * tile / 768),
         name=name,
-    )(bits, *lefts, *[piece for pieces in rights for piece in pieces])
+    )(bits, *lefts, *[piece for pieces in rights for piece in pieces], *into)
 
 
 def add_and_split(bits, level, kept, moved):
@@ -673,7 +685,7 @@
         ),
         out_shape=[out, out],
         compiler_params=pltpu.CompilerParams(vmem_limit_bytes=vmem_bytes),
-        cost_estimate=cost_of(3e-6),
+        cost_estimate=cost_of(1e-8),
         name="add_and_split",
     )(bits, kept, moved, kept, moved)
 
@@ -698,6 +710,53 @@
             self.total = self.kept[0].astype(f32) + moved[0].astype(f32)
             self.sent = self.total
 
+    def finish(self, *earlier):
+        while self.level < self.levels:
+            self.add(*earlier)
+
+    def finish_before(self, value):
+        while self.level < self.levels - 1:
+            self.add()
+        value, moved = lax.optimization_barrier((value, self.moved))
+        self.moved = moved
+        self.level += 1
+        self.total = self.kept[0].astype(f32) + moved[0].astype(f32)
+        return value
+
+    def columns(self, offset, shard_rows, width):
+        tile = self.total.shape[1]
+        parts = [
+            self.total[offset + k * shard_rows : offset + (k + 1) * shard_rows]
+            for k in range(width // tile)
+        ]
+        return jnp.concatenate(parts, axis=1)
+
+
+def assembled(early, late, layout, shapes, name):
+    tile = early[0].shape[2]
+
+    def kernel(early_kept, early_moved, late_kept, late_moved, *outs):
+        refs = ((early_kept, early_moved), (late_kept, late_moved))
+        for out, tiles in zip(outs, layout):
+            rows, width = out.shape
+            for column, (which, row) in enumerate(tiles):
+                left = column * tile
+                size = min(tile, width - left)
+                if size > 0:
+                    kept, moved = refs[which]
+                    place = slice(row, row + rows)
+                    out[:, left : left + size] = (
+                        kept[0, place, 0:size].astype(f32) + moved[0, place, 0:size].astype(f32)
+                    )
+
+    return pl.pallas_call(
+        kernel,
+        out_shape=[jax.ShapeDtypeStruct(shape, f32) for shape in shapes],
+        compiler_params=pltpu.CompilerParams(vmem_limit_bytes=vmem_bytes),
+        cost_estimate=cost_of(1e-6),
+        name=name,
+    )(*early, *late)
+
 
 def tensor_moved(array, step):
     count = lax.axis_size("tensor")
@@ -720,11 +779,15 @@
     return lax.ppermute(array, axis, [(i, i ^ (1 << bit)) for i in range(lax.axis_size(axis))])
 
 
-def gather_over_dp(array):
-    array = array[None]
+def gather_and_sum(between, own, part):
     for bit in reversed(bits_of("dp")):
-        array = jnp.concatenate([array, partner(array, "dp", bit)], axis=0)
-    return array
+        moved = partner(jnp.concatenate([own, part], axis=0), "dp", bit)
+        step = between.pop(0) if between else None
+        if step:
+            moved = step(moved)
+        own = jnp.concatenate([own, moved[: own.shape[0]]], axis=0)
+        part = part + moved[moved.shape[0] - part.shape[0] :]
+    return own, part
 
 
 def sum_over(array, axis):
@@ -825,7 +888,10 @@
     hit = (block_place[None, None, :] == jnp.arange(block_total)[:, None, None]) & (
         image_all[None, None, :] == jnp.arange(image_count)[None, :, None]
     )
-    present = jnp.max(hit.astype(jnp.int32), axis=2).reshape(-1)
+    hit = jnp.max(hit.astype(jnp.int32), axis=2)
+    first_image = jnp.argmax(hit, axis=1).astype(jnp.int32)[:, None]
+    beyond = jnp.where(jnp.arange(image_count)[None, :] == first_image, 0, hit)
+    present = jnp.concatenate([beyond, first_image], axis=1).reshape(-1)
     head_gate = jnp.tanh(cross_gate)
     gain_rows = jnp.stack(
         [
@@ -878,6 +944,8 @@
     cuts = range(chunks)
     bits = jnp.stack([(lax.axis_index("dp") >> bit) & 1 for bit in bits_of("dp")]).astype(jnp.int32)
     shards = lax.axis_size("dp")
+    hidden_columns = gate_weight.shape[1]
+    wide_tile = 256 if hidden_columns % 256 == 0 else lanes
 
     def piece_of(array, step, cut):
         start = step * local_rows + cut * chunk_rows
@@ -890,20 +958,23 @@
         return [tensor_moved(array, step) for step in steps]
 
     output_rows = pad_rows(output_weight, pair_columns)
+    output_rows = [output_rows] + [tensor_moved(output_rows, -step) for step in steps]
     tokens_cut = [piece_of(tokens, 0, cut) for cut in cuts]
     cotangent_cut = [piece_of(cotangent, 0, cut) for cut in cuts]
     images_cut = [piece_of(image_own, 0, cut) for cut in cuts]
 
-    attn_moved = [
-        returned([dot_nn(piece_of(mixed, step, cut), output_rows).astype(bf16) for step in steps])
+    mixed_own = [
+        [piece_of(mixed, 0, cut)] + returned([piece_of(mixed, step, cut) for step in steps])
         for cut in cuts
     ]
-    attn_kept = [dot_nn(piece_of(mixed, 0, cut), output_rows) for cut in cuts]
     attn, hidden, ffn_in = [], [], []
     for cut in cuts:
         attn_rows, hidden_rows, rows = row_stage(
             hidden_body,
-            [[attn_kept[cut]] + attn_moved[cut], [tokens_cut[cut]]],
+            [
+                [sum(dot_nn(part, rows) for part, rows in zip(mixed_own[cut], output_rows))],
+                [tokens_cut[cut]],
+            ],
             [post_attn, norm_ffn],
             images_cut[cut],
             [f32, f32, bf16],
@@ -976,10 +1047,13 @@
         return [of(cut, step) for step in range(tensor_count) for cut in cuts]
 
     grad_hidden, sums_ffn_norm, sums_attn_post, grad_attn = [], [], [], []
+    grad_mixed_own, grad_mixed_moved = [], []
     for cut in cuts:
         if cut == chunks - 1:
             lefts = group_pieces(lambda cut, step: grad_ffn[cut][step])
-            lefts[0] = after(lefts[0], latest)
+            lefts[0] = after(
+                lefts[0], latest, grad_mixed_own, [piece[2] for piece in backward[cut]]
+            )
             down_sum = DpSum(
                 bits,
                 weight_grad(
@@ -988,6 +1062,7 @@
                     lefts,
                     [whole_right(group_pieces(lambda cut, step: forward[cut][step][2]))],
                     "down_grad",
+                    wide_tile,
                 ),
             )
             down_sum.send()
@@ -1009,52 +1084,83 @@
         grad_hidden.append(hidden_grad)
         sums_ffn_norm.append(norm_sums)
         sums_attn_post.append(post_sums)
-        grad_attn.append([rows] + moved_in(rows))
-        latest = rows
+        grad_attn.append(rows)
+        grad_mixed_own.append([dot_nt(rows, weight).astype(bf16) for weight in output_rows])
+        grad_mixed_moved.append(
+            [tensor_moved(part, step) for step, part in enumerate(grad_mixed_own[cut][1:], 1)]
+        )
+        latest = (rows, grad_mixed_own[cut])
     lefts = group_pieces(lambda cut, step: ffn_in[cut][step])
-    lefts[0] = after(lefts[0], latest)
-    gate_up_sum = DpSum(
-        bits,
-        weight_grad(
+
+    def hidden_sum(index, *earlier):
+        rights = [whole_right(group_pieces(lambda cut, step: backward[cut][step][index]))]
+        own = [after(lefts[0], *earlier)] + lefts[1:]
+        return DpSum(bits, weight_grad(bits, shards, own, rights, "gate_up_grad", wide_tile))
+
+    gate_sum = hidden_sum(0, latest)
+    gate_sum.send()
+    up_sum = hidden_sum(1, gate_sum.sent, grad_mixed_moved)
+    up_sum.send()
+    down_sum.add(up_sum.sent)
+    grad_mixed = jnp.concatenate(
+        [grad_mixed_own[cut][0] for cut in cuts]
+        + [grad_mixed_moved[cut][step - 1] for step in steps for cut in cuts],
+        axis=0,
+    )
+    grad_mixed = after(grad_mixed, down_sum.sent)
+    grad_attn = [
+        [rows] + moved_in(after(rows, *[m for moved in grad_mixed_moved for m in moved]))
+        for rows in grad_attn
+    ]
+    grad_attn = group_pieces(lambda cut, step: grad_attn[cut][step])
+
+    width_rows, cap_rows = model_width // shards, cap_width // shards
+
+    def side_by_side(parts, start, width, with_output, earlier, between=None):
+        tile = 256 if start % 256 == 0 and width % 256 == 0 else lanes
+        tiles = width // tile
+        ahead = 2 * tiles * cap_rows
+        projection_at = -(-ahead // width_rows) * width_rows
+        output_at = projection_at + 3 * tiles * width_rows
+        height = output_at + (pair_columns // tile * width_rows if with_output else 0)
+        lefts = [after(normed[0], *earlier)] + list(normed[1:])
+        halves = weight_grad(
             bits,
             shards,
             lefts,
-            [
-                whole_right(group_pieces(lambda cut, step: backward[cut][step][k]))
-                for k in (0, 1)
-            ],
-            "gate_up_grad",
-        ),
-    )
-    gate_up_sum.send()
-    down_sum.add(gate_up_sum.sent)
-
-    grad_attn = group_pieces(lambda cut, step: grad_attn[cut][step])
-    grad_attn[-1] = after(grad_attn[-1], down_sum.sent)
-    grad_mixed = jnp.concatenate(
-        [dot_nt(piece, output_rows).astype(bf16) for piece in grad_attn], axis=0
-    )
-    output_sum = DpSum(
-        bits,
-        weight_grad(
+            [([part], start, width) for part in parts[:3]],
+            "projection_grad",
+            tile,
+            height,
+            projection_at,
+        )
+        halves = weight_grad(
             bits,
             shards,
-            grad_attn,
-            [whole_right([mixed])],
-            "output_grad",
-        ),
-    )
-    output_sum.send()
-    gate_up_sum.add(output_sum.sent)
-    grad_mixed = after(grad_mixed, gate_up_sum.sent)
-
-    def projection_sum(parts, start, width):
-        rights = [([part], start, width) for part in parts[:3]]
-        return DpSum(bits, weight_grad(bits, shards, normed, rights, "projection_grad"))
-
-    def caption_sum(parts, start, width):
-        rights = [([part], start, width) for part in parts[3:5]]
-        return DpSum(bits, weight_grad(bits, shards, [cap_flat], rights, "caption_grad"))
+            [cap_flat],
+            [([part], start, width) for part in parts[3:5]],
+            "caption_grad",
+            tile,
+            height,
+            0,
+            halves,
+        )
+        if with_output:
+            own = [after(grad_attn[0], between(halves))] + grad_attn[1:]
+            halves = weight_grad(
+                bits,
+                shards,
+                own,
+                [whole_right([mixed])],
+                "output_grad",
+                tile,
+                height,
+                output_at,
+                halves,
+            )
+        places = [projection_at + k * tiles * width_rows for k in range(3)]
+        places += [k * tiles * cap_rows for k in range(2)] + [output_at]
+        return DpSum(bits, halves), places
 
     parts = None
     first = 0
@@ -1075,25 +1181,33 @@
             kept,
             grad_mixed,
             image_count,
+            15e-6 if call == len(call_sizes) - 1 else 3e-6,
         )
         first += size
         if call == 0:
-            down_sum.add(parts[0])
-            output_sum.add(parts[0])
-            grad_mixed = after(grad_mixed, down_sum.sent, output_sum.sent)
+            gate_sum.add(parts[0])
+            down_sum.add(gate_sum.sent)
+            up_sum.add(down_sum.sent)
+            grad_mixed = after(grad_mixed, up_sum.sent)
         if call == len(call_sizes) - 2:
             early = first * lanes
-            query_early = projection_sum(parts, 0, early)
-            query_early.send()
-            caption_early = caption_sum(parts, 0, early)
-            caption_early.send()
-            gate_up_sum.add(parts[0])
-            down_sum.add(gate_up_sum.sent)
-            query_early.add(down_sum.sent, caption_early.sent)
-            output_sum.add(query_early.sent)
-            caption_early.add(output_sum.sent)
-            parts = [parts[0]] + list(after(tuple(parts[1:]), caption_early.sent))
-            grad_mixed = after(grad_mixed, caption_early.sent)
+            gate_sum.add(parts[0])
+            down_sum.add(gate_sum.sent)
+            early_sum, early_places = side_by_side(
+                parts,
+                0,
+                early,
+                True,
+                (down_sum.sent,),
+                lambda halves: gate_sum.add(halves) or up_sum.add(gate_sum.sent) or up_sum.sent,
+            )
+            early_sum.send()
+            early_sum.add()
+            parts = [parts[0]] + list(after(tuple(parts[1:]), early_sum.sent))
+            grad_mixed = after(grad_mixed, early_sum.sent)
+    parts = gate_sum.finish_before(down_sum.finish_before(tuple(parts)))
+    up_sum.add(parts[0])
+    parts = after(parts, up_sum.sent)
     grad_q, grad_k, grad_v, grad_ck, grad_cv, stats = parts
     stats = stats.transpose(1, 0, 2).reshape(8, pair_columns)[:, :head_columns]
     stats = stats.reshape(8, local_heads, head_size)
@@ -1112,20 +1226,25 @@
     sent = [[input_part(step, cut).astype(bf16) for step in steps] for cut in cuts]
     grad_normed_moved = [returned(part) for part in sent]
     late = pair_columns - early
-    query_late = projection_sum([after(grad_q, sent), grad_k, grad_v], early, late)
-    query_late.send()
-    grad_ck = after(grad_ck, query_late.sent)
-    caption_late = caption_sum([grad_q, grad_k, grad_v, grad_ck, grad_cv], early, late)
-    caption_late.send()
-    query_late.add(caption_late.sent)
-    gate_up_sum.add(query_late.sent)
-    caption_late.add(gate_up_sum.sent)
-    output_sum.add(caption_late.sent)
-    query_early.add(output_sum.sent)
-    grad_q = after(grad_q, query_early.sent)
+    late_sum, late_places = side_by_side(
+        [grad_q, grad_k, grad_v, grad_ck, grad_cv], early, late, False, (sent,)
+    )
+    late_sum.send()
+    up_sum.finish(late_sum.sent)
+    early_sum.add(late_sum.sent, up_sum.sent)
+    grad_q = after(grad_q, early_sum.sent)
     grad_normed_kept = [input_part(0, cut) for cut in cuts]
+    late_sum.add(grad_normed_kept)
+    grad_normed_moved = [
+        [after(moved, late_sum.sent) for moved in part] for part in grad_normed_moved
+    ]
     sums_attn_norm, tokens_grad = [], []
     for cut in cuts:
+        if cut == chunks - 1 and cut > 0:
+            early_sum.add(tokens_grad)
+            grad_normed_moved[cut] = [
+                after(moved, early_sum.sent) for moved in grad_normed_moved[cut]
+            ]
         rows, sums = row_stage(
             input_body,
             [[grad_normed_kept[cut]] + grad_normed_moved[cut], [tokens_cut[cut]], [grad_hidden[cut]]],
@@ -1134,37 +1253,35 @@
             [f32],
             1,
             "tokens_grad",
+            12e-6,
         )
         tokens_grad.append(rows)
         sums_attn_norm.append(sums)
-    sums_all = (
-        down_sum,
-        gate_up_sum,
-        output_sum,
-        query_early,
-        caption_early,
-        query_late,
-        caption_late,
-    )
-    for level in range(query_late.levels + 1):
-        for running in sums_all:
-            if running.level < level:
-                running.add()
-
-    def both_totals(first_sum, second_sum, index):
-        return jnp.concatenate(
-            [
-                first_sum.total[:, index * early : (index + 1) * early],
-                second_sum.total[:, index * late : (index + 1) * late],
-            ],
-            axis=1,
-        )[:, :head_columns]
+    def totals():
+        tile = early_sum.kept.shape[2]
+        layout = [
+            [(0, early_places[k] + c * rows) for c in range(early // tile)]
+            + [(1, late_places[k] + c * rows) for c in range(late // tile)]
+            for k, rows in enumerate([width_rows] * 3 + [cap_rows] * 2)
+        ]
+        return assembled(
+            (early_sum.kept, early_sum.moved),
+            (late_sum.kept, late_sum.moved),
+            layout,
+            [(width_rows, head_columns)] * 3 + [(cap_rows, head_columns)] * 2,
+            "assembled",
+        )
 
     sums = jnp.concatenate(
         [sum(part) for part in (sums_attn_norm, sums_attn_post, sums_ffn_norm, sums_ffn_post)],
         axis=1,
     )
-    sums = sum_over(sums, "tensor")
+    late_sum.add(tokens_grad)
+    sums = sum_over(after(sums, late_sum.sent), "tensor")
+    between = [
+        early_sum.finish_before,
+        lambda moved: late_sum.add(moved) or after(moved, late_sum.sent),
+    ]
     widths = [sums[:, k * model_width : (k + 1) * model_width] for k in range(4)]
     norm_parts = jnp.concatenate(
         [
@@ -1188,13 +1305,6 @@
     dp_count = lax.axis_size("dp")
     ada_width = silu_time.shape[1]
     ada_rows = ada_width // dp_count
-    gathered = gather_over_dp(
-        jnp.concatenate([grad_mod_own.astype(bf16), silu_time], axis=1).reshape(-1, lanes)
-    ).reshape(dp_count * image_count, mod_columns + ada_width)
-    time_own = lax.dynamic_slice_in_dim(
-        gathered, mod_columns + lax.axis_index("dp") * ada_rows, ada_rows, axis=1
-    )
-    ada_grad = dot_tn(time_own, gathered[:, :mod_columns])
     small = jnp.concatenate(
         [
             norm_parts,
@@ -1204,14 +1314,28 @@
         ]
     )
     length = small.shape[0]
-    small = sum_over(jnp.pad(small, (0, -length % 1024)).reshape(-1, lanes), "dp").reshape(-1)
+    gathered, small = gather_and_sum(
+        between,
+        jnp.concatenate([grad_mod_own, silu_time.astype(f32)], axis=1).reshape(-1, lanes),
+        jnp.pad(small, (0, -length % 1024)).reshape(-1, lanes),
+    )
+    gathered = gathered.astype(bf16).reshape(dp_count * image_count, mod_columns + ada_width)
+    small = small.reshape(-1)
+    time_own = lax.dynamic_slice_in_dim(
+        gathered, mod_columns + lax.axis_index("dp") * ada_rows, ada_rows, axis=1
+    )
+    ada_grad = dot_tn(time_own, gathered[:, :mod_columns])
+    for running in (down_sum, gate_sum, up_sum, early_sum):
+        running.finish(small)
+    while late_sum.level < late_sum.levels - 1:
+        late_sum.add()
+    projections = totals()
     norm_sums = small[: 4 * model_width].reshape(4, model_width)
     bias_own = small[4 * model_width : 4 * model_width + mod_columns]
     start = 4 * model_width + mod_columns
     gain_sums = small[start : start + 3 * head_columns].reshape(3, local_heads, head_size)
     start = start + 3 * head_columns
     gate_own = small[start : start + local_heads]
-    hidden_columns = gate_weight.shape[1]
     return (
         jnp.concatenate(layer_out, axis=0),
         jnp.concatenate(tokens_grad, axis=0),
@@ -1221,19 +1345,16 @@
         norm_sums[1],
         norm_sums[2],
         norm_sums[3],
-        both_totals(query_early, query_late, 0),
-        both_totals(query_early, query_late, 1),
-        both_totals(query_early, query_late, 2),
+        *projections[:3],
         gain_sums[0],
         gain_sums[1],
-        both_totals(caption_early, caption_late, 0),
-        both_totals(caption_early, caption_late, 1),
+        *projections[3:],
         gain_sums[2],
         gate_own,
-        output_sum.total.T[:head_columns],
-        gate_up_sum.total[:, :hidden_columns],
-        gate_up_sum.total[:, hidden_columns:],
-        down_sum.total.T,
+        early_sum.columns(early_places[5], width_rows, pair_columns).T[:head_columns],
+        gate_sum.columns(0, width_rows, hidden_columns),
+        up_sum.columns(0, width_rows, hidden_columns),
+        down_sum.columns(0, width_rows, hidden_columns).T,
     )
 
 

time: 796 us -> 752 us (0.945)
  waiting for transfers between devices: 109 us -> 83.9 us
  Pallas kernels: 382 us -> 360 us
  starting transfers between devices: 75.4 us -> 59.3 us
  local copies, waits for them, and re-layouts: 29 us -> 43 us
    ppermute x16 -> x19, waiting for transfers between devices: 71.5 us -> 20.4 us  [tensor_moved(): lax.ppermute(array, 'tensor', [((i + step) % count, i) for i in range(cou...]
    ppermute x37 -> x25, waiting for transfers between devices: 37.5 us -> 63.4 us  [partner(): lax.ppermute(array, axis, [(i, i ^ 1 << bit) for i in range(lax.axis_size...]
    ppermute x37 -> x25, starting transfers between devices: 43.5 us -> 25.9 us  [partner(): lax.ppermute(array, axis, [(i, i ^ 1 << bit) for i in range(lax.axis_size...]
    pallas_call x21 -> x15, Pallas kernels: 80.6 us -> 64.2 us  [add_and_split(): pl.pallas_call(kernel, grid_spec=pltpu.PrefetchScalarGridSpec(num_scalar_...]
    pallas_call x1, Pallas kernels: 57.5 us -> 43.8 us  [attention_forward(): pl.pallas_call(lambda *refs: forward_kernel(count, images, *refs), grid_s...]
    unnamed x244 -> x267, local copies, waits for them, and re-layouts: 13.1 us -> 24.2 us
    pallas_call x7 -> x8, Pallas kernels: 90.6 us -> 94.6 us  [weight_grad(): pl.pallas_call(kernel, grid_spec=pltpu.PrefetchScalarGridSpec(num_scalar_...]
    ppermute x16 -> x19, starting transfers between devices: 31.9 us -> 33.4 us  [tensor_moved(): lax.ppermute(array, 'tensor', [((i + step) % count, i) for i in range(cou...]
  transfers between devices with their start and end apart: 53 -> 44, of which waited for: 19 -> 11; matrix products, arithmetic and copies ran while one was open for 24% -> 28% of each run, Pallas kernels for 36% -> 47%
where the time goes in v3:
time: 752 us; the launch traced here: 741 us
  Pallas kernels  360 us (48%)
  matrix products  161 us (21%)
  waiting for transfers between devices  83.9 us (11%)
  starting transfers between devices  59.3 us (8%)
  local copies, waits for them, and re-layouts  43 us (6%)
  other arithmetic  29.7 us (4%)
    pallas_call x8, Pallas kernels, weight_grad(): pl.pallas_call(kernel, grid_spec=pltpu.PrefetchScalarGridSpec(num_scalar_...  94.6 us
    pallas_call x3, Pallas kernels, attention_backward(): pl.pallas_call(kernel, grid_spec=grid, out_shape=[jax.ShapeDtypeStruct((r...  90.5 us
    dot_general x25, matrix products, dot_nn(): lax.dot_general(left, right, (((1,), (0,)), ((), ())), preferred_element_...  81.2 us
    dot_general x28, matrix products, dot_nt(): lax.dot_general(left, right, (((1,), (1,)), ((), ())), preferred_element_...  78.4 us
    pallas_call x15, Pallas kernels, add_and_split(): pl.pallas_call(kernel, grid_spec=pltpu.PrefetchScalarGridSpec(num_scalar_...  64.2 us
    pallas_call x10, Pallas kernels, row_stage(): pl.pallas_call(kernel, grid=(count // tile,), in_specs=[row_spec] * len(f...  63.8 us
    ppermute x25, waiting for transfers between devices, partner(): lax.ppermute(array, axis, [(i, i ^ 1 << bit) for i in range(lax.axis_size...  63.4 us
    pallas_call x1, Pallas kernels, attention_forward(): pl.pallas_call(lambda *refs: forward_kernel(count, images, *refs), grid_s...  43.8 us
  transfers between devices with their start and end apart: 44, of which 11 were waited for; matrix products, arithmetic and copies ran while one was open for 28% of the time, Pallas kernels for 47%

profile of v3, /device:TPU:0, one launch (start us, length us, event | category | flops | bytes accessed | tf_op | source)
XLA Modules:
  0.0 740.8 jit_solution(9617908054350995238)
XLA Ops:
  0.7 3.9 convolution_add_fusion
  16.1 6.0 fusion.134.refs_7_.refs_6_
  31.3 4.0 sine_multiply_fusion
  40.5 5.3 normed_in.2.refs_0_
  45.8 5.1 fusion.130.refs_1_.refs_0_
  56.1 5.5 normed_in.3.refs_1_
  61.6 5.1 fusion.131.refs_2_.refs_1_
  71.9 43.8 %attention_forward.1 = (bf16[1152,768]{1,0:T(8,128)(2,1)}, bf16[1152,768]{1,0:T(8,128)(2,1)}, bf16[1152,768]{1,0:T(8,128)(2,1)}, bf16[1152,1536]{1,0:T(8,128)(2,...) custom-call(s32[12]{0:T(128)} %reshape.319.refs_0_.present_ref, f32[576,768]{1,0:T(8,128)} %fusion.130.refs_1_.refs_0_, ...), custom_call_target="tpu_custom_call" | custom-call | flops 48399998976 | bytes 132000000 | tf_op jit(solution)/shard_map/attention_forward/pallas_call | solution.py:377
  116.9 5.9 collective-permute-start.2
  128.2 5.7 collective-permute-done.2
  133.9 3.8 convolution_add_fusion.10.refs_0_
  137.7 4.8 hidden.2
  148.3 13.3 %hidden.3 = (f32[288,1536]{1,0:T(8,128)}, f32[288,1536]{1,0:T(8,128)}, bf16[288,1536]{1,0:T(8,128)(2,1)}) custom-call(f32[288,1536]{1,0:T(8,128)} %convolution_add_fusion.9.refs_0_, bf16[288,1536]{1,0:T(8,128)(2,1)} %get-tuple-element.372.refs_1_.refs_2_, f32[3,1536]{1,0:T(4,128)} %get-tuple-element.389.refs_2_.refs_6_, ...), custom_call_target="tpu_custom_call" | custom-call | flops 330000000 | bytes 900000 | tf_op jit(solution)/shard_map/hidden/pallas_call | solution.py:531
  161.8 4.9 fusion.135
  202.9 5.3 layer_out.2
  209.7 7.6 %fusion.11 = (bf16[288,2048]{1,0:T(8,128)(2,1)}, bf16[288,2048]{1,0:T(8,128)(2,1)S(1)}) fusion(f32[288,2048]{1,0:T(8,128)} %copy-done.97, bf16[288,2048]{1,0:T(8,128)(2,1)} %get-tuple-element.407, bf16[288,1536]{1,0:T(8,128)(2,1)} %get-tuple-element.210.refs_0_, bf16[2048,1536]{1,0:T(8,128)(2,1)} %param.50), kind=kOutput, calls=%fused_computation.41 | convolution fusion | flops 1821376512 | bytes 13074432 | tf_op jit(solution)/shard_map/dot_general | solution.py:39
  217.3 6.6 fusion.141
  224.8 5.8 layer_out.3
  231.3 7.0 convolution_add_fusion.14.refs_0_
  239.9 5.7 fusion.19
  267.3 10.5 %collective-permute-done.10.refs_1_ = bf16[288,1536]{1,0:T(8,128)(2,1)S(1)} collective-permute-done((bf16[288,1536]{1,0:T(8,128)(2,1)S(1)}, bf16[288,1536]{1,0:T(8,128)(2,1)S(1)}, u32[]{:S(2)}, u32[]{:S(2)}) %collective-permute-start.10) | collective-permute-done | bytes 884768 | tf_op jit(solution)/shard_map/ppermute | solution.py:763
  278.8 6.6 hidden_grad.2
  292.2 15.7 %down_grad.1 = (bf16[8,768,256]{2,1,0:T(8,128)(2,1)}, bf16[8,768,256]{2,1,0:T(8,128)(2,1)}) custom-call(s32[4]{0:T(128)} %pad_add_fusion.1.bits_ref, bf16[288,1536]{1,0:T(8,128)(2,1)} %get-tuple-element.210.refs_0_, bf16[288,1536]{1,0:T(8,128)(2,1)} %get-tuple-element.208.refs_1_, bf16[288,1536]{1,0:T(8,128)(2,1)} %copy-done.78, ...), custom_call_target="tpu_custom_call" | custom-call | flops 15253332992 | bytes 41600000 | tf_op jit(solution)/shard_map/down_grad/pallas_call | solution.py:644
  308.8 6.4 hidden_grad.3
  322.2 15.7 %gate_up_grad.2 = (bf16[8,768,256]{2,1,0:T(8,128)(2,1)}, bf16[8,768,256]{2,1,0:T(8,128)(2,1)}) custom-call(s32[4]{0:T(128)} %pad_add_fusion.1.bits_ref, bf16[288,1536]{1,0:T(8,128)(2,1)} %get-tuple-element.218.refs_0_, bf16[288,1536]{1,0:T(8,128)(2,1)} %get-tuple-element.194.refs_1_, bf16[288,1536]{1,0:T(8,128)(2,1)} %copy-done.74, ...), custom_call_target="tpu_custom_call" | custom-call | flops 15253332992 | bytes 41600000 | tf_op jit(solution)/shard_map/gate_up_grad/pallas_call | solution.py:644
  338.1 15.7 %gate_up_grad.3 = (bf16[8,768,256]{2,1,0:T(8,128)(2,1)}, bf16[8,768,256]{2,1,0:T(8,128)(2,1)}) custom-call(s32[4]{0:T(128)} %pad_add_fusion.1.bits_ref, bf16[288,1536]{1,0:T(8,128)(2,1)} %get-tuple-element.218.refs_0_, bf16[288,1536]{1,0:T(8,128)(2,1)} %get-tuple-element.194.refs_1_, bf16[288,1536]{1,0:T(8,128)(2,1)} %copy-done.74, ...), custom_call_target="tpu_custom_call" | custom-call | flops 15253332992 | bytes 41600000 | tf_op jit(solution)/shard_map/gate_up_grad/pallas_call | solution.py:644
  354.2 5.6 add_and_split.15
  364.3 30.1 %attention_backward.3 = (bf16[1152,768]{1,0:T(8,128)(2,1)}, bf16[1152,768]{1,0:T(8,128)(2,1)}, bf16[1152,768]{1,0:T(8,128)(2,1)}, bf16[768,768]{1,0:T(8,128)(2,1...) custom-call(s32[12]{0:T(128)} %reshape.319.refs_0_.present_ref, f32[576,768]{1,0:T(8,128)} %fusion.130.refs_1_.refs_0_, ...), custom_call_target="tpu_custom_call" | custom-call | flops 6600000000 | bytes 18000000 | tf_op jit(solution)/shard_map/attention_backward/pallas_call | solution.py:467
  394.5 5.6 add_and_split.16
  411.1 5.7 add_and_split.18
  418.2 30.3 %attention_backward.4 = (bf16[1152,768]{1,0:T(8,128)(2,1)}, bf16[1152,768]{1,0:T(8,128)(2,1)}, bf16[1152,768]{1,0:T(8,128)(2,1)}, bf16[768,768]{1,0:T(8,128)(2,1...) custom-call(s32[12]{0:T(128)} %reshape.319.refs_0_.present_ref, ...), custom_call_target="tpu_custom_call", output_to_operand_aliasing={{0}: (18, {}), {1}: (19, {}), {2}: (20, {}), {3}: (21, {}),... | custom-call | flops 6600000000 | bytes 18000000 | tf_op jit(solution)/shard_map/attention_backward/pallas_call | solution.py:467
  456.4 13.3 %projection_grad.2 = (bf16[8,1440,256]{2,1,0:T(8,128)(2,1)}, bf16[8,1440,256]{2,1,0:T(8,128)(2,1)}) custom-call(s32[4]{0:T(128)} %pad_add_fusion.1.bits_ref, bf16[576,1536]{1,0:T(8,128)(2,1)} %normed_in.2.refs_0_, bf16[576,1536]{1,0:T(8,128)(2,1)} %normed_in.3.refs_1_, bf16[1152,768]{1,0:T(8,128)(2,1)} %get-tuple-element.241.refs_2_.refs_17_, ...), custom_call_target="tpu_custom_call" | custom-call | flops 11440000000 | bytes 31200000 | tf_op jit(solution)/shard_map/projection_grad/pallas_call | solution.py:644
  469.7 9.5 %caption_grad.2 = (bf16[8,1440,256]{2,1,0:T(8,128)(2,1)}, bf16[8,1440,256]{2,1,0:T(8,128)(2,1)}) custom-call(s32[4]{0:T(128)} %pad_add_fusion.1.bits_ref, bf16[768,2048]{1,0:T(8,128)(2,1)} %bitcast.250, bf16[768,768]{1,0:T(8,128)(2,1)} %get-tuple-element.271.refs_1_.refs_20_, ...), custom_call_target="tpu_custom_call", output_to_operand_aliasing={{0}: (4, {}), {1}: (5, {})} | custom-call | flops 7626666496 | bytes 20800000 | tf_op jit(solution)/shard_map/caption_grad/pallas_call | solution.py:644
  487.7 8.8 %output_grad.1 = (bf16[8,1440,256]{2,1,0:T(8,128)(2,1)}, bf16[8,1440,256]{2,1,0:T(8,128)(2,1)}) custom-call(s32[4]{0:T(128)} %pad_add_fusion.1.bits_ref, bf16[288,1536]{1,0:T(8,128)(2,1)} %get-tuple-element.262.refs_0_, bf16[288,1536]{1,0:T(8,128)(2,1)} %get-tuple-element.263.refs_1_, ...), custom_call_target="tpu_custom_call", output_to_operand_aliasing={{0}: (6, {}), {1}: (7, {})} | custom-call | flops 5720000000 | bytes 15600000 | tf_op jit(solution)/shard_map/output_grad/pallas_call | solution.py:644
  506.6 7.9 %add_and_split.23 = (bf16[4,1440,256]{2,1,0:T(8,128)(2,1)}, bf16[4,1440,256]{2,1,0:T(8,128)(2,1)}) custom-call(s32[4]{0:T(128)} %pad_add_fusion.1.bits_ref, bf16[8,1440,256]{2,1,0:T(8,128)(2,1)} %get-tuple-element.264.kept_stay.kept_go, bf16[8,1440,256]{2,1,0:T(8,128)(2,1)} %collective-permute-done.25.moved_stay.moved_go, ...), custom_call_target="tpu_custom_call" | custom-call | flops 11000000 | bytes 30000 | tf_op jit(solution)/shard_map/add_and_split/pallas_call | solution.py:678
  515.0 30.1 %attention_backward.5 = (bf16[1152,768]{1,0:T(8,128)(2,1)}, bf16[1152,768]{1,0:T(8,128)(2,1)}, bf16[1152,768]{1,0:T(8,128)(2,1)}, bf16[768,768]{1,0:T(8,128)(2,1...) custom-call(s32[12]{0:T(128)} %reshape.319.refs_0_.present_ref, ...), custom_call_target="tpu_custom_call", output_to_operand_aliasing={{0}: (18, {}), {1}: (19, {}), {2}: (20, {}), {3}: (21, {}),... | custom-call | flops 32999999488 | bytes 90000000 | tf_op jit(solution)/shard_map/attention_backward/pallas_call | solution.py:467
  561.0 7.8 %collective-permute-start.32 = (bf16[288,1536]{1,0:T(8,128)(2,1)}, bf16[288,1536]{1,0:T(8,128)(2,1)}, u32[]{:S(2)}, u32[]{:S(2)}) collective-permute-start(bf16[288,1536]{1,0:T(8,128)(2,1)} %fusion.1), channel_id=1, source_target_pairs={{1,0},{0,1},{3,2},{2,3},{5,4},{4,5},{7,6},{6,7},{9,8},{8,9},{11,10... | collective-permute-start | bytes 2654216 | tf_op jit(solution)/shard_map/ppermute | solution.py:763
  571.7 9.1 %projection_grad.3 = (bf16[8,576,256]{2,1,0:T(8,128)(2,1)}, bf16[8,576,256]{2,1,0:T(8,128)(2,1)}) custom-call(s32[4]{0:T(128)} %pad_add_fusion.1.bits_ref, bf16[576,1536]{1,0:T(8,128)(2,1)} %normed_in.2.refs_0_, bf16[576,1536]{1,0:T(8,128)(2,1)} %normed_in.3.refs_1_, bf16[1152,768]{1,0:T(8,128)(2,1)} %get-tuple-element.307.refs_2_, ...), custom_call_target="tpu_custom_call" | custom-call | flops 5720000000 | bytes 15600000 | tf_op jit(solution)/shard_map/projection_grad/pallas_call | solution.py:644
  580.8 6.9 caption_grad.3
  601.2 5.0 add_and_split.25
  619.7 5.0 add_and_split.26
  626.3 5.4 tokens_grad.2
  631.7 9.5 %collective-permute-done.33.moved_stay.moved_go = bf16[2,1440,256]{2,1,0:T(8,128)(2,1)} collective-permute-done((bf16[2,1440,256]{2,1,0:T(8,128)(2,1)}, bf16[2,1440,256]{2,1,0:T(8,128)(2,1)}, u32[]{:S(2)}, u32[]{:S(2)}) %collective-permute-start.33) | collective-permute-done | bytes 1474592 | tf_op jit(solution)/shard_map/ppermute | solution.py:779
  645.0 5.5 tokens_grad.3
  668.5 33.3 %collective-permute-done.36 = f32[192,128]{1,0:T(8,128)S(1)} collective-permute-done((f32[192,128]{1,0:T(8,128)S(1)}, f32[192,128]{1,0:T(8,128)S(1)}, u32[]{:S(2)}, u32[]{:S(2)}) %collective-permute-start.36) | collective-permute-done | bytes 98336 | tf_op jit(solution)/shard_map/ppermute | solution.py:779
  703.9 4.3 collective-permute-done.38
  714.7 4.1 collective-permute-done.40
  721.4 8.6 %collective-permute-done.42.late_moved = bf16[1,576,256]{2,1,0:T(8,128)(2,1)} collective-permute-done((bf16[1,576,256]{2,1,0:T(8,128)(2,1)}, bf16[1,576,256]{2,1,0:T(8,128)(2,1)}, u32[]{:S(2)}, u32[]{:S(2)}) %collective-permute-start.42) | collective-permute-done | bytes 294944 | tf_op jit(solution)/shard_map/ppermute | solution.py:779
  (498 shorter events, 259.5 us)
Async XLA Ops:
  0.7 15.4 %copy-start = (bf16[2048,768]{1,0:T(8,128)(2,1)S(1)}, bf16[2048,768]{1,0:T(8,128)(2,1)}, u32[]{:S(2)}) copy-start(bf16[2048,768]{1,0:T(8,128)(2,1)} %param.43) | copy-start | bytes 9437188
  4.5 35.2 %collective-permute-start = (f32[3,3072]{1,0:T(4,128)S(1)}, f32[3,3072]{1,0:T(4,128)S(1)}, u32[]{:S(2)}, u32[]{:S(2)}) collective-permute-start(f32[3,3072]{1,0:T(4,128)S(1)} %convolution_add_fusion), channel_id=1, source_target_pairs={{1,0},{0,1},{3,2},{2,3},{5,4},{4,5},{7,6},{6,7},{9,8},{8,9},{11,10... | collective-permute-start | bytes 110600 | tf_op jit(solution)/shard_map/ppermute | solution.py:763
  7.5 48.6 %collective-permute-start.1 = (bf16[576,1536]{1,0:T(8,128)(2,1)}, bf16[576,1536]{1,0:T(8,128)(2,1)}, u32[]{:S(2)}, u32[]{:S(2)}) collective-permute-start(bf16[576,1536]{1,0:T(8,128)(2,1)} %refs_0_.1), channel_id=1, source_target_pairs={{1,0},{0,1},{3,2},{2,3},{5,4},{4,5},{7,6},{6,7},{9,8},{8,9},{11,10... | collective-permute-start | bytes 5308424 | tf_op jit(solution)/shard_map/ppermute | solution.py:763
  7.5 126.4 %collective-permute-start.3 = (bf16[768,1536]{1,0:T(8,128)(2,1)}, bf16[768,1536]{1,0:T(8,128)(2,1)}, u32[]{:S(2)}, u32[]{:S(2)}) collective-permute-start(bf16[768,1536]{1,0:T(8,128)(2,1)} %param.47), channel_id=1, source_target_pairs={{1,0},{0,1},{3,2},{2,3},{5,4},{4,5},{7,6},{6,7},{9,8},{8,9},{11,10... | collective-permute-start | bytes 7077896 | tf_op jit(solution)/shard_map/ppermute | solution.py:763
  116.9 17.0 %collective-permute-start.2 = (bf16[288,768]{1,0:T(8,128)(2,1)S(1)}, bf16[288,768]{1,0:T(8,128)(2,1)S(1)}, u32[]{:S(2)}, u32[]{:S(2)}) collective-permute-start(bf16[288,768]{1,0:T(8,128)(2,1)S(1)} %get-tuple-element.373), channel_id=1, source_target_pairs={{1,0},{0,1},{3,2},{2,3},{5,4},{4,5},{7,6},{6,7},{9,8},{8,9},{11,10... | collective-permute-start | bytes 1327112 | tf_op jit(solution)/shard_map/ppermute | solution.py:763
  125.5 19.1 %collective-permute-start.6 = (bf16[288,768]{1,0:T(8,128)(2,1)S(1)}, bf16[288,768]{1,0:T(8,128)(2,1)S(1)}, u32[]{:S(2)}, u32[]{:S(2)}) collective-permute-start(bf16[288,768]{1,0:T(8,128)(2,1)S(1)} %get-tuple-element.374), channel_id=1, source_target_pairs={{1,0},{0,1},{3,2},{2,3},{5,4},{4,5},{7,6},{6,7},{9,8},{8,9},{11,10... | collective-permute-start | bytes 1327112 | tf_op jit(solution)/shard_map/ppermute | solution.py:763
  142.5 31.5 %collective-permute-start.4 = (bf16[288,1536]{1,0:T(8,128)(2,1)}, bf16[288,1536]{1,0:T(8,128)(2,1)S(1)}, u32[]{:S(2)}, u32[]{:S(2)}) collective-permute-start(bf16[288,1536]{1,0:T(8,128)(2,1)} %get-tuple-element.218.refs_0_), channel_id=1, source_target_pairs={{1,0},{0,1},{3,2},{2,3},{5,4},{4,5},{7,6},{6,7},{9,8},{8,9},{11,10... | collective-permute-start | bytes 2654216 | tf_op jit(solution)/shard_map/ppermute | solution.py:763
  161.7 29.4 %collective-permute-start.7 = (bf16[288,1536]{1,0:T(8,128)(2,1)}, bf16[288,1536]{1,0:T(8,128)(2,1)S(1)}, u32[]{:S(2)}, u32[]{:S(2)}) collective-permute-start(bf16[288,1536]{1,0:T(8,128)(2,1)} %get-tuple-element.194.refs_1_), channel_id=1, source_target_pairs={{1,0},{0,1},{3,2},{2,3},{5,4},{4,5},{7,6},{6,7},{9,8},{8,9},{11,10... | collective-permute-start | bytes 2654216 | tf_op jit(solution)/shard_map/ppermute | solution.py:763
  181.2 20.6 %collective-permute-start.5 = (bf16[288,1536]{1,0:T(8,128)(2,1)S(1)}, bf16[288,1536]{1,0:T(8,128)(2,1)S(1)}, u32[]{:S(2)}, u32[]{:S(2)}) collective-permute-start(bf16[288,1536]{1,0:T(8,128)(2,1)S(1)} %convolution_convert_fusion.1), channel_id=1, source_target_pairs={{1,0},{0,1},{3,2},{2,3},{5,4},{4,5},{7,6},{6,7},{9,8},{8,9},{11,10... | collective-permute-start | bytes 2654216 | tf_op jit(solution)/shard_map/ppermute | solution.py:763
  198.3 25.6 %collective-permute-start.8 = (bf16[288,1536]{1,0:T(8,128)(2,1)S(1)}, bf16[288,1536]{1,0:T(8,128)(2,1)S(1)}, u32[]{:S(2)}, u32[]{:S(2)}) collective-permute-start(bf16[288,1536]{1,0:T(8,128)(2,1)S(1)} %convolution_convert_fusion), channel_id=1, source_target_pairs={{1,0},{0,1},{3,2},{2,3},{5,4},{4,5},{7,6},{6,7},{9,8},{8,9},{11,10... | collective-permute-start | bytes 2654216 | tf_op jit(solution)/shard_map/ppermute | solution.py:763
  208.2 31.7 %collective-permute-start.9 = (bf16[288,1536]{1,0:T(8,128)(2,1)}, bf16[288,1536]{1,0:T(8,128)(2,1)S(1)}, u32[]{:S(2)}, u32[]{:S(2)}) collective-permute-start(bf16[288,1536]{1,0:T(8,128)(2,1)} %get-tuple-element.210.refs_0_), channel_id=1, source_target_pairs={{1,0},{0,1},{3,2},{2,3},{5,4},{4,5},{7,6},{6,7},{9,8},{8,9},{11,10... | collective-permute-start | bytes 2654216 | tf_op jit(solution)/shard_map/ppermute | solution.py:763
  230.7 28.9 %collective-permute-start.11 = (bf16[288,1536]{1,0:T(8,128)(2,1)}, bf16[288,1536]{1,0:T(8,128)(2,1)S(1)}, u32[]{:S(2)}, u32[]{:S(2)}) collective-permute-start(bf16[288,1536]{1,0:T(8,128)(2,1)} %get-tuple-element.208.refs_1_), channel_id=1, source_target_pairs={{1,0},{0,1},{3,2},{2,3},{5,4},{4,5},{7,6},{6,7},{9,8},{8,9},{11,10... | collective-permute-start | bytes 2654216 | tf_op jit(solution)/shard_map/ppermute | solution.py:763
  231.3 16.5 %slice-start.10 = ((s8[6291456]{0:T(1024)(128)(4,1)}), s8[4194304]{0:T(1024)(128)(4,1)S(1)}, s32[]{:S(2)}) async-start(s8[6291456]{0:T(1024)(128)(4,1)} %bitcast.247), calls=%async_computation.10 | async-start | bytes 8388608
  249.9 27.9 %collective-permute-start.10 = (bf16[288,1536]{1,0:T(8,128)(2,1)S(1)}, bf16[288,1536]{1,0:T(8,128)(2,1)S(1)}, u32[]{:S(2)}, u32[]{:S(2)}) collective-permute-start(bf16[288,1536]{1,0:T(8,128)(2,1)S(1)} %fusion.2), channel_id=1, source_target_pairs={{1,0},{0,1},{3,2},{2,3},{5,4},{4,5},{7,6},{6,7},{9,8},{8,9},{11,10... | collective-permute-start | bytes 2654216 | tf_op jit(solution)/shard_map/ppermute | solution.py:763
  266.4 41.5 %collective-permute-start.12 = (bf16[288,1536]{1,0:T(8,128)(2,1)S(1)}, bf16[288,1536]{1,0:T(8,128)(2,1)S(1)}, u32[]{:S(2)}, u32[]{:S(2)}) collective-permute-start(bf16[288,1536]{1,0:T(8,128)(2,1)S(1)} %fusion.3), channel_id=1, source_target_pairs={{1,0},{0,1},{3,2},{2,3},{5,4},{4,5},{7,6},{6,7},{9,8},{8,9},{11,10... | collective-permute-start | bytes 2654216 | tf_op jit(solution)/shard_map/ppermute | solution.py:763
  290.8 47.3 %collective-permute-start.13 = (bf16[288,768]{1,0:T(8,128)(2,1)S(1)}, bf16[288,768]{1,0:T(8,128)(2,1)S(1)}, u32[]{:S(2)}, u32[]{:S(2)}) collective-permute-start(bf16[288,768]{1,0:T(8,128)(2,1)S(1)} %convolution_convert_fusion.7), channel_id=1, source_target_pairs={{1,0},{0,1},{3,2},{2,3},{5,4},{4,5},{7,6},{6,7},{9,8},{8,9},{11,10... | collective-permute-start | bytes 1327112 | tf_op jit(solution)/shard_map/ppermute | solution.py:763
  307.9 46.3 %collective-permute-start.15 = (bf16[8,768,256]{2,1,0:T(8,128)(2,1)}, bf16[8,768,256]{2,1,0:T(8,128)(2,1)}, u32[]{:S(2)}, u32[]{:S(2)}) collective-permute-start(bf16[8,768,256]{2,1,0:T(8,128)(2,1)} %get-tuple-element.211), channel_id=1, source_target_pairs={{0,2},{2,0},{4,6},{6,4},{8,10},{10,8},{12,14},{14,12},{16,18},{18,... | collective-permute-start | bytes 9437192 | tf_op jit(solution)/shard_map/ppermute | solution.py:779
  321.4 16.7 %collective-permute-start.14 = (bf16[288,768]{1,0:T(8,128)(2,1)S(1)}, bf16[288,768]{1,0:T(8,128)(2,1)S(1)}, u32[]{:S(2)}, u32[]{:S(2)}) collective-permute-start(bf16[288,768]{1,0:T(8,128)(2,1)S(1)} %convolution_convert_fusion.5), channel_id=1, source_target_pairs={{1,0},{0,1},{3,2},{2,3},{5,4},{4,5},{7,6},{6,7},{9,8},{8,9},{11,10... | collective-permute-start | bytes 1327112 | tf_op jit(solution)/shard_map/ppermute | solution.py:763
  337.9 56.5 %collective-permute-start.18 = (bf16[8,768,256]{2,1,0:T(8,128)(2,1)}, bf16[8,768,256]{2,1,0:T(8,128)(2,1)}, u32[]{:S(2)}, u32[]{:S(2)}) collective-permute-start(bf16[8,768,256]{2,1,0:T(8,128)(2,1)} %get-tuple-element.217), channel_id=1, source_target_pairs={{0,2},{2,0},{4,6},{6,4},{8,10},{10,8},{12,14},{14,12},{16,18},{18,... | collective-permute-start | bytes 9437192 | tf_op jit(solution)/shard_map/ppermute | solution.py:779
  338.1 15.7 %copy-start.33 = (bf16[288,768]{1,0:T(8,128)(2,1)}, bf16[288,768]{1,0:T(8,128)(2,1)S(1)}, u32[]{:S(2)}) copy-start(bf16[288,768]{1,0:T(8,128)(2,1)S(1)} %collective-permute-done.14) | copy-start | bytes 1327108
  353.8 55.6 %collective-permute-start.16 = (bf16[8,768,256]{2,1,0:T(8,128)(2,1)}, bf16[8,768,256]{2,1,0:T(8,128)(2,1)S(1)}, u32[]{:S(2)}, u32[]{:S(2)}) collective-permute-start(bf16[8,768,256]{2,1,0:T(8,128)(2,1)} %get-tuple-element.219), channel_id=1, source_target_pairs={{0,2},{2,0},{4,6},{6,4},{8,10},{10,8},{12,14},{14,12},{16,18},{18,... | collective-permute-start | bytes 9437192 | tf_op jit(solution)/shard_map/ppermute | solution.py:779
  359.8 40.3 %collective-permute-start.17 = (bf16[4,768,256]{2,1,0:T(8,128)(2,1)}, bf16[4,768,256]{2,1,0:T(8,128)(2,1)}, u32[]{:S(2)}, u32[]{:S(2)}) collective-permute-start(bf16[4,768,256]{2,1,0:T(8,128)(2,1)} %get-tuple-element.221), channel_id=1, source_target_pairs={{0,4},{2,6},{4,0},{6,2},{8,12},{10,14},{12,8},{14,10},{16,20},{18,... | collective-permute-start | bytes 4718600 | tf_op jit(solution)/shard_map/ppermute | solution.py:779
  400.0 48.5 %collective-permute-start.20 = (bf16[4,768,256]{2,1,0:T(8,128)(2,1)}, bf16[4,768,256]{2,1,0:T(8,128)(2,1)}, u32[]{:S(2)}, u32[]{:S(2)}) collective-permute-start(bf16[4,768,256]{2,1,0:T(8,128)(2,1)} %get-tuple-element.228), channel_id=1, source_target_pairs={{0,4},{2,6},{4,0},{6,2},{8,12},{10,14},{12,8},{14,10},{16,20},{18,... | collective-permute-start | bytes 4718600 | tf_op jit(solution)/shard_map/ppermute | solution.py:779
  403.6 48.9 %collective-permute-start.22 = (bf16[2,768,256]{2,1,0:T(8,128)(2,1)}, bf16[2,768,256]{2,1,0:T(8,128)(2,1)S(1)}, u32[]{:S(2)}, u32[]{:S(2)}) collective-permute-start(bf16[2,768,256]{2,1,0:T(8,128)(2,1)} %get-tuple-element.230), channel_id=1, source_target_pairs={{0,8},{2,10},{4,12},{6,14},{8,0},{10,2},{12,4},{14,6},{16,24},{18,... | collective-permute-start | bytes 2359304 | tf_op jit(solution)/shard_map/ppermute | solution.py:779
  405.6 82.1 %collective-permute-start.23 = (bf16[288,1536]{1,0:T(8,128)(2,1)}, bf16[288,1536]{1,0:T(8,128)(2,1)}, u32[]{:S(2)}, u32[]{:S(2)}) collective-permute-start(bf16[288,1536]{1,0:T(8,128)(2,1)} %get-tuple-element.262.refs_0_), channel_id=1, source_target_pairs={{1,0},{0,1},{3,2},{2,3},{5,4},{4,5},{7,6},{6,7},{9,8},{8,9},{11,10... | collective-permute-start | bytes 2654216 | tf_op jit(solution)/shard_map/ppermute | solution.py:763
  409.4 78.3 %collective-permute-start.24 = (bf16[288,1536]{1,0:T(8,128)(2,1)}, bf16[288,1536]{1,0:T(8,128)(2,1)}, u32[]{:S(2)}, u32[]{:S(2)}) collective-permute-start(bf16[288,1536]{1,0:T(8,128)(2,1)} %get-tuple-element.263.refs_1_), channel_id=1, source_target_pairs={{1,0},{0,1},{3,2},{2,3},{5,4},{4,5},{7,6},{6,7},{9,8},{8,9},{11,10... | collective-permute-start | bytes 2654216 | tf_op jit(solution)/shard_map/ppermute | solution.py:763
  416.8 66.3 %collective-permute-start.19 = (bf16[4,768,256]{2,1,0:T(8,128)(2,1)}, bf16[4,768,256]{2,1,0:T(8,128)(2,1)S(1)}, u32[]{:S(2)}, u32[]{:S(2)}) collective-permute-start(bf16[4,768,256]{2,1,0:T(8,128)(2,1)} %get-tuple-element.232), channel_id=1, source_target_pairs={{0,4},{2,6},{4,0},{6,2},{8,12},{10,14},{12,8},{14,10},{16,20},{18,... | collective-permute-start | bytes 4718600 | tf_op jit(solution)/shard_map/ppermute | solution.py:779
  452.0 27.1 %collective-permute-start.21 = (bf16[2,768,256]{2,1,0:T(8,128)(2,1)}, bf16[2,768,256]{2,1,0:T(8,128)(2,1)S(1)}, u32[]{:S(2)}, u32[]{:S(2)}) collective-permute-start(bf16[2,768,256]{2,1,0:T(8,128)(2,1)} %get-tuple-element.244), channel_id=1, source_target_pairs={{0,8},{2,10},{4,12},{6,14},{8,0},{10,2},{12,4},{14,6},{16,24},{18,... | collective-permute-start | bytes 2359304 | tf_op jit(solution)/shard_map/ppermute | solution.py:779
  496.6 10.0 %collective-permute-start.25 = (bf16[8,1440,256]{2,1,0:T(8,128)(2,1)}, bf16[8,1440,256]{2,1,0:T(8,128)(2,1)}, u32[]{:S(2)}, u32[]{:S(2)}) collective-permute-start(bf16[8,1440,256]{2,1,0:T(8,128)(2,1)} %get-tuple-element.265), channel_id=1, source_target_pairs={{0,2},{2,0},{4,6},{6,4},{8,10},{10,8},{12,14},{14,12},{16,18},{18,... | collective-permute-start | bytes 17694728 | tf_op jit(solution)/shard_map/ppermute | solution.py:779
  499.9 45.3 %collective-permute-start.26 = (bf16[1,768,256]{2,1,0:T(8,128)(2,1)S(1)}, bf16[1,768,256]{2,1,0:T(8,128)(2,1)S(1)}, u32[]{:S(2)}, u32[]{:S(2)}) collective-permute-start(bf16[1,768,256]{2,1,0:T(8,128)(2,1)S(1)} %copy-done.82), channel_id=1, source_target_pairs={{0,16},{2,18},{4,20},{6,22},{8,24},{10,26},{12,28},{14,30},{16,0},... | collective-permute-start | bytes 1179656 | tf_op jit(solution)/shard_map/ppermute | solution.py:779
  503.6 41.6 %collective-permute-start.27 = (bf16[1,768,256]{2,1,0:T(8,128)(2,1)}, bf16[1,768,256]{2,1,0:T(8,128)(2,1)S(1)}, u32[]{:S(2)}, u32[]{:S(2)}) collective-permute-start(bf16[1,768,256]{2,1,0:T(8,128)(2,1)} %get-tuple-element.258), channel_id=1, source_target_pairs={{0,16},{2,18},{4,20},{6,22},{8,24},{10,26},{12,28},{14,30},{16,0},... | collective-permute-start | bytes 1179656 | tf_op jit(solution)/shard_map/ppermute | solution.py:779
  503.6 41.6 %collective-permute-start.28 = (bf16[2,768,256]{2,1,0:T(8,128)(2,1)S(1)}, bf16[2,768,256]{2,1,0:T(8,128)(2,1)S(1)}, u32[]{:S(2)}, u32[]{:S(2)}) collective-permute-start(bf16[2,768,256]{2,1,0:T(8,128)(2,1)S(1)} %copy-done.81), channel_id=1, source_target_pairs={{0,8},{2,10},{4,12},{6,14},{8,0},{10,2},{12,4},{14,6},{16,24},{18,... | collective-permute-start | bytes 2359304 | tf_op jit(solution)/shard_map/ppermute | solution.py:779
  514.5 86.7 %collective-permute-start.29 = (bf16[4,1440,256]{2,1,0:T(8,128)(2,1)}, bf16[4,1440,256]{2,1,0:T(8,128)(2,1)}, u32[]{:S(2)}, u32[]{:S(2)}) collective-permute-start(bf16[4,1440,256]{2,1,0:T(8,128)(2,1)} %get-tuple-element.266), channel_id=1, source_target_pairs={{0,4},{2,6},{4,0},{6,2},{8,12},{10,14},{12,8},{14,10},{16,20},{18,... | collective-permute-start | bytes 8847368 | tf_op jit(solution)/shard_map/ppermute | solution.py:779
  561.0 65.2 %collective-permute-start.32 = (bf16[288,1536]{1,0:T(8,128)(2,1)}, bf16[288,1536]{1,0:T(8,128)(2,1)}, u32[]{:S(2)}, u32[]{:S(2)}) collective-permute-start(bf16[288,1536]{1,0:T(8,128)(2,1)} %fusion.1), channel_id=1, source_target_pairs={{1,0},{0,1},{3,2},{2,3},{5,4},{4,5},{7,6},{6,7},{9,8},{8,9},{11,10... | collective-permute-start | bytes 2654216 | tf_op jit(solution)/shard_map/ppermute | solution.py:763
  568.9 57.4 %collective-permute-start.30 = (bf16[288,1536]{1,0:T(8,128)(2,1)}, bf16[288,1536]{1,0:T(8,128)(2,1)}, u32[]{:S(2)}, u32[]{:S(2)}) collective-permute-start(bf16[288,1536]{1,0:T(8,128)(2,1)} %fusion), channel_id=1, source_target_pairs={{1,0},{0,1},{3,2},{2,3},{5,4},{4,5},{7,6},{6,7},{9,8},{8,9},{11,10... | collective-permute-start | bytes 2654216 | tf_op jit(solution)/shard_map/ppermute | solution.py:763
  568.9 30.1 %collective-permute-start.43 = (bf16[1,768,256]{2,1,0:T(8,128)(2,1)}, bf16[1,768,256]{2,1,0:T(8,128)(2,1)}, u32[]{:S(2)}, u32[]{:S(2)}) collective-permute-start(bf16[1,768,256]{2,1,0:T(8,128)(2,1)} %get-tuple-element.294), channel_id=1, source_target_pairs={{0,16},{2,18},{4,20},{6,22},{8,24},{10,26},{12,28},{14,30},{16,0},... | collective-permute-start | bytes 1179656 | tf_op jit(solution)/shard_map/ppermute | solution.py:779
  587.7 32.0 %collective-permute-start.31 = (bf16[8,576,256]{2,1,0:T(8,128)(2,1)}, bf16[8,576,256]{2,1,0:T(8,128)(2,1)}, u32[]{:S(2)}, u32[]{:S(2)}) collective-permute-start(bf16[8,576,256]{2,1,0:T(8,128)(2,1)} %get-tuple-element.304), channel_id=1, source_target_pairs={{0,2},{2,0},{4,6},{6,4},{8,10},{10,8},{12,14},{14,12},{16,18},{18,... | collective-permute-start | bytes 7077896 | tf_op jit(solution)/shard_map/ppermute | solution.py:779
  606.2 35.0 %collective-permute-start.33 = (bf16[2,1440,256]{2,1,0:T(8,128)(2,1)}, bf16[2,1440,256]{2,1,0:T(8,128)(2,1)}, u32[]{:S(2)}, u32[]{:S(2)}) collective-permute-start(bf16[2,1440,256]{2,1,0:T(8,128)(2,1)} %get-tuple-element.306), channel_id=1, source_target_pairs={{0,8},{2,10},{4,12},{6,14},{8,0},{10,2},{12,4},{14,6},{16,24},{18,... | collective-permute-start | bytes 4423688 | tf_op jit(solution)/shard_map/ppermute | solution.py:779
  624.8 28.3 %collective-permute-start.34 = (bf16[4,576,256]{2,1,0:T(8,128)(2,1)}, bf16[4,576,256]{2,1,0:T(8,128)(2,1)S(1)}, u32[]{:S(2)}, u32[]{:S(2)}) collective-permute-start(bf16[4,576,256]{2,1,0:T(8,128)(2,1)} %get-tuple-element.310), channel_id=1, source_target_pairs={{0,4},{2,6},{4,0},{6,2},{8,12},{10,14},{12,8},{14,10},{16,20},{18,... | collective-permute-start | bytes 3538952 | tf_op jit(solution)/shard_map/ppermute | solution.py:779
  657.6 6.3 collective-permute-start.35
  663.1 39.5 %copy-start.31 = (bf16[1,1440,256]{2,1,0:T(8,128)(2,1)S(1)}, bf16[1,1440,256]{2,1,0:T(8,128)(2,1)}, u32[]{:S(2)}) copy-start(bf16[1,1440,256]{2,1,0:T(8,128)(2,1)} %get-tuple-element.339.early_kept) | copy-start | bytes 2211844
  663.1 38.6 %collective-permute-start.37 = (bf16[1,1440,256]{2,1,0:T(8,128)(2,1)}, bf16[1,1440,256]{2,1,0:T(8,128)(2,1)S(1)}, u32[]{:S(2)}, u32[]{:S(2)}) collective-permute-start(bf16[1,1440,256]{2,1,0:T(8,128)(2,1)} %get-tuple-element.317), channel_id=1, source_target_pairs={{0,16},{2,18},{4,20},{6,22},{8,24},{10,26},{12,28},{14,30},{16,0},... | collective-permute-start | bytes 2211848 | tf_op jit(solution)/shard_map/ppermute | solution.py:779
  663.4 40.5 %collective-permute-start.39 = (bf16[2,576,256]{2,1,0:T(8,128)(2,1)}, bf16[2,576,256]{2,1,0:T(8,128)(2,1)S(1)}, u32[]{:S(2)}, u32[]{:S(2)}) collective-permute-start(bf16[2,576,256]{2,1,0:T(8,128)(2,1)} %get-tuple-element.331), channel_id=1, source_target_pairs={{0,8},{2,10},{4,12},{6,14},{8,0},{10,2},{12,4},{14,6},{16,24},{18,... | collective-permute-start | bytes 1769480 | tf_op jit(solution)/shard_map/ppermute | solution.py:779
  664.5 37.2 %collective-permute-start.36 = (f32[192,128]{1,0:T(8,128)S(1)}, f32[192,128]{1,0:T(8,128)S(1)}, u32[]{:S(2)}, u32[]{:S(2)}) collective-permute-start(f32[192,128]{1,0:T(8,128)S(1)} %pad_maximum_fusion.6), channel_id=1, source_target_pairs={{0,16},{2,18},{4,20},{6,22},{8,24},{10,26},{12,28},{14,30},{16,0},... | collective-permute-start | bytes 294920 | tf_op jit(solution)/shard_map/ppermute | solution.py:779
  702.4 5.8 collective-permute-start.38
  711.7 7.1 collective-permute-start.40
  714.7 15.3 %collective-permute-start.42 = (bf16[1,576,256]{2,1,0:T(8,128)(2,1)}, bf16[1,576,256]{2,1,0:T(8,128)(2,1)}, u32[]{:S(2)}, u32[]{:S(2)}) collective-permute-start(bf16[1,576,256]{2,1,0:T(8,128)(2,1)} %get-tuple-element.337), channel_id=1, source_target_pairs={{0,16},{2,18},{4,20},{6,22},{8,24},{10,26},{12,28},{14,30},{16,0},... | collective-permute-start | bytes 884744 | tf_op jit(solution)/shard_map/ppermute | solution.py:779
  720.1 12.7 %collective-permute-start.41 = (f32[864,128]{1,0:T(8,128)}, f32[864,128]{1,0:T(8,128)S(1)}, u32[]{:S(2)}, u32[]{:S(2)}) collective-permute-start(f32[864,128]{1,0:T(8,128)} %constant_dynamic-update-slice_fusion.1), channel_id=1, source_target_pairs={{0,2},{2,0},{4,6},{6,4},{8,10},{10,8},{12,14},{14,12},{16,18},{18,... | collective-permute-start | bytes 1327112 | tf_op jit(solution)/shard_map/ppermute | solution.py:779
  (113 other events, 521.4 us)

commit v4 on v3

--- a/solution.py
+++ b/solution.py
@@ -1277,9 +1277,9 @@
         axis=1,
     )
     late_sum.add(tokens_grad)
-    sums = sum_over(after(sums, late_sum.sent), "tensor")
+    sums = early_sum.finish_before(sum_over(after(sums, late_sum.sent), "tensor"))
     between = [
-        early_sum.finish_before,
+        None,
         lambda moved: late_sum.add(moved) or after(moved, late_sum.sent),
     ]
     widths = [sums[:, k * model_width : (k + 1) * model_width] for k in range(4)]

time: 752 us -> 741 us (0.985)
    unnamed x267 -> x265, local copies, waits for them, and re-layouts: 24.2 us -> 24.6 us
  transfers between devices with their start and end apart: 44 -> 44, of which waited for: 11 -> 13; matrix products, arithmetic and copies ran while one was open for 28% -> 28% of each run, Pallas kernels for 47% -> 48%
where the time goes in v4:
time: 741 us; the launch traced here: 730 us
  Pallas kernels  360 us (49%)
  matrix products  161 us (22%)
  waiting for transfers between devices  77.3 us (10%)
  starting transfers between devices  54.4 us (7%)
  local copies, waits for them, and re-layouts  43.4 us (6%)
  other arithmetic  30 us (4%)
    pallas_call x8, Pallas kernels, weight_grad(): pl.pallas_call(kernel, grid_spec=pltpu.PrefetchScalarGridSpec(num_scalar_...  94.5 us
    pallas_call x3, Pallas kernels, attention_backward(): pl.pallas_call(kernel, grid_spec=grid, out_shape=[jax.ShapeDtypeStruct((r...  90.4 us
    dot_general x25, matrix products, dot_nn(): lax.dot_general(left, right, (((1,), (0,)), ((), ())), preferred_element_...  81.2 us
    dot_general x28, matrix products, dot_nt(): lax.dot_general(left, right, (((1,), (1,)), ((), ())), preferred_element_...  78.4 us
    pallas_call x15, Pallas kernels, add_and_split(): pl.pallas_call(kernel, grid_spec=pltpu.PrefetchScalarGridSpec(num_scalar_...  64.2 us
    pallas_call x10, Pallas kernels, row_stage(): pl.pallas_call(kernel, grid=(count // tile,), in_specs=[row_spec] * len(f...  63.9 us
    ppermute x25, waiting for transfers between devices, partner(): lax.ppermute(array, axis, [(i, i ^ 1 << bit) for i in range(lax.axis_size...  57.1 us
    pallas_call x1, Pallas kernels, attention_forward(): pl.pallas_call(lambda *refs: forward_kernel(count, images, *refs), grid_s...  43.8 us
  transfers between devices with their start and end apart: 44, of which 13 were waited for; matrix products, arithmetic and copies ran while one was open for 28% of the time, Pallas kernels for 48%

profile of v4, /device:TPU:0, one launch (start us, length us, event | category | flops | bytes accessed | tf_op | source)
XLA Modules:
  0.0 729.8 jit_solution(9301168257924485779)
XLA Ops:
  0.7 3.9 convolution_add_fusion
  16.1 6.0 fusion.134.refs_7_.refs_6_
  31.3 4.0 sine_multiply_fusion
  40.5 5.3 normed_in.2.refs_0_
  45.8 5.1 fusion.130.refs_1_.refs_0_
  56.1 5.5 normed_in.3.refs_1_
  61.6 5.1 fusion.131.refs_2_.refs_1_
  71.9 43.8 %attention_forward.1 = (bf16[1152,768]{1,0:T(8,128)(2,1)}, bf16[1152,768]{1,0:T(8,128)(2,1)}, bf16[1152,768]{1,0:T(8,128)(2,1)}, bf16[1152,1536]{1,0:T(8,128)(2,...) custom-call(s32[12]{0:T(128)} %reshape.319.refs_0_.present_ref, f32[576,768]{1,0:T(8,128)} %fusion.130.refs_1_.refs_0_, ...), custom_call_target="tpu_custom_call" | custom-call | flops 48399998976 | bytes 132000000 | tf_op jit(solution)/shard_map/attention_forward/pallas_call | solution.py:377
  116.9 5.8 collective-permute-start.2
  128.2 5.7 collective-permute-done.2
  137.7 4.8 hidden.2
  148.3 13.3 %hidden.3 = (f32[288,1536]{1,0:T(8,128)}, f32[288,1536]{1,0:T(8,128)}, bf16[288,1536]{1,0:T(8,128)(2,1)}) custom-call(f32[288,1536]{1,0:T(8,128)} %convolution_add_fusion.9.refs_0_, bf16[288,1536]{1,0:T(8,128)(2,1)} %get-tuple-element.372.refs_1_.refs_2_, f32[3,1536]{1,0:T(4,128)} %get-tuple-element.389.refs_2_.refs_6_, ...), custom_call_target="tpu_custom_call" | custom-call | flops 330000000 | bytes 900000 | tf_op jit(solution)/shard_map/hidden/pallas_call | solution.py:531
  161.8 4.9 fusion.135
  202.9 5.3 layer_out.2
  209.7 7.6 %fusion.11 = (bf16[288,2048]{1,0:T(8,128)(2,1)}, bf16[288,2048]{1,0:T(8,128)(2,1)S(1)}) fusion(f32[288,2048]{1,0:T(8,128)} %copy-done.96, bf16[288,2048]{1,0:T(8,128)(2,1)} %get-tuple-element.407, bf16[288,1536]{1,0:T(8,128)(2,1)} %get-tuple-element.210.refs_0_, bf16[2048,1536]{1,0:T(8,128)(2,1)} %param.50), kind=kOutput, calls=%fused_computation.41 | convolution fusion | flops 1821376512 | bytes 13074432 | tf_op jit(solution)/shard_map/dot_general | solution.py:39
  217.3 6.6 fusion.141
  224.9 5.9 layer_out.3
  231.4 7.0 convolution_add_fusion.14.refs_0_
  239.8 5.7 fusion.19
  267.3 10.4 %collective-permute-done.10.refs_1_ = bf16[288,1536]{1,0:T(8,128)(2,1)S(1)} collective-permute-done((bf16[288,1536]{1,0:T(8,128)(2,1)S(1)}, bf16[288,1536]{1,0:T(8,128)(2,1)S(1)}, u32[]{:S(2)}, u32[]{:S(2)}) %collective-permute-start.10) | collective-permute-done | bytes 884768 | tf_op jit(solution)/shard_map/ppermute | solution.py:763
  278.7 6.6 hidden_grad.2
  292.2 15.6 %down_grad.1 = (bf16[8,768,256]{2,1,0:T(8,128)(2,1)}, bf16[8,768,256]{2,1,0:T(8,128)(2,1)}) custom-call(s32[4]{0:T(128)} %pad_add_fusion.1.bits_ref, bf16[288,1536]{1,0:T(8,128)(2,1)} %get-tuple-element.210.refs_0_, bf16[288,1536]{1,0:T(8,128)(2,1)} %get-tuple-element.208.refs_1_, bf16[288,1536]{1,0:T(8,128)(2,1)} %copy-done.77, ...), custom_call_target="tpu_custom_call" | custom-call | flops 15253332992 | bytes 41600000 | tf_op jit(solution)/shard_map/down_grad/pallas_call | solution.py:644
  308.8 6.4 hidden_grad.3
  322.1 15.6 %gate_up_grad.2 = (bf16[8,768,256]{2,1,0:T(8,128)(2,1)}, bf16[8,768,256]{2,1,0:T(8,128)(2,1)}) custom-call(s32[4]{0:T(128)} %pad_add_fusion.1.bits_ref, bf16[288,1536]{1,0:T(8,128)(2,1)} %get-tuple-element.218.refs_0_, bf16[288,1536]{1,0:T(8,128)(2,1)} %get-tuple-element.194.refs_1_, bf16[288,1536]{1,0:T(8,128)(2,1)} %copy-done.73, ...), custom_call_target="tpu_custom_call" | custom-call | flops 15253332992 | bytes 41600000 | tf_op jit(solution)/shard_map/gate_up_grad/pallas_call | solution.py:644
  337.9 15.6 %gate_up_grad.3 = (bf16[8,768,256]{2,1,0:T(8,128)(2,1)}, bf16[8,768,256]{2,1,0:T(8,128)(2,1)}) custom-call(s32[4]{0:T(128)} %pad_add_fusion.1.bits_ref, bf16[288,1536]{1,0:T(8,128)(2,1)} %get-tuple-element.218.refs_0_, bf16[288,1536]{1,0:T(8,128)(2,1)} %get-tuple-element.194.refs_1_, bf16[288,1536]{1,0:T(8,128)(2,1)} %copy-done.73, ...), custom_call_target="tpu_custom_call" | custom-call | flops 15253332992 | bytes 41600000 | tf_op jit(solution)/shard_map/gate_up_grad/pallas_call | solution.py:644
  354.0 5.6 add_and_split.15
  364.1 30.1 %attention_backward.3 = (bf16[1152,768]{1,0:T(8,128)(2,1)}, bf16[1152,768]{1,0:T(8,128)(2,1)}, bf16[1152,768]{1,0:T(8,128)(2,1)}, bf16[768,768]{1,0:T(8,128)(2,1...) custom-call(s32[12]{0:T(128)} %reshape.319.refs_0_.present_ref, f32[576,768]{1,0:T(8,128)} %fusion.130.refs_1_.refs_0_, ...), custom_call_target="tpu_custom_call" | custom-call | flops 6600000000 | bytes 18000000 | tf_op jit(solution)/shard_map/attention_backward/pallas_call | solution.py:467
  394.3 5.6 add_and_split.16
  411.0 5.6 add_and_split.18
  418.2 30.2 %attention_backward.4 = (bf16[1152,768]{1,0:T(8,128)(2,1)}, bf16[1152,768]{1,0:T(8,128)(2,1)}, bf16[1152,768]{1,0:T(8,128)(2,1)}, bf16[768,768]{1,0:T(8,128)(2,1...) custom-call(s32[12]{0:T(128)} %reshape.319.refs_0_.present_ref, ...), custom_call_target="tpu_custom_call", output_to_operand_aliasing={{0}: (18, {}), {1}: (19, {}), {2}: (20, {}), {3}: (21, {}),... | custom-call | flops 6600000000 | bytes 18000000 | tf_op jit(solution)/shard_map/attention_backward/pallas_call | solution.py:467
  457.8 13.3 %projection_grad.2 = (bf16[8,1440,256]{2,1,0:T(8,128)(2,1)}, bf16[8,1440,256]{2,1,0:T(8,128)(2,1)}) custom-call(s32[4]{0:T(128)} %pad_add_fusion.1.bits_ref, bf16[576,1536]{1,0:T(8,128)(2,1)} %normed_in.2.refs_0_, bf16[576,1536]{1,0:T(8,128)(2,1)} %normed_in.3.refs_1_, bf16[1152,768]{1,0:T(8,128)(2,1)} %get-tuple-element.241.refs_2_.refs_17_, ...), custom_call_target="tpu_custom_call" | custom-call | flops 11440000000 | bytes 31200000 | tf_op jit(solution)/shard_map/projection_grad/pallas_call | solution.py:644
  471.1 9.5 %caption_grad.2 = (bf16[8,1440,256]{2,1,0:T(8,128)(2,1)}, bf16[8,1440,256]{2,1,0:T(8,128)(2,1)}) custom-call(s32[4]{0:T(128)} %pad_add_fusion.1.bits_ref, bf16[768,2048]{1,0:T(8,128)(2,1)} %bitcast.250, bf16[768,768]{1,0:T(8,128)(2,1)} %get-tuple-element.271.refs_1_.refs_20_, ...), custom_call_target="tpu_custom_call", output_to_operand_aliasing={{0}: (4, {}), {1}: (5, {})} | custom-call | flops 7626666496 | bytes 20800000 | tf_op jit(solution)/shard_map/caption_grad/pallas_call | solution.py:644
  489.2 8.8 %output_grad.1 = (bf16[8,1440,256]{2,1,0:T(8,128)(2,1)}, bf16[8,1440,256]{2,1,0:T(8,128)(2,1)}) custom-call(s32[4]{0:T(128)} %pad_add_fusion.1.bits_ref, bf16[288,1536]{1,0:T(8,128)(2,1)} %get-tuple-element.262.refs_0_, bf16[288,1536]{1,0:T(8,128)(2,1)} %get-tuple-element.263.refs_1_, ...), custom_call_target="tpu_custom_call", output_to_operand_aliasing={{0}: (6, {}), {1}: (7, {})} | custom-call | flops 5720000000 | bytes 15600000 | tf_op jit(solution)/shard_map/output_grad/pallas_call | solution.py:644
  508.0 7.9 %add_and_split.23 = (bf16[4,1440,256]{2,1,0:T(8,128)(2,1)}, bf16[4,1440,256]{2,1,0:T(8,128)(2,1)}) custom-call(s32[4]{0:T(128)} %pad_add_fusion.1.bits_ref, bf16[8,1440,256]{2,1,0:T(8,128)(2,1)} %get-tuple-element.264.kept_stay.kept_go, bf16[8,1440,256]{2,1,0:T(8,128)(2,1)} %collective-permute-done.25.moved_stay.moved_go, ...), custom_call_target="tpu_custom_call" | custom-call | flops 11000000 | bytes 30000 | tf_op jit(solution)/shard_map/add_and_split/pallas_call | solution.py:678
  516.5 30.1 %attention_backward.5 = (bf16[1152,768]{1,0:T(8,128)(2,1)}, bf16[1152,768]{1,0:T(8,128)(2,1)}, bf16[1152,768]{1,0:T(8,128)(2,1)}, bf16[768,768]{1,0:T(8,128)(2,1...) custom-call(s32[12]{0:T(128)} %reshape.319.refs_0_.present_ref, ...), custom_call_target="tpu_custom_call", output_to_operand_aliasing={{0}: (18, {}), {1}: (19, {}), {2}: (20, {}), {3}: (21, {}),... | custom-call | flops 32999999488 | bytes 90000000 | tf_op jit(solution)/shard_map/attention_backward/pallas_call | solution.py:467
  562.5 6.4 collective-permute-start.32
  571.4 9.1 %projection_grad.3 = (bf16[8,576,256]{2,1,0:T(8,128)(2,1)}, bf16[8,576,256]{2,1,0:T(8,128)(2,1)}) custom-call(s32[4]{0:T(128)} %pad_add_fusion.1.bits_ref, bf16[576,1536]{1,0:T(8,128)(2,1)} %normed_in.2.refs_0_, bf16[576,1536]{1,0:T(8,128)(2,1)} %normed_in.3.refs_1_, bf16[1152,768]{1,0:T(8,128)(2,1)} %get-tuple-element.307.refs_2_, ...), custom_call_target="tpu_custom_call" | custom-call | flops 5720000000 | bytes 15600000 | tf_op jit(solution)/shard_map/projection_grad/pallas_call | solution.py:644
  580.5 6.9 caption_grad.3
  601.0 5.0 add_and_split.25
  619.6 5.0 add_and_split.26
  626.1 5.4 tokens_grad.2
  631.6 9.4 %collective-permute-done.33.moved_stay.moved_go = bf16[2,1440,256]{2,1,0:T(8,128)(2,1)} collective-permute-done((bf16[2,1440,256]{2,1,0:T(8,128)(2,1)}, bf16[2,1440,256]{2,1,0:T(8,128)(2,1)}, u32[]{:S(2)}, u32[]{:S(2)}) %collective-permute-start.33) | collective-permute-done | bytes 1474592 | tf_op jit(solution)/shard_map/ppermute | solution.py:779
  645.2 5.5 tokens_grad.3
  663.5 16.4 %collective-permute-done.36.early_moved = bf16[1,1440,256]{2,1,0:T(8,128)(2,1)S(1)} collective-permute-done((bf16[1,1440,256]{2,1,0:T(8,128)(2,1)}, bf16[1,1440,256]{2,1,0:T(8,128)(2,1)S(1)}, u32[]{:S(2)}, u32[]{:S(2)}) %collective-permute-start.36) | collective-permute-done | bytes 737312 | tf_op jit(solution)/shard_map/ppermute | solution.py:779
  683.2 4.4 collective-permute-done.37
  688.9 5.7 collective-permute-done.39.moved_stay.moved_go
  703.7 4.7 collective-permute-done.40
  711.0 7.9 %collective-permute-done.42.late_moved = bf16[1,576,256]{2,1,0:T(8,128)(2,1)} collective-permute-done((bf16[1,576,256]{2,1,0:T(8,128)(2,1)}, bf16[1,576,256]{2,1,0:T(8,128)(2,1)}, u32[]{:S(2)}, u32[]{:S(2)}) %collective-permute-start.42) | collective-permute-done | bytes 294944 | tf_op jit(solution)/shard_map/ppermute | solution.py:779
  (496 shorter events, 265.3 us)
Async XLA Ops:
  4.5 35.2 %collective-permute-start = (f32[3,3072]{1,0:T(4,128)S(1)}, f32[3,3072]{1,0:T(4,128)S(1)}, u32[]{:S(2)}, u32[]{:S(2)}) collective-permute-start(f32[3,3072]{1,0:T(4,128)S(1)} %convolution_add_fusion), channel_id=1, source_target_pairs={{1,0},{0,1},{3,2},{2,3},{5,4},{4,5},{7,6},{6,7},{9,8},{8,9},{11,10... | collective-permute-start | bytes 110600 | tf_op jit(solution)/shard_map/ppermute | solution.py:763
  7.5 48.6 %collective-permute-start.1 = (bf16[576,1536]{1,0:T(8,128)(2,1)}, bf16[576,1536]{1,0:T(8,128)(2,1)}, u32[]{:S(2)}, u32[]{:S(2)}) collective-permute-start(bf16[576,1536]{1,0:T(8,128)(2,1)} %refs_0_.1), channel_id=1, source_target_pairs={{1,0},{0,1},{3,2},{2,3},{5,4},{4,5},{7,6},{6,7},{9,8},{8,9},{11,10... | collective-permute-start | bytes 5308424 | tf_op jit(solution)/shard_map/ppermute | solution.py:763
  7.5 126.3 %collective-permute-start.3 = (bf16[768,1536]{1,0:T(8,128)(2,1)}, bf16[768,1536]{1,0:T(8,128)(2,1)}, u32[]{:S(2)}, u32[]{:S(2)}) collective-permute-start(bf16[768,1536]{1,0:T(8,128)(2,1)} %param.47), channel_id=1, source_target_pairs={{1,0},{0,1},{3,2},{2,3},{5,4},{4,5},{7,6},{6,7},{9,8},{8,9},{11,10... | collective-permute-start | bytes 7077896 | tf_op jit(solution)/shard_map/ppermute | solution.py:763
  116.9 16.9 %collective-permute-start.2 = (bf16[288,768]{1,0:T(8,128)(2,1)S(1)}, bf16[288,768]{1,0:T(8,128)(2,1)S(1)}, u32[]{:S(2)}, u32[]{:S(2)}) collective-permute-start(bf16[288,768]{1,0:T(8,128)(2,1)S(1)} %get-tuple-element.373), channel_id=1, source_target_pairs={{1,0},{0,1},{3,2},{2,3},{5,4},{4,5},{7,6},{6,7},{9,8},{8,9},{11,10... | collective-permute-start | bytes 1327112 | tf_op jit(solution)/shard_map/ppermute | solution.py:763
  125.4 19.1 %collective-permute-start.6 = (bf16[288,768]{1,0:T(8,128)(2,1)S(1)}, bf16[288,768]{1,0:T(8,128)(2,1)S(1)}, u32[]{:S(2)}, u32[]{:S(2)}) collective-permute-start(bf16[288,768]{1,0:T(8,128)(2,1)S(1)} %get-tuple-element.374), channel_id=1, source_target_pairs={{1,0},{0,1},{3,2},{2,3},{5,4},{4,5},{7,6},{6,7},{9,8},{8,9},{11,10... | collective-permute-start | bytes 1327112 | tf_op jit(solution)/shard_map/ppermute | solution.py:763
  142.4 31.5 %collective-permute-start.4 = (bf16[288,1536]{1,0:T(8,128)(2,1)}, bf16[288,1536]{1,0:T(8,128)(2,1)S(1)}, u32[]{:S(2)}, u32[]{:S(2)}) collective-permute-start(bf16[288,1536]{1,0:T(8,128)(2,1)} %get-tuple-element.218.refs_0_), channel_id=1, source_target_pairs={{1,0},{0,1},{3,2},{2,3},{5,4},{4,5},{7,6},{6,7},{9,8},{8,9},{11,10... | collective-permute-start | bytes 2654216 | tf_op jit(solution)/shard_map/ppermute | solution.py:763
  161.6 29.4 %collective-permute-start.7 = (bf16[288,1536]{1,0:T(8,128)(2,1)}, bf16[288,1536]{1,0:T(8,128)(2,1)S(1)}, u32[]{:S(2)}, u32[]{:S(2)}) collective-permute-start(bf16[288,1536]{1,0:T(8,128)(2,1)} %get-tuple-element.194.refs_1_), channel_id=1, source_target_pairs={{1,0},{0,1},{3,2},{2,3},{5,4},{4,5},{7,6},{6,7},{9,8},{8,9},{11,10... | collective-permute-start | bytes 2654216 | tf_op jit(solution)/shard_map/ppermute | solution.py:763
  181.2 20.7 %collective-permute-start.5 = (bf16[288,1536]{1,0:T(8,128)(2,1)S(1)}, bf16[288,1536]{1,0:T(8,128)(2,1)S(1)}, u32[]{:S(2)}, u32[]{:S(2)}) collective-permute-start(bf16[288,1536]{1,0:T(8,128)(2,1)S(1)} %convolution_convert_fusion.1), channel_id=1, source_target_pairs={{1,0},{0,1},{3,2},{2,3},{5,4},{4,5},{7,6},{6,7},{9,8},{8,9},{11,10... | collective-permute-start | bytes 2654216 | tf_op jit(solution)/shard_map/ppermute | solution.py:763
  198.2 25.7 %collective-permute-start.8 = (bf16[288,1536]{1,0:T(8,128)(2,1)S(1)}, bf16[288,1536]{1,0:T(8,128)(2,1)S(1)}, u32[]{:S(2)}, u32[]{:S(2)}) collective-permute-start(bf16[288,1536]{1,0:T(8,128)(2,1)S(1)} %convolution_convert_fusion), channel_id=1, source_target_pairs={{1,0},{0,1},{3,2},{2,3},{5,4},{4,5},{7,6},{6,7},{9,8},{8,9},{11,10... | collective-permute-start | bytes 2654216 | tf_op jit(solution)/shard_map/ppermute | solution.py:763
  208.2 31.6 %collective-permute-start.9 = (bf16[288,1536]{1,0:T(8,128)(2,1)}, bf16[288,1536]{1,0:T(8,128)(2,1)S(1)}, u32[]{:S(2)}, u32[]{:S(2)}) collective-permute-start(bf16[288,1536]{1,0:T(8,128)(2,1)} %get-tuple-element.210.refs_0_), channel_id=1, source_target_pairs={{1,0},{0,1},{3,2},{2,3},{5,4},{4,5},{7,6},{6,7},{9,8},{8,9},{11,10... | collective-permute-start | bytes 2654216 | tf_op jit(solution)/shard_map/ppermute | solution.py:763
  230.8 28.9 %collective-permute-start.11 = (bf16[288,1536]{1,0:T(8,128)(2,1)}, bf16[288,1536]{1,0:T(8,128)(2,1)S(1)}, u32[]{:S(2)}, u32[]{:S(2)}) collective-permute-start(bf16[288,1536]{1,0:T(8,128)(2,1)} %get-tuple-element.208.refs_1_), channel_id=1, source_target_pairs={{1,0},{0,1},{3,2},{2,3},{5,4},{4,5},{7,6},{6,7},{9,8},{8,9},{11,10... | collective-permute-start | bytes 2654216 | tf_op jit(solution)/shard_map/ppermute | solution.py:763
  249.8 27.9 %collective-permute-start.10 = (bf16[288,1536]{1,0:T(8,128)(2,1)S(1)}, bf16[288,1536]{1,0:T(8,128)(2,1)S(1)}, u32[]{:S(2)}, u32[]{:S(2)}) collective-permute-start(bf16[288,1536]{1,0:T(8,128)(2,1)S(1)} %fusion.2), channel_id=1, source_target_pairs={{1,0},{0,1},{3,2},{2,3},{5,4},{4,5},{7,6},{6,7},{9,8},{8,9},{11,10... | collective-permute-start | bytes 2654216 | tf_op jit(solution)/shard_map/ppermute | solution.py:763
  266.4 41.4 %collective-permute-start.12 = (bf16[288,1536]{1,0:T(8,128)(2,1)S(1)}, bf16[288,1536]{1,0:T(8,128)(2,1)S(1)}, u32[]{:S(2)}, u32[]{:S(2)}) collective-permute-start(bf16[288,1536]{1,0:T(8,128)(2,1)S(1)} %fusion.3), channel_id=1, source_target_pairs={{1,0},{0,1},{3,2},{2,3},{5,4},{4,5},{7,6},{6,7},{9,8},{8,9},{11,10... | collective-permute-start | bytes 2654216 | tf_op jit(solution)/shard_map/ppermute | solution.py:763
  290.7 47.2 %collective-permute-start.13 = (bf16[288,768]{1,0:T(8,128)(2,1)S(1)}, bf16[288,768]{1,0:T(8,128)(2,1)S(1)}, u32[]{:S(2)}, u32[]{:S(2)}) collective-permute-start(bf16[288,768]{1,0:T(8,128)(2,1)S(1)} %convolution_convert_fusion.7), channel_id=1, source_target_pairs={{1,0},{0,1},{3,2},{2,3},{5,4},{4,5},{7,6},{6,7},{9,8},{8,9},{11,10... | collective-permute-start | bytes 1327112 | tf_op jit(solution)/shard_map/ppermute | solution.py:763
  307.8 46.1 %collective-permute-start.15 = (bf16[8,768,256]{2,1,0:T(8,128)(2,1)}, bf16[8,768,256]{2,1,0:T(8,128)(2,1)}, u32[]{:S(2)}, u32[]{:S(2)}) collective-permute-start(bf16[8,768,256]{2,1,0:T(8,128)(2,1)} %get-tuple-element.211), channel_id=1, source_target_pairs={{0,2},{2,0},{4,6},{6,4},{8,10},{10,8},{12,14},{14,12},{16,18},{18,... | collective-permute-start | bytes 9437192 | tf_op jit(solution)/shard_map/ppermute | solution.py:779
  321.4 16.5 %collective-permute-start.14 = (bf16[288,768]{1,0:T(8,128)(2,1)S(1)}, bf16[288,768]{1,0:T(8,128)(2,1)S(1)}, u32[]{:S(2)}, u32[]{:S(2)}) collective-permute-start(bf16[288,768]{1,0:T(8,128)(2,1)S(1)} %convolution_convert_fusion.5), channel_id=1, source_target_pairs={{1,0},{0,1},{3,2},{2,3},{5,4},{4,5},{7,6},{6,7},{9,8},{8,9},{11,10... | collective-permute-start | bytes 1327112 | tf_op jit(solution)/shard_map/ppermute | solution.py:763
  337.7 56.5 %collective-permute-start.18 = (bf16[8,768,256]{2,1,0:T(8,128)(2,1)}, bf16[8,768,256]{2,1,0:T(8,128)(2,1)}, u32[]{:S(2)}, u32[]{:S(2)}) collective-permute-start(bf16[8,768,256]{2,1,0:T(8,128)(2,1)} %get-tuple-element.217), channel_id=1, source_target_pairs={{0,2},{2,0},{4,6},{6,4},{8,10},{10,8},{12,14},{14,12},{16,18},{18,... | collective-permute-start | bytes 9437192 | tf_op jit(solution)/shard_map/ppermute | solution.py:779
  353.6 55.8 %collective-permute-start.16 = (bf16[8,768,256]{2,1,0:T(8,128)(2,1)}, bf16[8,768,256]{2,1,0:T(8,128)(2,1)S(1)}, u32[]{:S(2)}, u32[]{:S(2)}) collective-permute-start(bf16[8,768,256]{2,1,0:T(8,128)(2,1)} %get-tuple-element.219), channel_id=1, source_target_pairs={{0,2},{2,0},{4,6},{6,4},{8,10},{10,8},{12,14},{14,12},{16,18},{18,... | collective-permute-start | bytes 9437192 | tf_op jit(solution)/shard_map/ppermute | solution.py:779
  359.6 41.8 %collective-permute-start.17 = (bf16[4,768,256]{2,1,0:T(8,128)(2,1)}, bf16[4,768,256]{2,1,0:T(8,128)(2,1)}, u32[]{:S(2)}, u32[]{:S(2)}) collective-permute-start(bf16[4,768,256]{2,1,0:T(8,128)(2,1)} %get-tuple-element.221), channel_id=1, source_target_pairs={{0,4},{2,6},{4,0},{6,2},{8,12},{10,14},{12,8},{14,10},{16,20},{18,... | collective-permute-start | bytes 4718600 | tf_op jit(solution)/shard_map/ppermute | solution.py:779
  399.8 48.6 %collective-permute-start.20 = (bf16[4,768,256]{2,1,0:T(8,128)(2,1)}, bf16[4,768,256]{2,1,0:T(8,128)(2,1)}, u32[]{:S(2)}, u32[]{:S(2)}) collective-permute-start(bf16[4,768,256]{2,1,0:T(8,128)(2,1)} %get-tuple-element.228), channel_id=1, source_target_pairs={{0,4},{2,6},{4,0},{6,2},{8,12},{10,14},{12,8},{14,10},{16,20},{18,... | collective-permute-start | bytes 4718600 | tf_op jit(solution)/shard_map/ppermute | solution.py:779
  404.9 49.0 %collective-permute-start.22 = (bf16[2,768,256]{2,1,0:T(8,128)(2,1)}, bf16[2,768,256]{2,1,0:T(8,128)(2,1)S(1)}, u32[]{:S(2)}, u32[]{:S(2)}) collective-permute-start(bf16[2,768,256]{2,1,0:T(8,128)(2,1)} %get-tuple-element.230), channel_id=1, source_target_pairs={{0,8},{2,10},{4,12},{6,14},{8,0},{10,2},{12,4},{14,6},{16,24},{18,... | collective-permute-start | bytes 2359304 | tf_op jit(solution)/shard_map/ppermute | solution.py:779
  406.9 82.2 %collective-permute-start.23 = (bf16[288,1536]{1,0:T(8,128)(2,1)}, bf16[288,1536]{1,0:T(8,128)(2,1)}, u32[]{:S(2)}, u32[]{:S(2)}) collective-permute-start(bf16[288,1536]{1,0:T(8,128)(2,1)} %get-tuple-element.262.refs_0_), channel_id=1, source_target_pairs={{1,0},{0,1},{3,2},{2,3},{5,4},{4,5},{7,6},{6,7},{9,8},{8,9},{11,10... | collective-permute-start | bytes 2654216 | tf_op jit(solution)/shard_map/ppermute | solution.py:763
  409.3 79.8 %collective-permute-start.24 = (bf16[288,1536]{1,0:T(8,128)(2,1)}, bf16[288,1536]{1,0:T(8,128)(2,1)}, u32[]{:S(2)}, u32[]{:S(2)}) collective-permute-start(bf16[288,1536]{1,0:T(8,128)(2,1)} %get-tuple-element.263.refs_1_), channel_id=1, source_target_pairs={{1,0},{0,1},{3,2},{2,3},{5,4},{4,5},{7,6},{6,7},{9,8},{8,9},{11,10... | collective-permute-start | bytes 2654216 | tf_op jit(solution)/shard_map/ppermute | solution.py:763
  416.7 67.8 %collective-permute-start.19 = (bf16[4,768,256]{2,1,0:T(8,128)(2,1)}, bf16[4,768,256]{2,1,0:T(8,128)(2,1)S(1)}, u32[]{:S(2)}, u32[]{:S(2)}) collective-permute-start(bf16[4,768,256]{2,1,0:T(8,128)(2,1)} %get-tuple-element.232), channel_id=1, source_target_pairs={{0,4},{2,6},{4,0},{6,2},{8,12},{10,14},{12,8},{14,10},{16,20},{18,... | collective-permute-start | bytes 4718600 | tf_op jit(solution)/shard_map/ppermute | solution.py:779
  451.9 28.6 %collective-permute-start.21 = (bf16[2,768,256]{2,1,0:T(8,128)(2,1)}, bf16[2,768,256]{2,1,0:T(8,128)(2,1)S(1)}, u32[]{:S(2)}, u32[]{:S(2)}) collective-permute-start(bf16[2,768,256]{2,1,0:T(8,128)(2,1)} %get-tuple-element.244), channel_id=1, source_target_pairs={{0,8},{2,10},{4,12},{6,14},{8,0},{10,2},{12,4},{14,6},{16,24},{18,... | collective-permute-start | bytes 2359304 | tf_op jit(solution)/shard_map/ppermute | solution.py:779
  498.0 10.0 %collective-permute-start.25 = (bf16[8,1440,256]{2,1,0:T(8,128)(2,1)}, bf16[8,1440,256]{2,1,0:T(8,128)(2,1)}, u32[]{:S(2)}, u32[]{:S(2)}) collective-permute-start(bf16[8,1440,256]{2,1,0:T(8,128)(2,1)} %get-tuple-element.265), channel_id=1, source_target_pairs={{0,2},{2,0},{4,6},{6,4},{8,10},{10,8},{12,14},{14,12},{16,18},{18,... | collective-permute-start | bytes 17694728 | tf_op jit(solution)/shard_map/ppermute | solution.py:779
  501.3 45.3 %collective-permute-start.26 = (bf16[1,768,256]{2,1,0:T(8,128)(2,1)S(1)}, bf16[1,768,256]{2,1,0:T(8,128)(2,1)S(1)}, u32[]{:S(2)}, u32[]{:S(2)}) collective-permute-start(bf16[1,768,256]{2,1,0:T(8,128)(2,1)S(1)} %copy-done.81), channel_id=1, source_target_pairs={{0,16},{2,18},{4,20},{6,22},{8,24},{10,26},{12,28},{14,30},{16,0},... | collective-permute-start | bytes 1179656 | tf_op jit(solution)/shard_map/ppermute | solution.py:779
  502.4 44.3 %collective-permute-start.27 = (bf16[1,768,256]{2,1,0:T(8,128)(2,1)}, bf16[1,768,256]{2,1,0:T(8,128)(2,1)S(1)}, u32[]{:S(2)}, u32[]{:S(2)}) collective-permute-start(bf16[1,768,256]{2,1,0:T(8,128)(2,1)} %get-tuple-element.258), channel_id=1, source_target_pairs={{0,16},{2,18},{4,20},{6,22},{8,24},{10,26},{12,28},{14,30},{16,0},... | collective-permute-start | bytes 1179656 | tf_op jit(solution)/shard_map/ppermute | solution.py:779
  504.3 42.4 %collective-permute-start.28 = (bf16[2,768,256]{2,1,0:T(8,128)(2,1)S(1)}, bf16[2,768,256]{2,1,0:T(8,128)(2,1)S(1)}, u32[]{:S(2)}, u32[]{:S(2)}) collective-permute-start(bf16[2,768,256]{2,1,0:T(8,128)(2,1)S(1)} %copy-done.80), channel_id=1, source_target_pairs={{0,8},{2,10},{4,12},{6,14},{8,0},{10,2},{12,4},{14,6},{16,24},{18,... | collective-permute-start | bytes 2359304 | tf_op jit(solution)/shard_map/ppermute | solution.py:779
  515.9 85.0 %collective-permute-start.29 = (bf16[4,1440,256]{2,1,0:T(8,128)(2,1)}, bf16[4,1440,256]{2,1,0:T(8,128)(2,1)}, u32[]{:S(2)}, u32[]{:S(2)}) collective-permute-start(bf16[4,1440,256]{2,1,0:T(8,128)(2,1)} %get-tuple-element.266), channel_id=1, source_target_pairs={{0,4},{2,6},{4,0},{6,2},{8,12},{10,14},{12,8},{14,10},{16,20},{18,... | collective-permute-start | bytes 8847368 | tf_op jit(solution)/shard_map/ppermute | solution.py:779
  562.5 63.6 %collective-permute-start.32 = (bf16[288,1536]{1,0:T(8,128)(2,1)}, bf16[288,1536]{1,0:T(8,128)(2,1)}, u32[]{:S(2)}, u32[]{:S(2)}) collective-permute-start(bf16[288,1536]{1,0:T(8,128)(2,1)} %fusion.1), channel_id=1, source_target_pairs={{1,0},{0,1},{3,2},{2,3},{5,4},{4,5},{7,6},{6,7},{9,8},{8,9},{11,10... | collective-permute-start | bytes 2654216 | tf_op jit(solution)/shard_map/ppermute | solution.py:763
  568.9 57.2 %collective-permute-start.30 = (bf16[288,1536]{1,0:T(8,128)(2,1)}, bf16[288,1536]{1,0:T(8,128)(2,1)}, u32[]{:S(2)}, u32[]{:S(2)}) collective-permute-start(bf16[288,1536]{1,0:T(8,128)(2,1)} %fusion), channel_id=1, source_target_pairs={{1,0},{0,1},{3,2},{2,3},{5,4},{4,5},{7,6},{6,7},{9,8},{8,9},{11,10... | collective-permute-start | bytes 2654216 | tf_op jit(solution)/shard_map/ppermute | solution.py:763
  569.0 29.8 %collective-permute-start.43 = (bf16[1,768,256]{2,1,0:T(8,128)(2,1)}, bf16[1,768,256]{2,1,0:T(8,128)(2,1)}, u32[]{:S(2)}, u32[]{:S(2)}) collective-permute-start(bf16[1,768,256]{2,1,0:T(8,128)(2,1)} %get-tuple-element.294), channel_id=1, source_target_pairs={{0,16},{2,18},{4,20},{6,22},{8,24},{10,26},{12,28},{14,30},{16,0},... | collective-permute-start | bytes 1179656 | tf_op jit(solution)/shard_map/ppermute | solution.py:779
  587.5 32.1 %collective-permute-start.31 = (bf16[8,576,256]{2,1,0:T(8,128)(2,1)}, bf16[8,576,256]{2,1,0:T(8,128)(2,1)}, u32[]{:S(2)}, u32[]{:S(2)}) collective-permute-start(bf16[8,576,256]{2,1,0:T(8,128)(2,1)} %get-tuple-element.304), channel_id=1, source_target_pairs={{0,2},{2,0},{4,6},{6,4},{8,10},{10,8},{12,14},{14,12},{16,18},{18,... | collective-permute-start | bytes 7077896 | tf_op jit(solution)/shard_map/ppermute | solution.py:779
  606.0 35.0 %collective-permute-start.33 = (bf16[2,1440,256]{2,1,0:T(8,128)(2,1)}, bf16[2,1440,256]{2,1,0:T(8,128)(2,1)}, u32[]{:S(2)}, u32[]{:S(2)}) collective-permute-start(bf16[2,1440,256]{2,1,0:T(8,128)(2,1)} %get-tuple-element.306), channel_id=1, source_target_pairs={{0,8},{2,10},{4,12},{6,14},{8,0},{10,2},{12,4},{14,6},{16,24},{18,... | collective-permute-start | bytes 4423688 | tf_op jit(solution)/shard_map/ppermute | solution.py:779
  624.6 28.3 %collective-permute-start.34 = (bf16[4,576,256]{2,1,0:T(8,128)(2,1)}, bf16[4,576,256]{2,1,0:T(8,128)(2,1)S(1)}, u32[]{:S(2)}, u32[]{:S(2)}) collective-permute-start(bf16[4,576,256]{2,1,0:T(8,128)(2,1)} %get-tuple-element.310), channel_id=1, source_target_pairs={{0,4},{2,6},{4,0},{6,2},{8,12},{10,14},{12,8},{14,10},{16,20},{18,... | collective-permute-start | bytes 3538952 | tf_op jit(solution)/shard_map/ppermute | solution.py:779
  644.7 35.1 %collective-permute-start.36 = (bf16[1,1440,256]{2,1,0:T(8,128)(2,1)}, bf16[1,1440,256]{2,1,0:T(8,128)(2,1)S(1)}, u32[]{:S(2)}, u32[]{:S(2)}) collective-permute-start(bf16[1,1440,256]{2,1,0:T(8,128)(2,1)} %get-tuple-element.317), channel_id=1, source_target_pairs={{0,16},{2,18},{4,20},{6,22},{8,24},{10,26},{12,28},{14,30},{16,0},... | collective-permute-start | bytes 2211848 | tf_op jit(solution)/shard_map/ppermute | solution.py:779
  657.3 22.5 %copy-start.28 = (f32[2,3,3072]{2,1,0:T(4,128)S(1)}, f32[2,3,3072]{2,1,0:T(4,128)}, u32[]{:S(2)}) copy-start(f32[2,3,3072]{2,1,0:T(4,128)} %copy-done.27) | copy-start | bytes 221188
  657.3 22.5 %copy-start.45 = (f32[1536]{0:T(1024)S(1)}, f32[1536]{0:T(1024)}, u32[]{:S(2)}) copy-start(f32[1536]{0:T(1024)} %param.37) | copy-start | bytes 18436
  657.4 23.4 %copy-start.37 = (f32[11648]{0:T(1024)S(1)}, f32[11648]{0:T(1024)}, u32[]{:S(2)}) copy-start(f32[11648]{0:T(1024)} %custom-call.5) | copy-start | bytes 139780
  657.4 23.5 %copy-start.42 = (f32[2304]{0:T(1024)S(1)}, f32[2304]{0:T(1024)}, u32[]{:S(2)}) copy-start(f32[2304]{0:T(1024)} %reshape.324) | copy-start | bytes 27652
  657.4 6.0 collective-permute-start.35
  663.0 31.7 %collective-permute-start.39 = (bf16[2,576,256]{2,1,0:T(8,128)(2,1)}, bf16[2,576,256]{2,1,0:T(8,128)(2,1)S(1)}, u32[]{:S(2)}, u32[]{:S(2)}) collective-permute-start(bf16[2,576,256]{2,1,0:T(8,128)(2,1)} %get-tuple-element.331), channel_id=1, source_target_pairs={{0,8},{2,10},{4,12},{6,14},{8,0},{10,2},{12,4},{14,6},{16,24},{18,... | collective-permute-start | bytes 1769480 | tf_op jit(solution)/shard_map/ppermute | solution.py:779
  680.9 6.6 collective-permute-start.37
  688.2 9.1 %collective-permute-start.38 = (f32[288,128]{1,0:T(8,128)S(1)}, f32[288,128]{1,0:T(8,128)S(1)}, u32[]{:S(2)}, u32[]{:S(2)}) collective-permute-start(f32[288,128]{1,0:T(8,128)S(1)} %pad_maximum_fusion.4), channel_id=1, source_target_pairs={{0,8},{2,10},{4,12},{6,14},{8,0},{10,2},{12,4},{14,6},{16,24},{18,... | collective-permute-start | bytes 442376 | tf_op jit(solution)/shard_map/ppermute | solution.py:779
  700.8 7.6 %collective-permute-start.40 = (f32[480,128]{1,0:T(8,128)S(1)}, f32[480,128]{1,0:T(8,128)S(1)}, u32[]{:S(2)}, u32[]{:S(2)}) collective-permute-start(f32[480,128]{1,0:T(8,128)S(1)} %pad_maximum_fusion.3), channel_id=1, source_target_pairs={{0,4},{2,6},{4,0},{6,2},{8,12},{10,14},{12,8},{14,10},{16,20},{18,... | collective-permute-start | bytes 737288 | tf_op jit(solution)/shard_map/ppermute | solution.py:779
  703.7 15.2 %collective-permute-start.42 = (bf16[1,576,256]{2,1,0:T(8,128)(2,1)}, bf16[1,576,256]{2,1,0:T(8,128)(2,1)}, u32[]{:S(2)}, u32[]{:S(2)}) collective-permute-start(bf16[1,576,256]{2,1,0:T(8,128)(2,1)} %get-tuple-element.337), channel_id=1, source_target_pairs={{0,16},{2,18},{4,20},{6,22},{8,24},{10,26},{12,28},{14,30},{16,0},... | collective-permute-start | bytes 884744 | tf_op jit(solution)/shard_map/ppermute | solution.py:779
  709.7 12.1 %collective-permute-start.41 = (f32[864,128]{1,0:T(8,128)}, f32[864,128]{1,0:T(8,128)S(1)}, u32[]{:S(2)}, u32[]{:S(2)}) collective-permute-start(f32[864,128]{1,0:T(8,128)} %constant_dynamic-update-slice_fusion.1), channel_id=1, source_target_pairs={{0,2},{2,0},{4,6},{6,4},{8,10},{10,8},{12,14},{14,12},{16,18},{18,... | collective-permute-start | bytes 1327112 | tf_op jit(solution)/shard_map/ppermute | solution.py:779
  (112 other events, 586.3 us)
